TPU v7x, 32 devices: a whole 2x2x4 slice. The times are simulated.
32 devices in a mesh: seq: 8 (over z, x), head: 4 (over y, core).
Axes of the slice: x: 2, y: 2, z: 4, core: 2. Of those that a mesh axis runs over, the one named last changes fastest.
Arguments:
- tokens: bfloat16 [2048, 1536], P('seq'), may hold values from -6 to 6
- attn_gain: float32 [1536], replicated, may hold values from 0.5 to 1.5
- query_weight: bfloat16 [1536, 1536], P('seq', 'head'), may hold values from -0.15625 to 0.15625
- key_weight: bfloat16 [1536, 1536], P('seq', 'head'), may hold values from -0.15625 to 0.15625
- value_weight: bfloat16 [1536, 1536], P('seq', 'head'), may hold values from -0.15625 to 0.15625
- forget_weight: bfloat16 [1536, 24], P('seq', 'head'), may hold values from -0.15625 to 0.15625
- forget_bias: float32 [24], P('head'), may hold values from 3 to 10
- out_weight: bfloat16 [1536, 1536], P('head', 'seq'), may hold values from -1.5 to 1.5
- ffn_gain: float32 [1536], replicated, may hold values from 0.5 to 1.5
- gate_weight: bfloat16 [1536, 4096], P('seq', 'head'), may hold values from -0.15625 to 0.15625
- up_weight: bfloat16 [1536, 4096], P('seq', 'head'), may hold values from -0.15625 to 0.15625
- down_weight: bfloat16 [4096, 1536], P('head', 'seq'), may hold values from -0.09375 to 0.09375
- doc_lengths: int32 [4], replicated, may hold values from 1 to 1024, 2048 in all
- out_grad: bfloat16 [2048, 1536], P('seq'), may hold values from -6 to 6
Outputs:
- layer_out: bfloat16 [2048, 1536], P('seq')
- tokens_grad: bfloat16 [2048, 1536], P('seq')
- attn_gain_grad: float32 [1536], replicated
- query_weight_grad: float32 [1536, 1536], P('seq', 'head')
- key_weight_grad: float32 [1536, 1536], P('seq', 'head')
- value_weight_grad: float32 [1536, 1536], P('seq', 'head')
- forget_weight_grad: float32 [1536, 24], P('seq', 'head')
- forget_bias_grad: float32 [24], P('head')
- out_weight_grad: float32 [1536, 1536], P('head', 'seq')
- ffn_gain_grad: float32 [1536], replicated
- gate_weight_grad: float32 [1536, 4096], P('seq', 'head')
- up_weight_grad: float32 [1536, 4096], P('seq', 'head')
- down_weight_grad: float32 [4096, 1536], P('head', 'seq')
Inputs may be any that keep to these rules, and one draw needn't show every extreme that they name: `doc_lengths`: document lengths in position order summing to 2048; the longest is exactly 1024.
All inputs are finite; a program needn't handle non-finite values.
Results may differ from a plain program's by a relative error of at most 0.02.
Values may be sent and summed in bfloat16 or wider, within the bound.
A program may use at most 256 MiB of HBM per device.

v0:
```python
import jax
import jax.numpy as jnp
from jax import lax
from jax.sharding import PartitionSpec as P

HEAD_DIM = 64


EPSILON = 1e-06
HIGHEST = lax.Precision.HIGHEST
MASKED = -1e30


def unchanged(carried):
    return carried


def contract_rows(left, right):
    return lax.dot_general(
        left, right, (((0,), (0,)), ((), ())), preferred_element_type=jnp.float32
    )


def contract_cols(left, right):
    return lax.dot_general(
        left, right, (((1,), (1,)), ((), ())), preferred_element_type=jnp.float32
    )


def norm_rows(values_in, gain):
    inverse = lax.rsqrt(jnp.mean(values_in * values_in, axis=-1, keepdims=True) + EPSILON)
    normed = values_in * inverse
    return (normed, inverse, normed * gain)


def norm_back(grad_in, normed, inverse, gain):
    scaled = grad_in * gain
    inner = jnp.mean(scaled * normed, axis=-1, keepdims=True)
    return (inverse * (scaled - normed * inner), jnp.sum(grad_in * normed, axis=0))


def doc_index(positions, doc_ends):
    return jnp.sum((positions[:, None] >= doc_ends[None, :]).astype(jnp.int32), axis=1)


def stored_positions(rows, n_seq, local_rows):
    half_rows = local_rows // 2
    device_of = rows // local_rows
    within = rows % local_rows
    group_of = jnp.where(within < half_rows, device_of, 2 * n_seq - 1 - device_of)
    return group_of * half_rows + within % half_rows


def to_positions(stored, n_seq):
    columns = stored.shape[1]
    half_rows = stored.shape[0] // (2 * n_seq)
    parts = stored.reshape(n_seq, 2, half_rows, columns)
    first = parts[:, 0]
    second = jnp.flip(parts[:, 1], 0)
    return jnp.concatenate([first, second], axis=0).reshape(-1, columns)


def to_stored(ordered, n_seq):
    columns = ordered.shape[1]
    half_rows = ordered.shape[0] // (2 * n_seq)
    parts = ordered.reshape(2 * n_seq, half_rows, columns)
    first = parts[:n_seq]
    second = jnp.flip(parts[n_seq:], 0)
    return jnp.stack([first, second], axis=1).reshape(-1, columns)


def block_scores(
    query_heads, key_heads, query_offsets, key_offsets, query_pos, key_pos, query_docs, key_docs
):
    raw_scores = jnp.einsum(
        "qhd,khd->hqk", query_heads, key_heads, preferred_element_type=jnp.float32
    )
    scores = (
        raw_scores * HEAD_DIM ** (-0.5) + query_offsets.T[:, :, None] - key_offsets.T[:, None, :]
    )
    allowed = (query_docs[:, None] == key_docs[None, :]) & (key_pos[None, :] <= query_pos[:, None])
    return (jnp.where(allowed[None], scores, MASKED), allowed)


def piece_grads(
    query_heads,
    grad_heads,
    log_mass,
    row_delta,
    query_offsets,
    key_heads,
    value_heads,
    key_offsets,
    query_pos,
    key_pos,
    query_docs,
    key_docs,
):
    scores, allowed = block_scores(
        query_heads, key_heads, query_offsets, key_offsets, query_pos, key_pos, query_docs, key_docs
    )
    probs = jnp.where(allowed[None], jnp.exp(scores - log_mass[:, :, None]), 0.0)
    grad_probs = jnp.einsum(
        "qhd,khd->hqk", grad_heads, value_heads, preferred_element_type=jnp.float32
    )
    grad_scores = (probs * (grad_probs - row_delta[:, :, None])).astype(jnp.bfloat16)
    score_sums = grad_scores.astype(jnp.float32)
    query_rows = query_heads.shape[0]
    key_rows = key_heads.shape[0]
    grad_query = jnp.einsum(
        "hqk,khd->qhd", grad_scores, key_heads, preferred_element_type=jnp.float32
    ).reshape(query_rows, -1)
    grad_key = (
        jnp.einsum("hqk,qhd->khd", grad_scores, query_heads, preferred_element_type=jnp.float32)
        * HEAD_DIM ** (-0.5)
    ).reshape(key_rows, -1)
    grad_value = jnp.einsum(
        "hqk,qhd->khd", probs.astype(jnp.bfloat16), grad_heads, preferred_element_type=jnp.float32
    ).reshape(key_rows, -1)
    return (
        grad_query,
        jnp.sum(score_sums, axis=2).T,
        grad_key,
        grad_value,
        -jnp.sum(score_sums, axis=1).T,
    )


def body(
    tokens,
    attn_gain,
    query_weight,
    key_weight,
    value_weight,
    forget_weight,
    forget_bias,
    out_weight,
    ffn_gain,
    gate_weight,
    up_weight,
    down_weight,
    doc_lengths,
    out_grad,
):
    local_rows = tokens.shape[0]
    local_heads = forget_bias.shape[0]
    head_cols = local_heads * HEAD_DIM
    n_seq = lax.axis_size("seq")
    my_index = lax.axis_index("seq")
    first_row = my_index * local_rows
    doc_ends = jnp.cumsum(doc_lengths)
    local_pos = stored_positions(
        first_row + jnp.arange(local_rows, dtype=jnp.int32), n_seq, local_rows
    )
    local_docs = doc_index(local_pos, doc_ends)
    pos_low = jnp.min(local_pos)
    pos_high = jnp.max(local_pos)
    doc_low = jnp.min(local_docs)
    doc_high = jnp.max(local_docs)
    w_query, w_key, w_value, w_forget, w_out, w_gate, w_up, w_down = (
        lax.all_gather(query_weight, "seq", axis=0, tiled=True),
        lax.all_gather(key_weight, "seq", axis=0, tiled=True),
        lax.all_gather(value_weight, "seq", axis=0, tiled=True),
        lax.all_gather(forget_weight, "seq", axis=0, tiled=True),
        lax.all_gather(out_weight, "seq", axis=1, tiled=True),
        lax.all_gather(gate_weight, "seq", axis=0, tiled=True),
        lax.all_gather(up_weight, "seq", axis=0, tiled=True),
        lax.all_gather(down_weight, "seq", axis=1, tiled=True),
    )
    inputs = tokens.astype(jnp.float32)
    normed_one, inverse_one, scaled_one = norm_rows(inputs, attn_gain)
    h_one = scaled_one.astype(jnp.bfloat16)
    query_flat = jnp.dot(h_one, w_query, preferred_element_type=jnp.float32).astype(jnp.bfloat16)
    key_flat = jnp.dot(h_one, w_key, preferred_element_type=jnp.float32).astype(jnp.bfloat16)
    value_flat = jnp.dot(h_one, w_value, preferred_element_type=jnp.float32).astype(jnp.bfloat16)
    forget_logit = jnp.dot(h_one, w_forget, preferred_element_type=jnp.float32) + forget_bias
    log_forget_all = lax.all_gather(jax.nn.log_sigmoid(forget_logit), "seq", axis=0, tiled=True)
    offsets_all = to_stored(jnp.cumsum(to_positions(log_forget_all, n_seq), axis=0), n_seq)
    offsets = lax.dynamic_slice_in_dim(offsets_all, first_row, local_rows, 0)
    query_heads = query_flat.reshape(local_rows, local_heads, HEAD_DIM)
    key_heads = key_flat.reshape(local_rows, local_heads, HEAD_DIM)
    value_heads = value_flat.reshape(local_rows, local_heads, HEAD_DIM)

    def key_range(piece_rows):
        key_pos = stored_positions(jnp.arange(piece_rows, dtype=jnp.int32), n_seq, local_rows)
        key_docs = doc_index(key_pos, doc_ends)
        is_live = (
            (jnp.min(key_pos) <= pos_high)
            & (jnp.max(key_docs) >= doc_low)
            & (jnp.min(key_docs) <= doc_high)
        )
        return (key_pos, key_docs, offsets_all, is_live)

    mass_state = (
        jnp.full((local_heads, local_rows), MASKED, jnp.float32),
        jnp.zeros((local_heads, local_rows), jnp.float32),
    )
    key_block = lax.all_gather(key_flat, "seq", axis=0, tiled=True)
    piece_rows = key_block.shape[0]
    key_pos, key_docs, key_offsets, is_live = key_range(piece_rows)

    def mass_update(carried_in):
        running_max, running_sum = carried_in
        scores, allowed = block_scores(
            query_heads,
            key_block.reshape(piece_rows, local_heads, HEAD_DIM),
            offsets,
            key_offsets,
            local_pos,
            key_pos,
            local_docs,
            key_docs,
        )
        new_max = jnp.maximum(running_max, jnp.max(scores, axis=2))
        weights = jnp.where(allowed[None], jnp.exp(scores - new_max[:, :, None]), 0.0)
        return (new_max, jnp.sum(weights, axis=2))

    running_max, running_sum = lax.cond(is_live, mass_update, unchanged, mass_state)
    log_mass = running_max + jnp.log(running_sum)
    start_state = (
        jnp.zeros((local_heads, local_rows, HEAD_DIM), jnp.float32),
        jnp.zeros((local_heads, local_rows, HEAD_DIM), jnp.float32),
    )
    attend_key_block = lax.all_gather(key_flat, "seq", axis=0, tiled=True)
    value_block = lax.all_gather(value_flat, "seq", axis=0, tiled=True)
    attend_piece_rows = attend_key_block.shape[0]
    attend_key_pos, attend_key_docs, attend_key_offsets, is_live = key_range(attend_piece_rows)

    def attend_update(carried_in):
        scores, allowed = block_scores(
            query_heads,
            attend_key_block.reshape(attend_piece_rows, local_heads, HEAD_DIM),
            offsets,
            attend_key_offsets,
            local_pos,
            attend_key_pos,
            local_docs,
            attend_key_docs,
        )
        probs = jnp.where(allowed[None], jnp.exp(scores - log_mass[:, :, None]), 0.0)
        probs_low = probs.astype(jnp.bfloat16)
        remainder = (probs - probs_low.astype(jnp.float32)).astype(jnp.bfloat16)
        value_piece = value_block.reshape(attend_piece_rows, local_heads, HEAD_DIM)
        rounded_acc = jnp.einsum(
            "hqk,khd->hqd", probs_low, value_piece, preferred_element_type=jnp.float32
        )
        remainder_acc = jnp.einsum(
            "hqk,khd->hqd", remainder, value_piece, preferred_element_type=jnp.float32
        )
        return (rounded_acc, remainder_acc)

    rounded_acc, remainder_acc = lax.cond(is_live, attend_update, unchanged, start_state)
    attended_rows = rounded_acc.transpose(1, 0, 2)
    exact_rows = (rounded_acc + remainder_acc).transpose(1, 0, 2)
    mixed = attended_rows.reshape(local_rows, head_cols).astype(jnp.bfloat16)
    attn_part = jnp.dot(mixed, w_out, preferred_element_type=jnp.float32)
    middle = inputs + lax.psum(attn_part, "head")
    normed_two, inverse_two, scaled_two = norm_rows(middle, ffn_gain)
    h_two = scaled_two.astype(jnp.bfloat16)
    gate_value = jnp.dot(h_two, w_gate, preferred_element_type=jnp.float32)
    up_value = jnp.dot(h_two, w_up, preferred_element_type=jnp.float32)
    gate_sigmoid = jax.nn.sigmoid(gate_value)
    gate_silu = gate_value * gate_sigmoid
    activation = (gate_silu * up_value).astype(jnp.bfloat16)
    ffn_part = jnp.dot(activation, w_down, preferred_element_type=jnp.float32)
    layer_out = (
        middle + lax.psum(ffn_part.astype(jnp.bfloat16), "head").astype(jnp.float32)
    ).astype(jnp.bfloat16)
    grad_act = contract_cols(out_grad, w_down)
    grad_gate = (
        grad_act * up_value * gate_sigmoid * (1.0 + gate_value * (1.0 - gate_sigmoid))
    ).astype(jnp.bfloat16)
    grad_up = (grad_act * gate_silu).astype(jnp.bfloat16)
    part_two = contract_cols(grad_gate, w_gate) + contract_cols(grad_up, w_up)
    grad_two = lax.psum(part_two, "head")
    back_two, gain_two = norm_back(grad_two, normed_two, inverse_two, ffn_gain)
    grad_middle = out_grad.astype(jnp.float32) + back_two
    grad_attn = grad_middle.astype(jnp.bfloat16)
    grad_mixed = contract_cols(grad_attn, w_out).astype(jnp.bfloat16)
    grad_heads = grad_mixed.reshape(local_rows, local_heads, HEAD_DIM)
    row_delta = jnp.sum(grad_heads.astype(jnp.float32) * exact_rows, axis=2).T
    back_state = (
        jnp.zeros((local_rows, head_cols), jnp.float32),
        jnp.zeros((local_rows, local_heads), jnp.float32),
    )
    back_key_block = lax.all_gather(key_flat, "seq", axis=0, tiled=True)
    back_value_block = lax.all_gather(value_flat, "seq", axis=0, tiled=True)
    back_piece_rows = back_key_block.shape[0]
    back_key_pos, back_key_docs, back_key_offsets, is_live = key_range(back_piece_rows)

    def back_update(carried_in):
        terms = piece_grads(
            query_heads,
            grad_heads,
            log_mass,
            row_delta,
            offsets,
            back_key_block.reshape(back_piece_rows, local_heads, HEAD_DIM),
            back_value_block.reshape(back_piece_rows, local_heads, HEAD_DIM),
            back_key_offsets,
            local_pos,
            back_key_pos,
            local_docs,
            back_key_docs,
        )
        return (terms[0], terms[1])

    grad_query, grad_query_off = lax.cond(is_live, back_update, unchanged, back_state)
    stats_mass, stats_delta = (
        lax.all_gather(log_mass.T, "seq", axis=0, tiled=True),
        lax.all_gather(row_delta.T, "seq", axis=0, tiled=True),
    )
    key_state = (
        jnp.zeros((local_rows, head_cols), jnp.float32),
        jnp.zeros((local_rows, head_cols), jnp.float32),
        jnp.zeros((local_rows, local_heads), jnp.float32),
    )
    piece_query = lax.all_gather(query_flat, "seq", axis=0, tiled=True)
    piece_grad = lax.all_gather(grad_mixed, "seq", axis=0, tiled=True)
    key_piece_rows = piece_query.shape[0]
    piece_pos = stored_positions(jnp.arange(key_piece_rows, dtype=jnp.int32), n_seq, local_rows)
    piece_docs = doc_index(piece_pos, doc_ends)
    is_live = (
        (pos_low <= jnp.max(piece_pos))
        & (jnp.max(piece_docs) >= doc_low)
        & (jnp.min(piece_docs) <= doc_high)
    )

    def key_update(carried_in):
        piece_mass = stats_mass.T
        piece_delta = stats_delta.T
        terms = piece_grads(
            piece_query.reshape(key_piece_rows, local_heads, HEAD_DIM),
            piece_grad.reshape(key_piece_rows, local_heads, HEAD_DIM),
            piece_mass,
            piece_delta,
            offsets_all,
            key_heads,
            value_heads,
            offsets,
            piece_pos,
            local_pos,
            piece_docs,
            local_docs,
        )
        return (terms[2], terms[3], terms[4])

    grad_key, grad_value, grad_key_off = lax.cond(is_live, key_update, unchanged, key_state)
    grad_query_low = (grad_query * HEAD_DIM ** (-0.5)).astype(jnp.bfloat16)
    grad_key_low = grad_key.astype(jnp.bfloat16)
    grad_value_low = grad_value.astype(jnp.bfloat16)
    grad_offsets = grad_query_off + grad_key_off
    grad_off_all = lax.all_gather(grad_offsets, "seq", axis=0, tiled=True)
    ordered_grads = to_positions(grad_off_all, n_seq)
    suffix_sums = jnp.flip(jnp.cumsum(jnp.flip(ordered_grads, 0), axis=0), 0)
    grad_log = lax.dynamic_slice_in_dim(to_stored(suffix_sums, n_seq), first_row, local_rows, 0)
    grad_logit = grad_log * jax.nn.sigmoid(-forget_logit)
    forget_table = w_forget.astype(jnp.float32)
    part_one = (
        contract_cols(grad_query_low, w_query)
        + contract_cols(grad_key_low, w_key)
        + contract_cols(grad_value_low, w_value)
        + lax.dot_general(grad_logit, forget_table, (((1,), (1,)), ((), ())), precision=HIGHEST)
    )
    grad_one = lax.psum(part_one.astype(jnp.bfloat16), "head").astype(jnp.float32)
    back_one, gain_one = norm_back(grad_one, normed_one, inverse_one, attn_gain)
    tokens_grad = (grad_middle + back_one).astype(jnp.bfloat16)
    weight_terms = (
        contract_rows(h_one, grad_query_low),
        contract_rows(h_one, grad_key_low),
        contract_rows(h_one, grad_value_low),
        lax.dot_general(
            h_one.astype(jnp.float32), grad_logit, (((0,), (0,)), ((), ())), precision=HIGHEST
        ),
        contract_rows(mixed, grad_attn),
        contract_rows(h_two, grad_gate),
        contract_rows(h_two, grad_up),
        contract_rows(activation, out_grad),
    )
    (
        query_weight_grad,
        key_weight_grad,
        value_weight_grad,
        forget_weight_grad,
        out_weight_grad,
        gate_weight_grad,
        up_weight_grad,
        down_weight_grad,
    ) = (
        lax.psum_scatter(
            weight_terms[0].astype(jnp.bfloat16), "seq", scatter_dimension=0, tiled=True
        ).astype(jnp.float32),
        lax.psum_scatter(
            weight_terms[1].astype(jnp.bfloat16), "seq", scatter_dimension=0, tiled=True
        ).astype(jnp.float32),
        lax.psum_scatter(
            weight_terms[2].astype(jnp.bfloat16), "seq", scatter_dimension=0, tiled=True
        ).astype(jnp.float32),
        lax.psum_scatter(
            weight_terms[3].astype(jnp.bfloat16), "seq", scatter_dimension=0, tiled=True
        ).astype(jnp.float32),
        lax.psum_scatter(
            weight_terms[4].astype(jnp.bfloat16), "seq", scatter_dimension=1, tiled=True
        ).astype(jnp.float32),
        lax.psum_scatter(
            weight_terms[5].astype(jnp.bfloat16), "seq", scatter_dimension=0, tiled=True
        ).astype(jnp.float32),
        lax.psum_scatter(
            weight_terms[6].astype(jnp.bfloat16), "seq", scatter_dimension=0, tiled=True
        ).astype(jnp.float32),
        lax.psum_scatter(
            weight_terms[7].astype(jnp.bfloat16), "seq", scatter_dimension=1, tiled=True
        ).astype(jnp.float32),
    )
    attn_gain_grad, ffn_gain_grad, forget_bias_grad = lax.psum(
        (gain_one, gain_two, jnp.sum(grad_logit, axis=0)), "seq"
    )
    return (
        layer_out,
        tokens_grad,
        attn_gain_grad,
        query_weight_grad,
        key_weight_grad,
        value_weight_grad,
        forget_weight_grad,
        forget_bias_grad,
        out_weight_grad,
        ffn_gain_grad,
        gate_weight_grad,
        up_weight_grad,
        down_weight_grad,
    )


def solution(mesh):
    return jax.shard_map(
        body,
        mesh=mesh,
        in_specs=(
            P("seq", None),
            P(),
            P("seq", "head"),
            P("seq", "head"),
            P("seq", "head"),
            P("seq", "head"),
            P("head"),
            P("head", "seq"),
            P(),
            P("seq", "head"),
            P("seq", "head"),
            P("head", "seq"),
            P(),
            P("seq", None),
        ),
        out_specs=(
            P("seq", None),
            P("seq", None),
            P(),
            P("seq", "head"),
            P("seq", "head"),
            P("seq", "head"),
            P("seq", "head"),
            P("head"),
            P("head", "seq"),
            P(),
            P("seq", "head"),
            P("seq", "head"),
            P("head", "seq"),
        ),
        check_vma=False,
    )
```

profile of v0, /device:TPU:0, one launch (start us, length us, event | category | flops | bytes accessed | tf_op | source)
XLA Modules:
  0.0 1260.1 jit_solution(11489083903228579848)
XLA Ops:
  10.9 43.1 %all-gather.13.cloned.1.call-done = bf16[1536,384]{1,0:T(8,128)(2,1)} async-done(((bf16[192,384]{1,0:T(8,128)(2,1)}), bf16[1536,384]{1,0:T(8,128)(2,1)}) %all-gather.13.cloned.1.call-update) | async-done | bytes 1179664 | tf_op jit(solution)/shard_map/all_gather | solution.py:162
  56.9 39.1 %all-gather.19.cloned.1.call-done = bf16[1536,384]{1,0:T(8,128)(2,1)} async-done(((bf16[192,384]{1,0:T(8,128)(2,1)}), bf16[1536,384]{1,0:T(8,128)(2,1)}) %all-gather.19.cloned.1.call-update) | async-done | bytes 1179664 | tf_op jit(solution)/shard_map/all_gather | solution.py:163
  106.2 30.5 %all-gather = bf16[8,192,6]{1,2,0:T(8,128)(2,1)S(1)} all-gather(bf16[1,192,6]{1,2,0:T(8,128)(2,1)S(1)} %bitcast.248), channel_id=1, replica_groups=mesh['seq'=8,'head'=4] {'seq'}, dimensions={0}, use_global_device_ids=true | all-gather | bytes 20736 | tf_op jit(solution)/shard_map/all_gather | solution.py:164
  137.8 30.6 %all_gather.55 = f32[2048,6]{0,1:T(8,128)S(1)} all-gather(f32[256,6]{0,1:T(8,128)S(1)} %get-tuple-element.364), channel_id=1, replica_groups=mesh['seq'=8,'head'=4] {'seq'}, dimensions={0}, use_global_device_ids=true | all-gather | bytes 55296 | tf_op jit(solution)/shard_map/all_gather | solution.py:177
  173.1 10.8 all-gather.15.cloned.1.call-done
  183.9 12.6 %conditional.4 = (f32[6,256]{1,0:T(8,128)}, f32[6,256]{1,0:T(8,128)S(1)}) conditional(s32[]{:T(128)} %convert_element_type.186, () %tuple.47, (s32[256]{0:T(256)S(1)}, s32[2048]{0:T(1024)S(1)}, s32[2048]{0:T(1024)S(1)}, s32[256]{0:T(256)S(1)}, bf16[2048,384]{1,0:T(8,128)(2,1)}, /*index=5*/bf16[256,6,64]{0,2,1:T(8,128)(2,1)S(1)}, ...), branch_computations={%region_12.13_spmd, %region_13.16_spmd} | conditional | flops 441973248 | bytes 31825936 | solution.py:218
  190.5 6.0 select_reduce_fusion
  197.8 31.7 %all-gather.21.cloned.1.call-done = bf16[2048,384]{1,0:T(8,128)(2,1)} async-done(((bf16[256,384]{1,0:T(8,128)(2,1)}), bf16[2048,384]{1,0:T(8,128)(2,1)}) %all-gather.21.cloned.1.call-update) | async-done | bytes 1572880 | tf_op jit(solution)/shard_map/all_gather | solution.py:225
  229.5 18.8 %conditional.5 = (f32[6,256,64]{1,2,0:T(8,128)S(1)}, f32[6,256,64]{1,2,0:T(8,128)S(1)}) conditional(s32[]{:T(128)} %convert_element_type.186, () %tuple.46, (s32[256]{0:T(256)S(1)}, s32[2048]{0:T(1024)S(1)}, s32[2048]{0:T(1024)S(1)}, s32[256]{0:T(256)S(1)}, bf16[2048,384]{1,0:T(8,128)(2,1)}, /*index=5*/bf16[256,6,64]{0,2,1:T(8,128)(2,1)S(1)}, ...), branch_computations={%region_16.17_spmd, %region_17.18_spmd} | conditional | flops 1263009792 | bytes 64038984 | solution.py:252
  242.9 5.4 fusion.2
  248.3 23.1 %all-gather.23.cloned.1.call-done = bf16[384,1536]{0,1:T(8,128)(2,1)} async-done(((bf16[384,192]{0,1:T(8,128)(2,1)}), bf16[384,1536]{0,1:T(8,128)(2,1)}) %all-gather.23.cloned.1.call-update) | async-done | bytes 1179664 | tf_op jit(solution)/shard_map/all_gather | solution.py:165
  277.0 39.3 %all-reduce.6.cloned.1.call-done = f32[256,1536]{1,0:T(8,128)} async-done(((f32[256,1536]{1,0:T(8,128)}), f32[256,1536]{1,0:T(8,128)}) %all-reduce.6.cloned.1.call-update) | async-done | bytes 1572880 | tf_op jit(solution)/shard_map/psum | solution.py:257
  318.2 60.8 %all-gather.25.cloned.1.call-done = bf16[1536,1024]{1,0:T(8,128)(2,1)} async-done(((bf16[192,1024]{1,0:T(8,128)(2,1)}), bf16[1536,1024]{1,0:T(8,128)(2,1)}) %all-gather.25.cloned.1.call-update) | async-done | bytes 3145744 | tf_op jit(solution)/shard_map/all_gather | solution.py:166
  382.9 57.4 %all-gather.27.cloned.1.call-done = bf16[1536,1024]{1,0:T(8,128)(2,1)} async-done(((bf16[192,1024]{1,0:T(8,128)(2,1)}), bf16[1536,1024]{1,0:T(8,128)(2,1)}) %all-gather.27.cloned.1.call-update) | async-done | bytes 3145744 | tf_op jit(solution)/shard_map/all_gather | solution.py:167
  444.2 57.3 %all-gather.29.cloned.1.call-done = bf16[1024,1536]{0,1:T(8,128)(2,1)} async-done(((bf16[1024,192]{0,1:T(8,128)(2,1)}), bf16[1024,1536]{0,1:T(8,128)(2,1)}) %all-gather.29.cloned.1.call-update) | async-done | bytes 3145744 | tf_op jit(solution)/shard_map/all_gather | solution.py:168
  511.3 41.0 %all-reduce.8.cloned.1.call-done = f32[256,1536]{1,0:T(8,128)} async-done(((f32[256,1536]{1,0:T(8,128)}), f32[256,1536]{1,0:T(8,128)}) %all-reduce.8.cloned.1.call-update) | async-done | bytes 1572880 | tf_op jit(solution)/shard_map/psum | solution.py:275
  561.5 21.4 %conditional.6 = (f32[256,384]{0,1:T(8,128)}, f32[256,6]{0,1:T(8,128)S(1)}) conditional(s32[]{:T(128)} %convert_element_type.186, () %tuple.50, (s32[256]{0:T(256)}, s32[2048]{0:T(1024)S(1)}, s32[2048]{0:T(1024)S(1)}, s32[256]{0:T(256)}, bf16[2048,384]{1,0:T(8,128)(2,1)}, /*index=5*/bf16[256,6,64]{0,2,1:T(8,128)(2,1)S(1)}, f32[256,6]{0,1:T(8,128)}, ...), branch_computations={%region_24.25_spmd, %region_25.27_spmd} | conditional | flops 1244133888 | bytes 64063644 | solution.py:308
  571.7 8.4 convert_reduce_fusion
  589.7 32.8 %all_gather.63 = f32[2048,6]{0,1:T(8,128)} all-gather(f32[256,6]{0,1:T(8,128)} %bitcast.42), channel_id=1, replica_groups=mesh['seq'=8,'head'=4] {'seq'}, dimensions={0}, use_global_device_ids=true | all-gather | bytes 55296 | tf_op jit(solution)/shard_map/all_gather | solution.py:310
  626.5 32.6 %all_gather.65 = f32[2048,6]{0,1:T(8,128)} all-gather(f32[256,6]{0,1:T(8,128)S(1)} %copy-done.39), channel_id=1, replica_groups=mesh['seq'=8,'head'=4] {'seq'}, dimensions={0}, use_global_device_ids=true | all-gather | bytes 55296 | tf_op jit(solution)/shard_map/all_gather | solution.py:311
  661.9 26.9 %conditional.7 = (f32[256,6]{0,1:T(8,128)}, bf16[256,384]{0,1:T(8,128)(2,1)S(1)}, bf16[256,384]{0,1:T(8,128)(2,1)S(1)}) conditional(s32[]{:T(128)} %convert_element_type.206, () %tuple.52, (s32[2048]{0:T(1024)S(1)}, s32[256]{0:T(256)}, s32[256]{0:T(256)}, s32[2048]{0:T(1024)S(1)}, bf16[2048,384]{1,0:T(8,128)(2,1)}, ...), branch_computations={%region_29.30_spmd, %region_30.32_spmd} | conditional | flops 1669103616 | bytes 81920328 | solution.py:348
  673.5 9.1 convert_reduce_fusion.1
  689.6 32.5 %all_gather.66 = f32[2048,6]{0,1:T(8,128)} all-gather(f32[256,6]{0,1:T(8,128)S(1)} %add.282), channel_id=1, replica_groups=mesh['seq'=8,'head'=4] {'seq'}, dimensions={0}, use_global_device_ids=true | all-gather | bytes 55296 | tf_op jit(solution)/shard_map/all_gather | solution.py:353
  727.9 8.1 rev.21
  792.2 48.7 %reduce-scatter.25.cloned.1.call-done = bf16[192,6]{1,0:T(8,128)(2,1)} async-done(((bf16[1536,6]{1,0:T(8,128)(2,1)}), bf16[192,6]{1,0:T(8,128)(2,1)}) %reduce-scatter.25.cloned.1.call-update) | async-done | bytes 2320
  842.3 43.4 %all-reduce.10.cloned.1.call-done = (bf16[256,1536]{1,0:T(8,128)(2,1)}, bf16[256,1536]{1,0:T(8,128)(2,1)}) async-done(((bf16[256,1536]{1,0:T(8,128)(2,1)}, bf16[256,1536]{1,0:T(8,128)(2,1)}), (bf16[256,1536]{1,0:T(8,128)(2,1)}, bf16[256,1536]{1,0:T(8,128)(2,1)})) %all-reduce.10.cloned.1.call-update) | async-done | bytes 1572880 | tf_op jit(solution)/shard_map/psum | solution.py:267
  887.8 37.8 %all-reduce = (f32[1536]{0:T(1024)}, f32[6]{0:T(128)}, f32[1536]{0:T(1024)}) all-reduce(f32[1536]{0:T(1024)S(1)} %get-tuple-element.332, f32[6]{0:T(128)S(1)} %copy-done.52, f32[1536]{0:T(1024)S(1)} %copy-done.40), channel_id=1, replica_groups=mesh['seq'=8,'head'=4] {'seq'}, use_global_device_ids=true, to_apply=%region_37.38 | all-reduce | flops 3078 | bytes 24624 | tf_op jit(solution)/shard_map/psum | solution.py:415
  929.3 23.8 %reduce-scatter.13.cloned.1.call-done = bf16[192,384]{1,0:T(8,128)(2,1)} async-done(((bf16[1536,384]{1,0:T(8,128)(2,1)}), bf16[192,384]{1,0:T(8,128)(2,1)}) %reduce-scatter.13.cloned.1.call-update) | async-done | bytes 147472 | tf_op jit(solution)/shard_map/reduce_scatter | solution.py:393
  954.8 64.8 %reduce-scatter.15.cloned.1.call-done = bf16[192,384]{1,0:T(8,128)(2,1)} async-done(((bf16[1536,384]{1,0:T(8,128)(2,1)}), bf16[192,384]{1,0:T(8,128)(2,1)}) %reduce-scatter.15.cloned.1.call-update) | async-done | bytes 147472 | tf_op jit(solution)/shard_map/reduce_scatter | solution.py:396
  1021.2 75.3 %reduce-scatter.19.cloned.1.call-done = bf16[192,1024]{1,0:T(8,128)(2,1)} async-done(((bf16[1536,1024]{1,0:T(8,128)(2,1)}), bf16[192,1024]{1,0:T(8,128)(2,1)}) %reduce-scatter.19.cloned.1.call-update) | async-done | bytes 393232 | tf_op jit(solution)/shard_map/reduce_scatter | solution.py:405
  1098.4 75.2 %reduce-scatter.21.cloned.1.call-done = bf16[192,1024]{1,0:T(8,128)(2,1)} async-done(((bf16[1536,1024]{1,0:T(8,128)(2,1)}), bf16[192,1024]{1,0:T(8,128)(2,1)}) %reduce-scatter.21.cloned.1.call-update) | async-done | bytes 393232 | tf_op jit(solution)/shard_map/reduce_scatter | solution.py:408
  1175.6 75.3 %reduce-scatter.23.cloned.1.call-done = bf16[1024,192]{0,1:T(8,128)(2,1)} async-done(((bf16[1024,1536]{0,1:T(8,128)(2,1)}), bf16[1024,192]{0,1:T(8,128)(2,1)}) %reduce-scatter.23.cloned.1.call-update) | async-done | bytes 393232 | tf_op jit(solution)/shard_map/reduce_scatter | solution.py:411
  (285 shorter events, 194.9 us)
Async XLA Ops:
  7.2 46.8 %all-gather.13.cloned.1.call-start = ((), (), s32[]{:S(2)}) async-start(), calls=%async_computation.8 | async-start | bytes 1327104 | tf_op jit(solution)/shard_map/all_gather | solution.py:162
  7.9 88.1 %all-gather.19.cloned.1.call-start = ((), (), s32[]{:S(2)}) async-start(), calls=%async_computation.11 | async-start | bytes 1327104 | tf_op jit(solution)/shard_map/all_gather | solution.py:163
  8.7 162.4 %all-gather.17.cloned.1.call-start = ((), (), s32[]{:S(2)}) async-start(), calls=%async_computation.10 | async-start | bytes 1327104 | tf_op jit(solution)/shard_map/all_gather | solution.py:161
  9.4 174.5 %all-gather.15.cloned.1.call-start = ((), (), s32[]{:S(2)}) async-start(), calls=%async_computation.9 | async-start | bytes 1769472 | tf_op jit(solution)/shard_map/all_gather | solution.py:224
  10.8 160.2 %copy-start.47 = (f32[256]{0:T(256)}, f32[256]{0:T(256)S(1)}, u32[]{:S(2)}) copy-start(f32[256]{0:T(256)S(1)} %add_rsqrt_fusion.1) | copy-start | bytes 3076
  10.8 85.2 %copy-start.1 = (bf16[256,1536]{1,0:T(8,128)(2,1)S(1)}, bf16[256,1536]{1,0:T(8,128)(2,1)}, u32[]{:S(2)}) copy-start(bf16[256,1536]{1,0:T(8,128)(2,1)} %param.22) | copy-start | bytes 2359300
  10.8 85.2 %copy-start.32 = (f32[1536]{0:T(1024)S(1)}, f32[1536]{0:T(1024)}, u32[]{:S(2)}) copy-start(f32[1536]{0:T(1024)} %param.23) | copy-start | bytes 18436
  56.9 79.9 %copy-start.54 = (f32[6]{0:T(128)S(1)}, f32[6]{0:T(128)}, u32[]{:S(2)}) copy-start(f32[6]{0:T(128)} %param.28) | copy-start | bytes 76
  56.9 172.6 %all-gather.21.cloned.1.call-start = ((), (), s32[]{:S(2)}) async-start(), calls=%async_computation.12 | async-start | bytes 1769472 | tf_op jit(solution)/shard_map/all_gather | solution.py:225
  98.6 172.8 %all-gather.23.cloned.1.call-start = ((), (), s32[]{:S(2)}) async-start(), calls=%async_computation.13 | async-start | bytes 1327104 | tf_op jit(solution)/shard_map/all_gather | solution.py:165
  99.2 217.1 %all-reduce.6.cloned.1.call-start = ((), (), s32[]{:S(2)}) async-start(), calls=%async_computation.14 | async-start | bytes 3145728 | tf_op jit(solution)/shard_map/psum | solution.py:257
  99.3 130.2 %copy-start.44 = (s32[256]{0:T(256)}, s32[256]{0:T(256)S(1)}, u32[]{:S(2)}) copy-start(s32[256]{0:T(256)S(1)} %fusion.56) | copy-start | bytes 3076
  99.6 129.9 %copy-start.36 = (s32[256]{0:T(256)}, s32[256]{0:T(256)S(1)}, u32[]{:S(2)}) copy-start(s32[256]{0:T(256)S(1)} %convert_reduce_fusion.3) | copy-start | bytes 3076
  274.5 104.5 %all-gather.25.cloned.1.call-start = ((), (), s32[]{:S(2)}) async-start(), calls=%async_computation.15 | async-start | bytes 3538944 | tf_op jit(solution)/shard_map/all_gather | solution.py:166
  275.3 165.1 %all-gather.27.cloned.1.call-start = ((), (), s32[]{:S(2)}) async-start(), calls=%async_computation.16 | async-start | bytes 3538944 | tf_op jit(solution)/shard_map/all_gather | solution.py:167
  276.0 225.5 %all-gather.29.cloned.1.call-start = ((), (), s32[]{:S(2)}) async-start(), calls=%async_computation.17 | async-start | bytes 3538944 | tf_op jit(solution)/shard_map/all_gather | solution.py:168
  276.6 275.7 %all-reduce.8.cloned.1.call-start = ((), (), s32[]{:S(2)}) async-start(), calls=%async_computation.18 | async-start | bytes 3145728 | tf_op jit(solution)/shard_map/psum | solution.py:275
  318.2 122.1 %copy-start.4 = (bf16[256,1536]{1,0:T(8,128)(2,1)}, bf16[256,1536]{1,0:T(8,128)(2,1)S(1)}, u32[]{:S(2)}) copy-start(bf16[256,1536]{1,0:T(8,128)(2,1)S(1)} %multiply_convert_fusion.2) | copy-start | bytes 2359300
  382.9 118.5 %copy-start.9 = (bf16[256,1536]{1,0:T(8,128)(2,1)S(1)}, bf16[256,1536]{1,0:T(8,128)(2,1)}, u32[]{:S(2)}) copy-start(bf16[256,1536]{1,0:T(8,128)(2,1)} %param.35) | copy-start | bytes 2359300
  510.7 151.3 %all-gather.31.cloned.1.call-start = ((), (), s32[]{:S(2)}) async-start(), calls=%async_computation.19 | async-start | bytes 1769472 | tf_op jit(solution)/shard_map/all_gather | solution.py:318
  511.2 150.7 %all-gather.33.cloned.1.call-start = ((), (), s32[]{:S(2)}) async-start(), calls=%async_computation.20 | async-start | bytes 1769472 | tf_op jit(solution)/shard_map/all_gather | solution.py:319
  557.9 231.0 %reduce-scatter.11.cloned.1.call-start = ((), (), s32[]{:S(2)}) async-start(), calls=%async_computation.21 | async-start | bytes 1327104 | tf_op jit(solution)/shard_map/reduce_scatter | solution.py:390
  586.0 204.6 %reduce-scatter.17.cloned.1.call-start = ((), (), s32[]{:S(2)}) async-start(), calls=%async_computation.24 | async-start | bytes 1327104 | tf_op jit(solution)/shard_map/reduce_scatter | solution.py:402
  587.7 253.1 %reduce-scatter.25.cloned.1.call-start = ((), (), s32[]{:S(2)}) async-start(), calls=%async_computation.28 | async-start | bytes 442368
  765.1 120.7 %all-reduce.10.cloned.1.call-start = ((), (), s32[]{:S(2)}) async-start(), calls=%async_computation.29 | async-start | bytes 3145728 | tf_op jit(solution)/shard_map/psum | solution.py:267
  770.2 182.9 %reduce-scatter.13.cloned.1.call-start = ((), (), s32[]{:S(2)}) async-start(), calls=%async_computation.22 | async-start | bytes 1327104 | tf_op jit(solution)/shard_map/reduce_scatter | solution.py:393
  773.8 245.8 %reduce-scatter.15.cloned.1.call-start = ((), (), s32[]{:S(2)}) async-start(), calls=%async_computation.23 | async-start | bytes 1327104 | tf_op jit(solution)/shard_map/reduce_scatter | solution.py:396
  776.7 319.8 %reduce-scatter.19.cloned.1.call-start = ((), (), s32[]{:S(2)}) async-start(), calls=%async_computation.25 | async-start | bytes 3538944 | tf_op jit(solution)/shard_map/reduce_scatter | solution.py:405
  780.7 392.9 %reduce-scatter.21.cloned.1.call-start = ((), (), s32[]{:S(2)}) async-start(), calls=%async_computation.26 | async-start | bytes 3538944 | tf_op jit(solution)/shard_map/reduce_scatter | solution.py:408
  784.7 466.2 %reduce-scatter.23.cloned.1.call-start = ((), (), s32[]{:S(2)}) async-start(), calls=%async_computation.27 | async-start | bytes 3538944 | tf_op jit(solution)/shard_map/reduce_scatter | solution.py:411
  788.9 99.0 %copy-start.40 = (f32[1536]{0:T(1024)S(1)}, f32[1536]{0:T(1024)}, u32[]{:S(2)}) copy-start(f32[1536]{0:T(1024)} %get-tuple-element.330) | copy-start | bytes 18436
  788.9 99.0 %copy-start.52 = (f32[6]{0:T(128)S(1)}, f32[6]{0:T(128)}, u32[]{:S(2)}) copy-start(f32[6]{0:T(128)} %get-tuple-element.343) | copy-start | bytes 76
  (45 other events, 679.8 us)
Sparse Core Ops, SparseCore 0:
  10.2 43.7 all-gather.12
  56.2 39.8 all-gather.18
  98.2 39.9 all-gather.16
  140.8 43.0 all-gather.14
  186.5 42.9 all-gather.20
  231.5 39.8 all-gather.22
  274.6 41.6 all-reduce.5
  318.5 60.4 all-gather.24
  381.2 59.0 all-gather.26
  442.3 59.0 all-gather.28
  510.8 41.4 all-reduce.7
  554.3 44.1 all-gather.30
  601.3 43.3 all-gather.32
  647.9 63.0 reduce-scatter.10
  714.2 63.0 reduce-scatter.16
  780.5 60.3 reduce-scatter.24
  843.7 42.0 all-reduce.9
  889.0 64.0 reduce-scatter.12
  956.5 62.9 reduce-scatter.14
  1023.0 73.4 reduce-scatter.18
  1100.1 73.4 reduce-scatter.20
  1177.2 73.6 reduce-scatter.22
where the time goes:
time: 1270 us; the launch traced here: 1260 us
  waiting for transfers between devices  815 us (64%)
  blocking collectives  197 us (16%)
  matrix products  115 us (9%)
  other arithmetic  55.6 us (4%)
  local copies, waits for them, and re-layouts  54.8 us (4%)
  between operations  20.6 us (2%)
    reduce_scatter x1, waiting for transfers between devices, body(): lax.psum_scatter(weight_terms[7].astype(jnp.bfloat16), 'seq', scatter_dim...  75.3 us
    reduce_scatter x1, waiting for transfers between devices, body(): lax.psum_scatter(weight_terms[5].astype(jnp.bfloat16), 'seq', scatter_dim...  75.3 us
    reduce_scatter x1, waiting for transfers between devices, body(): lax.psum_scatter(weight_terms[6].astype(jnp.bfloat16), 'seq', scatter_dim...  75.2 us
    reduce_scatter x1, waiting for transfers between devices, body(): lax.psum_scatter(weight_terms[2].astype(jnp.bfloat16), 'seq', scatter_dim...  64.8 us
    all_gather x1, waiting for transfers between devices, body(): lax.all_gather(gate_weight, 'seq', axis=0, tiled=True)  60.8 us
    all_gather x1, waiting for transfers between devices, body(): lax.all_gather(up_weight, 'seq', axis=0, tiled=True)  57.4 us
    all_gather x1, waiting for transfers between devices, body(): lax.all_gather(down_weight, 'seq', axis=1, tiled=True)  57.3 us
    unnamed x23, waiting for transfers between devices  53.9 us
  transfers between devices with their start and end apart: 22, of which 17 were waited for; matrix products, arithmetic and copies ran while one was open for 17% of the time, Pallas kernels for 0%

commit v1 on v0

--- a/solution.py
+++ b/solution.py
@@ -49,24 +49,6 @@
     within = rows % local_rows
     group_of = jnp.where(within < half_rows, device_of, 2 * n_seq - 1 - device_of)
     return group_of * half_rows + within % half_rows
-
-
-def to_positions(stored, n_seq):
-    columns = stored.shape[1]
-    half_rows = stored.shape[0] // (2 * n_seq)
-    parts = stored.reshape(n_seq, 2, half_rows, columns)
-    first = parts[:, 0]
-    second = jnp.flip(parts[:, 1], 0)
-    return jnp.concatenate([first, second], axis=0).reshape(-1, columns)
-
-
-def to_stored(ordered, n_seq):
-    columns = ordered.shape[1]
-    half_rows = ordered.shape[0] // (2 * n_seq)
-    parts = ordered.reshape(2 * n_seq, half_rows, columns)
-    first = parts[:n_seq]
-    second = jnp.flip(parts[n_seq:], 0)
-    return jnp.stack([first, second], axis=1).reshape(-1, columns)
 
 
 def block_scores(
@@ -148,7 +130,8 @@
     n_seq = lax.axis_size("seq")
     my_index = lax.axis_index("seq")
     first_row = my_index * local_rows
-    doc_ends = jnp.cumsum(doc_lengths)
+    docs = doc_lengths.shape[0]
+    doc_ends = jnp.sum(jnp.where(jnp.tri(docs, dtype=jnp.bool_), doc_lengths[None, :], 0), axis=1)
     local_pos = stored_positions(
         first_row + jnp.arange(local_rows, dtype=jnp.int32), n_seq, local_rows
     )
@@ -157,16 +140,28 @@
     pos_high = jnp.max(local_pos)
     doc_low = jnp.min(local_docs)
     doc_high = jnp.max(local_docs)
-    w_query, w_key, w_value, w_forget, w_out, w_gate, w_up, w_down = (
-        lax.all_gather(query_weight, "seq", axis=0, tiled=True),
-        lax.all_gather(key_weight, "seq", axis=0, tiled=True),
-        lax.all_gather(value_weight, "seq", axis=0, tiled=True),
-        lax.all_gather(forget_weight, "seq", axis=0, tiled=True),
-        lax.all_gather(out_weight, "seq", axis=1, tiled=True),
-        lax.all_gather(gate_weight, "seq", axis=0, tiled=True),
-        lax.all_gather(up_weight, "seq", axis=0, tiled=True),
-        lax.all_gather(down_weight, "seq", axis=1, tiled=True),
-    )
+    hidden = gate_weight.shape[1]
+    forget_pad = jnp.pad(forget_weight, ((0, 0), (0, 128 - local_heads)))
+    w_attn = lax.all_gather(
+        jnp.concatenate([query_weight, key_weight, value_weight, forget_pad], axis=1),
+        "seq",
+        axis=0,
+        tiled=True,
+    )
+    w_rest = lax.all_gather(
+        jnp.concatenate([out_weight.T, gate_weight, up_weight, down_weight.T], axis=1),
+        "seq",
+        axis=0,
+        tiled=True,
+    )
+    w_query = w_attn[:, :head_cols]
+    w_key = w_attn[:, head_cols : 2 * head_cols]
+    w_value = w_attn[:, 2 * head_cols : 3 * head_cols]
+    w_forget = w_attn[:, 3 * head_cols : 3 * head_cols + local_heads]
+    w_out_t = w_rest[:, :head_cols]
+    w_gate = w_rest[:, head_cols : head_cols + hidden]
+    w_up = w_rest[:, head_cols + hidden : head_cols + 2 * hidden]
+    w_down_t = w_rest[:, head_cols + 2 * hidden :]
     inputs = tokens.astype(jnp.float32)
     normed_one, inverse_one, scaled_one = norm_rows(inputs, attn_gain)
     h_one = scaled_one.astype(jnp.bfloat16)
@@ -175,7 +170,11 @@
     value_flat = jnp.dot(h_one, w_value, preferred_element_type=jnp.float32).astype(jnp.bfloat16)
     forget_logit = jnp.dot(h_one, w_forget, preferred_element_type=jnp.float32) + forget_bias
     log_forget_all = lax.all_gather(jax.nn.log_sigmoid(forget_logit), "seq", axis=0, tiled=True)
-    offsets_all = to_stored(jnp.cumsum(to_positions(log_forget_all, n_seq), axis=0), n_seq)
+    all_pos = stored_positions(
+        jnp.arange(n_seq * local_rows, dtype=jnp.int32), n_seq, local_rows
+    )
+    earlier = (all_pos[None, :] <= all_pos[:, None]).astype(jnp.float32)
+    offsets_all = jnp.dot(earlier, log_forget_all, precision=HIGHEST)
     offsets = lax.dynamic_slice_in_dim(offsets_all, first_row, local_rows, 0)
     query_heads = query_flat.reshape(local_rows, local_heads, HEAD_DIM)
     key_heads = key_flat.reshape(local_rows, local_heads, HEAD_DIM)
@@ -195,7 +194,10 @@
         jnp.full((local_heads, local_rows), MASKED, jnp.float32),
         jnp.zeros((local_heads, local_rows), jnp.float32),
     )
-    key_block = lax.all_gather(key_flat, "seq", axis=0, tiled=True)
+    gathered = lax.all_gather(
+        jnp.concatenate([key_flat, value_flat, query_flat], axis=1), "seq", axis=0, tiled=True
+    )
+    key_block = gathered[:, :head_cols]
     piece_rows = key_block.shape[0]
     key_pos, key_docs, key_offsets, is_live = key_range(piece_rows)
 
@@ -221,8 +223,8 @@
         jnp.zeros((local_heads, local_rows, HEAD_DIM), jnp.float32),
         jnp.zeros((local_heads, local_rows, HEAD_DIM), jnp.float32),
     )
-    attend_key_block = lax.all_gather(key_flat, "seq", axis=0, tiled=True)
-    value_block = lax.all_gather(value_flat, "seq", axis=0, tiled=True)
+    attend_key_block = key_block
+    value_block = gathered[:, head_cols : 2 * head_cols]
     attend_piece_rows = attend_key_block.shape[0]
     attend_key_pos, attend_key_docs, attend_key_offsets, is_live = key_range(attend_piece_rows)
 
@@ -253,7 +255,7 @@
     attended_rows = rounded_acc.transpose(1, 0, 2)
     exact_rows = (rounded_acc + remainder_acc).transpose(1, 0, 2)
     mixed = attended_rows.reshape(local_rows, head_cols).astype(jnp.bfloat16)
-    attn_part = jnp.dot(mixed, w_out, preferred_element_type=jnp.float32)
+    attn_part = contract_cols(mixed, w_out_t)
     middle = inputs + lax.psum(attn_part, "head")
     normed_two, inverse_two, scaled_two = norm_rows(middle, ffn_gain)
     h_two = scaled_two.astype(jnp.bfloat16)
@@ -262,11 +264,11 @@
     gate_sigmoid = jax.nn.sigmoid(gate_value)
     gate_silu = gate_value * gate_sigmoid
     activation = (gate_silu * up_value).astype(jnp.bfloat16)
-    ffn_part = jnp.dot(activation, w_down, preferred_element_type=jnp.float32)
+    ffn_part = contract_cols(activation, w_down_t)
     layer_out = (
         middle + lax.psum(ffn_part.astype(jnp.bfloat16), "head").astype(jnp.float32)
     ).astype(jnp.bfloat16)
-    grad_act = contract_cols(out_grad, w_down)
+    grad_act = jnp.dot(out_grad, w_down_t, preferred_element_type=jnp.float32)
     grad_gate = (
         grad_act * up_value * gate_sigmoid * (1.0 + gate_value * (1.0 - gate_sigmoid))
     ).astype(jnp.bfloat16)
@@ -276,15 +278,17 @@
     back_two, gain_two = norm_back(grad_two, normed_two, inverse_two, ffn_gain)
     grad_middle = out_grad.astype(jnp.float32) + back_two
     grad_attn = grad_middle.astype(jnp.bfloat16)
-    grad_mixed = contract_cols(grad_attn, w_out).astype(jnp.bfloat16)
+    grad_mixed = jnp.dot(grad_attn, w_out_t, preferred_element_type=jnp.float32).astype(
+        jnp.bfloat16
+    )
     grad_heads = grad_mixed.reshape(local_rows, local_heads, HEAD_DIM)
     row_delta = jnp.sum(grad_heads.astype(jnp.float32) * exact_rows, axis=2).T
     back_state = (
         jnp.zeros((local_rows, head_cols), jnp.float32),
         jnp.zeros((local_rows, local_heads), jnp.float32),
     )
-    back_key_block = lax.all_gather(key_flat, "seq", axis=0, tiled=True)
-    back_value_block = lax.all_gather(value_flat, "seq", axis=0, tiled=True)
+    back_key_block = key_block
+    back_value_block = value_block
     back_piece_rows = back_key_block.shape[0]
     back_key_pos, back_key_docs, back_key_offsets, is_live = key_range(back_piece_rows)
 
@@ -306,16 +310,16 @@
         return (terms[0], terms[1])
 
     grad_query, grad_query_off = lax.cond(is_live, back_update, unchanged, back_state)
-    stats_mass, stats_delta = (
-        lax.all_gather(log_mass.T, "seq", axis=0, tiled=True),
-        lax.all_gather(row_delta.T, "seq", axis=0, tiled=True),
-    )
+    stats = lax.all_gather(
+        jnp.concatenate([log_mass.T, row_delta.T], axis=1), "seq", axis=0, tiled=True
+    )
+    stats_mass, stats_delta = stats[:, :local_heads], stats[:, local_heads:]
     key_state = (
         jnp.zeros((local_rows, head_cols), jnp.float32),
         jnp.zeros((local_rows, head_cols), jnp.float32),
         jnp.zeros((local_rows, local_heads), jnp.float32),
     )
-    piece_query = lax.all_gather(query_flat, "seq", axis=0, tiled=True)
+    piece_query = gathered[:, 2 * head_cols :]
     piece_grad = lax.all_gather(grad_mixed, "seq", axis=0, tiled=True)
     key_piece_rows = piece_query.shape[0]
     piece_pos = stored_positions(jnp.arange(key_piece_rows, dtype=jnp.int32), n_seq, local_rows)
@@ -351,9 +355,8 @@
     grad_value_low = grad_value.astype(jnp.bfloat16)
     grad_offsets = grad_query_off + grad_key_off
     grad_off_all = lax.all_gather(grad_offsets, "seq", axis=0, tiled=True)
-    ordered_grads = to_positions(grad_off_all, n_seq)
-    suffix_sums = jnp.flip(jnp.cumsum(jnp.flip(ordered_grads, 0), axis=0), 0)
-    grad_log = lax.dynamic_slice_in_dim(to_stored(suffix_sums, n_seq), first_row, local_rows, 0)
+    later = (all_pos[None, :] >= local_pos[:, None]).astype(jnp.float32)
+    grad_log = jnp.dot(later, grad_off_all, precision=HIGHEST)
     grad_logit = grad_log * jax.nn.sigmoid(-forget_logit)
     forget_table = w_forget.astype(jnp.float32)
     part_one = (
@@ -365,53 +368,39 @@
     grad_one = lax.psum(part_one.astype(jnp.bfloat16), "head").astype(jnp.float32)
     back_one, gain_one = norm_back(grad_one, normed_one, inverse_one, attn_gain)
     tokens_grad = (grad_middle + back_one).astype(jnp.bfloat16)
-    weight_terms = (
+    forget_term = lax.dot_general(
+        h_one.astype(jnp.float32), grad_logit, (((0,), (0,)), ((), ())), precision=HIGHEST
+    )
+    scatter_cols = [
+        contract_rows(grad_attn, mixed),
+        contract_rows(h_two, grad_gate),
+        contract_rows(h_two, grad_up),
+        contract_rows(out_grad, activation),
         contract_rows(h_one, grad_query_low),
         contract_rows(h_one, grad_key_low),
         contract_rows(h_one, grad_value_low),
-        lax.dot_general(
-            h_one.astype(jnp.float32), grad_logit, (((0,), (0,)), ((), ())), precision=HIGHEST
-        ),
-        contract_rows(mixed, grad_attn),
-        contract_rows(h_two, grad_gate),
-        contract_rows(h_two, grad_up),
-        contract_rows(activation, out_grad),
-    )
-    (
-        query_weight_grad,
-        key_weight_grad,
-        value_weight_grad,
-        forget_weight_grad,
-        out_weight_grad,
-        gate_weight_grad,
-        up_weight_grad,
-        down_weight_grad,
-    ) = (
-        lax.psum_scatter(
-            weight_terms[0].astype(jnp.bfloat16), "seq", scatter_dimension=0, tiled=True
-        ).astype(jnp.float32),
-        lax.psum_scatter(
-            weight_terms[1].astype(jnp.bfloat16), "seq", scatter_dimension=0, tiled=True
-        ).astype(jnp.float32),
-        lax.psum_scatter(
-            weight_terms[2].astype(jnp.bfloat16), "seq", scatter_dimension=0, tiled=True
-        ).astype(jnp.float32),
-        lax.psum_scatter(
-            weight_terms[3].astype(jnp.bfloat16), "seq", scatter_dimension=0, tiled=True
-        ).astype(jnp.float32),
-        lax.psum_scatter(
-            weight_terms[4].astype(jnp.bfloat16), "seq", scatter_dimension=1, tiled=True
-        ).astype(jnp.float32),
-        lax.psum_scatter(
-            weight_terms[5].astype(jnp.bfloat16), "seq", scatter_dimension=0, tiled=True
-        ).astype(jnp.float32),
-        lax.psum_scatter(
-            weight_terms[6].astype(jnp.bfloat16), "seq", scatter_dimension=0, tiled=True
-        ).astype(jnp.float32),
-        lax.psum_scatter(
-            weight_terms[7].astype(jnp.bfloat16), "seq", scatter_dimension=1, tiled=True
-        ).astype(jnp.float32),
-    )
+        jnp.pad(forget_term, ((0, 0), (0, 128 - local_heads))),
+    ]
+    first_sum = lax.psum_scatter(
+        jnp.concatenate([t.astype(jnp.bfloat16) for t in scatter_cols[:4]], axis=1),
+        "seq",
+        scatter_dimension=0,
+        tiled=True,
+    ).astype(jnp.float32)
+    second_sum = lax.psum_scatter(
+        jnp.concatenate([t.astype(jnp.bfloat16) for t in scatter_cols[4:]], axis=1),
+        "seq",
+        scatter_dimension=0,
+        tiled=True,
+    ).astype(jnp.float32)
+    out_weight_grad = first_sum[:, :head_cols].T
+    gate_weight_grad = first_sum[:, head_cols : head_cols + hidden]
+    up_weight_grad = first_sum[:, head_cols + hidden : head_cols + 2 * hidden]
+    down_weight_grad = first_sum[:, head_cols + 2 * hidden :].T
+    query_weight_grad = second_sum[:, :head_cols]
+    key_weight_grad = second_sum[:, head_cols : 2 * head_cols]
+    value_weight_grad = second_sum[:, 2 * head_cols : 3 * head_cols]
+    forget_weight_grad = second_sum[:, 3 * head_cols : 3 * head_cols + local_heads]
     attn_gain_grad, ffn_gain_grad, forget_bias_grad = lax.psum(
         (gain_one, gain_two, jnp.sum(grad_logit, axis=0)), "seq"
     )

time: 1270 us -> 918 us (0.72)
  waiting for transfers between devices: 815 us -> 533 us
  blocking collectives: 197 us -> 134 us
  local copies, waits for them, and re-layouts: 54.8 us -> 69.3 us
    reduce_scatter x7 -> x0, waiting for transfers between devices: 314 us -> none  [the longest x1 75.3 us: body(): lax.psum_scatter(weight_terms[7].astype(jnp.bfloat16), 'seq', scatter_dim...]
    unnamed x23 -> x11, waiting for transfers between devices: 53.9 us -> 223 us
    all_gather x10 -> x3, waiting for transfers between devices: 323 us -> 217 us  [the longest x1 114 us: body(): lax.all_gather(jnp.concatenate([out_weight.T, gate_weight, up_weight, dow...]
    all_gather x3 -> x1, blocking collectives: 95.9 us -> 32.6 us  [body(): lax.all_gather(jnp.concatenate([log_mass.T, row_delta.T], axis=1), 'seq',...]
    psum x1, waiting for transfers between devices: 43.4 us -> 8.99 us  [body(): lax.psum(ffn_part.astype(jnp.bfloat16), 'head').astype(jnp.float32)]
    unnamed x87 -> x100, local copies, waits for them, and re-layouts: 8 us -> 36.2 us
    concatenate x0 -> x6, other arithmetic: none -> 13.2 us  [the longest x1 4.99 us: body(): jnp.concatenate([t.astype(jnp.bfloat16) for t in scatter_cols[:4]], axis=1)]
    convert_element_type x8 -> x1, other arithmetic: 13.1 us -> 0.27 us  [body(): first_sum = lax.psum_scatter(jnp.concatenate([t.astype(jnp.bfloat16) for...]
  transfers between devices with their start and end apart: 22 -> 9, of which waited for: 17 -> 8; matrix products, arithmetic and copies ran while one was open for 17% -> 14% of each run, Pallas kernels for 0% -> 0%
where the time goes in v1:
time: 918 us; the launch traced here: 909 us
  waiting for transfers between devices  533 us (58%)
  blocking collectives  134 us (15%)
  matrix products  108 us (12%)
  local copies, waits for them, and re-layouts  69.3 us (8%)
  other arithmetic  43.9 us (5%)
  between operations  20.2 us (2%)
    unnamed x11, waiting for transfers between devices  223 us
    all_gather x1, waiting for transfers between devices, body(): lax.all_gather(jnp.concatenate([out_weight.T, gate_weight, up_weight, dow...  114 us
    all_gather x1, waiting for transfers between devices, body(): lax.all_gather(jnp.concatenate([query_weight, key_weight, value_weight, f...  72.1 us
    psum x1, waiting for transfers between devices, body(): grad_two = lax.psum(part_two, 'head')  43 us
    psum x1, waiting for transfers between devices, body(): middle = inputs + lax.psum(attn_part, 'head')  40.7 us
    psum x1, blocking collectives, body(): lax.psum((gain_one, gain_two, jnp.sum(grad_logit, axis=0)), 'seq')  39.4 us
    unnamed x100, local copies, waits for them, and re-layouts  36.2 us
    all_gather x1, blocking collectives, body(): lax.all_gather(jnp.concatenate([log_mass.T, row_delta.T], axis=1), 'seq',...  32.6 us
  transfers between devices with their start and end apart: 9, of which 8 were waited for; matrix products, arithmetic and copies ran while one was open for 14% of the time, Pallas kernels for 0%

profile of v1, /device:TPU:0, one launch (start us, length us, event | category | flops | bytes accessed | tf_op | source)
XLA Modules:
  0.0 909.3 jit_solution(12436164927727384056)
XLA Ops:
  11.5 72.1 %all-gather.5.cloned.1.call-done = bf16[1536,1280]{1,0:T(8,128)(2,1)} async-done(((bf16[192,1280]{1,0:T(8,128)(2,1)}), bf16[1536,1280]{1,0:T(8,128)(2,1)}) %all-gather.5.cloned.1.call-update) | async-done | bytes 3932176 | tf_op jit(solution)/shard_map/all_gather | solution.py:145
  101.0 30.9 %all_gather.23 = f32[2048,6]{0,1:T(8,128)S(1)} all-gather(f32[256,6]{0,1:T(8,128)S(1)} %get-tuple-element.412), channel_id=1, replica_groups=mesh['seq'=8,'head'=4] {'seq'}, dimensions={0}, use_global_device_ids=true | all-gather | bytes 55296 | tf_op jit(solution)/shard_map/all_gather | solution.py:172
  131.9 6.9 fusion.24
  138.8 30.7 %all-gather.7.cloned.1.call-done = bf16[2048,1152]{1,0:T(8,128)(2,1)} async-done(((bf16[256,1152]{1,0:T(8,128)(2,1)}), bf16[2048,1152]{1,0:T(8,128)(2,1)}) %all-gather.7.cloned.1.call-update) | async-done | bytes 4718608 | tf_op jit(solution)/shard_map/all_gather | solution.py:197
  172.9 14.2 %conditional.4 = (f32[6,256]{1,0:T(8,128)}, f32[6,256]{1,0:T(8,128)S(1)}) conditional(s32[]{:T(128)} %convert_element_type.175, () %tuple.47, (s32[256]{0:T(256)S(1)}, s32[2048]{0:T(1024)S(1)}, s32[2048]{0:T(1024)S(1)}, s32[256]{0:T(256)S(1)}, bf16[2048,384]{1,0:T(8,128)(2,1)S(1)}, /*index=5*/bf16[256,6,64]{0,2,1:T(8,128)(2,1)S(1)}, ...), branch_computations={%region_10.11_spmd, %region_11.14_spmd} | conditional | flops 441973248 | bytes 31825936 | solution.py:220
  175.2 5.2 fusion
  181.0 6.0 select_reduce_fusion
  188.4 18.7 %conditional.5 = (f32[6,256,64]{1,2,0:T(8,128)S(1)}, f32[6,256,64]{1,2,0:T(8,128)S(1)}) conditional(s32[]{:T(128)} %convert_element_type.175, () %tuple.46, (s32[256]{0:T(256)S(1)}, s32[2048]{0:T(1024)S(1)}, s32[2048]{0:T(1024)S(1)}, s32[256]{0:T(256)S(1)}, bf16[2048,384]{1,0:T(8,128)(2,1)S(1)}, /*index=5*/bf16[256,6,64]{0,2,1:T(8,128)(2,1)S(1)}, ...), branch_computations={%region_14.15_spmd, %region_15.16_spmd} | conditional | flops 1263009792 | bytes 57747500 | solution.py:254
  196.9 4.8 fusion.5
  201.7 5.4 fusion.2
  208.0 114.4 %all-gather.9.cloned.1.call-done = bf16[1536,3456]{1,0:T(8,128)(2,1)} async-done(((bf16[192,3456]{1,0:T(8,128)(2,1)}), bf16[1536,3456]{1,0:T(8,128)(2,1)}) %all-gather.9.cloned.1.call-update) | async-done | bytes 10616848 | tf_op jit(solution)/shard_map/all_gather | solution.py:151
  326.0 40.7 %all-reduce.8.cloned.1.call-done = f32[256,1536]{1,0:T(8,128)} async-done(((f32[256,1536]{1,0:T(8,128)}), f32[256,1536]{1,0:T(8,128)}) %all-reduce.8.cloned.1.call-update) | async-done | bytes 1572880 | tf_op jit(solution)/shard_map/psum | solution.py:259
  378.7 43.0 %all-reduce.10.cloned.1.call-done = f32[256,1536]{1,0:T(8,128)} async-done(((f32[256,1536]{1,0:T(8,128)}), f32[256,1536]{1,0:T(8,128)}) %all-reduce.10.cloned.1.call-update) | async-done | bytes 1572880 | tf_op jit(solution)/shard_map/psum | solution.py:277
  430.6 4.0 fusion.42
  437.3 21.2 %conditional.6 = (f32[256,384]{0,1:T(8,128)}, f32[256,6]{0,1:T(8,128)S(1)}) conditional(s32[]{:T(128)} %convert_element_type.175, () %tuple.50, (s32[256]{0:T(256)}, s32[2048]{0:T(1024)S(1)}, s32[2048]{0:T(1024)S(1)}, s32[256]{0:T(256)}, bf16[2048,384]{1,0:T(8,128)(2,1)}, /*index=5*/bf16[256,6,64]{0,2,1:T(8,128)(2,1)S(1)}, f32[256,6]{0,1:T(8,128)}, ...), branch_computations={%region_22.23_spmd, %region_23.25_spmd} | conditional | flops 1244133888 | bytes 64309488 | solution.py:312
  442.7 3.4 fusion.122
  447.4 8.2 convert_reduce_fusion
  459.8 32.6 %all_gather.25 = f32[2048,12]{0,1:T(8,128)} all-gather(f32[256,12]{0,1:T(8,128)S(1)} %pad_maximum_fusion.3), channel_id=1, replica_groups=mesh['seq'=8,'head'=4] {'seq'}, dimensions={0}, use_global_device_ids=true | all-gather | bytes 110592 | tf_op jit(solution)/shard_map/all_gather | solution.py:313
  498.2 35.3 %conditional.7 = (f32[256,6]{0,1:T(8,128)}, bf16[256,384]{0,1:T(8,128)(2,1)S(1)}, bf16[256,384]{0,1:T(8,128)(2,1)S(1)}) conditional(s32[]{:T(128)} %convert_element_type.195, () %tuple.52, (s32[2048]{0:T(1024)S(1)}, s32[256]{0:T(256)}, s32[256]{0:T(256)}, s32[2048]{0:T(1024)S(1)}, bf16[2048,1152]{1,0:T(8,128)(2,1)}, ...), branch_computations={%region_27.28_spmd, %region_28.30_spmd} | conditional | flops 1669103616 | bytes 91554120 | solution.py:352
  503.5 6.7 copy.99
  513.3 3.4 fusion.124
  518.2 9.1 %convert_reduce_fusion.1 = (f32[6,256]{1,0:T(8,128)S(1)}, bf16[6,2048,256]{2,1,0:T(8,128)(2,1)S(1)}) fusion(f32[6,2048]{1,0:T(8,128)S(1)} %copy-done.44, bf16[2048,6,64]{0,2,1:T(8,128)(2,1)S(1)} %bitcast.109, bf16[256,6,64]{0,2,1:T(8,128)(2,1)S(1)} %bitcast.119, f32[6,2048]{1,0:T(8,128)S(1)} %copy-done.43, f32[6,256]{1,0:T(8,128)S(1)} %bitcast.135, ...), kind=kOutput, calls=%fused_computation.21 | convolution fusion | flops 437254656 | bytes 21327872 | tf_op jit(solution)/shard_map/cond/branch_1_fun/qhd,khd->hqk/dot_general | solution.py:85
  529.1 4.4 fusion.17
  534.3 30.7 %all_gather.27 = f32[2048,6]{0,1:T(8,128)S(1)} all-gather(f32[256,6]{0,1:T(8,128)S(1)} %add.306), channel_id=1, replica_groups=mesh['seq'=8,'head'=4] {'seq'}, dimensions={0}, use_global_device_ids=true | all-gather | bytes 55296 | tf_op jit(solution)/shard_map/all_gather | solution.py:357
  576.6 3.5 fusion.29
  580.1 6.2 copy.111
  591.8 5.0 pad_maximum_fusion
  596.8 14.0 %copy.113 = bf16[1536,3456]{1,0:T(8,128)(2,1)} copy(bf16[1536,3456]{0,1:T(8,128)(2,1)} %pad_maximum_fusion) | data formatting | bytes 21233664
  610.8 9.0 all-reduce.12.cloned.1.call-done
  621.7 39.4 %all-reduce.2 = (f32[1536]{0:T(1024)}, f32[6]{0:T(128)}, f32[1536]{0:T(1024)}) all-reduce(f32[1536]{0:T(1024)S(1)} %get-tuple-element.381, f32[6]{0:T(128)S(1)} %copy-done.61, f32[1536]{0:T(1024)S(1)} %copy-done.51), channel_id=1, replica_groups=mesh['seq'=8,'head'=4] {'seq'}, use_global_device_ids=true, to_apply=%region_33.34 | all-reduce | flops 3078 | bytes 24624 | tf_op jit(solution)/shard_map/psum | solution.py:404
  664.8 43.5 %reduce-scatter.7.cloned.1.call-done = bf16[192,1280]{1,0:T(8,128)(2,1)} async-done(((bf16[1536,1280]{1,0:T(8,128)(2,1)}), bf16[192,1280]{1,0:T(8,128)(2,1)}) %reduce-scatter.7.cloned.1.call-update) | async-done | bytes 491536
  712.9 179.1 %reduce-scatter.9.cloned.1.call-done = bf16[192,3456]{1,0:T(8,128)(2,1)} async-done(((bf16[1536,3456]{1,0:T(8,128)(2,1)}), bf16[192,3456]{1,0:T(8,128)(2,1)}) %reduce-scatter.9.cloned.1.call-update) | async-done | bytes 1327120
  (241 shorter events, 125.6 us)
Async XLA Ops:
  7.2 76.4 %all-gather.5.cloned.1.call-start = ((), (), s32[]{:S(2)}) async-start(), calls=%async_computation.2 | async-start | bytes 4423680 | tf_op jit(solution)/shard_map/all_gather | solution.py:145
  8.1 77.7 %copy-start = (bf16[256,1536]{1,0:T(8,128)(2,1)S(1)}, bf16[256,1536]{1,0:T(8,128)(2,1)}, u32[]{:S(2)}) copy-start(bf16[256,1536]{1,0:T(8,128)(2,1)} %param.22) | copy-start | bytes 2359300
  8.1 77.7 %copy-start.35 = (f32[1536]{0:T(1024)S(1)}, f32[1536]{0:T(1024)}, u32[]{:S(2)}) copy-start(f32[1536]{0:T(1024)} %param.23) | copy-start | bytes 18436
  10.0 159.5 %all-gather.7.cloned.1.call-start = ((), (), s32[]{:S(2)}) async-start(), calls=%async_computation.3 | async-start | bytes 5308416 | tf_op jit(solution)/shard_map/all_gather | solution.py:197
  11.5 87.5 %copy-start.45 = (f32[256]{0:T(256)}, f32[256]{0:T(256)S(1)}, u32[]{:S(2)}) copy-start(f32[256]{0:T(256)S(1)} %add_rsqrt_fusion.1) | copy-start | bytes 3076
  90.6 8.4 copy-start.63
  90.7 231.7 %all-gather.9.cloned.1.call-start = ((), (), s32[]{:S(2)}) async-start(), calls=%async_computation.4 | async-start | bytes 11943936 | tf_op jit(solution)/shard_map/all_gather | solution.py:151
  91.9 274.7 %all-reduce.8.cloned.1.call-start = ((), (), s32[]{:S(2)}) async-start(), calls=%async_computation.5 | async-start | bytes 3145728 | tf_op jit(solution)/shard_map/psum | solution.py:259
  94.6 93.7 %copy-start.57 = (s32[256]{0:T(256)}, s32[256]{0:T(256)S(1)}, u32[]{:S(2)}) copy-start(s32[256]{0:T(256)S(1)} %fusion.100) | copy-start | bytes 3076
  94.8 93.5 %copy-start.48 = (s32[256]{0:T(256)}, s32[256]{0:T(256)S(1)}, u32[]{:S(2)}) copy-start(s32[256]{0:T(256)S(1)} %convert_reduce_fusion.3) | copy-start | bytes 3076
  138.8 49.6 %copy-start.39 = (f32[2048,6]{0,1:T(8,128)}, f32[2048,6]{0,1:T(8,128)S(1)}, u32[]{:S(2)}) copy-start(f32[2048,6]{0,1:T(8,128)S(1)} %fusion.24) | copy-start | bytes 147460
  138.8 49.6 %copy-start.54 = (f32[256,6]{0,1:T(8,128)}, f32[256,6]{0,1:T(8,128)S(1)}, u32[]{:S(2)}) copy-start(f32[256,6]{0,1:T(8,128)S(1)} %constant_dynamic-slice_fusion) | copy-start | bytes 18436
  172.9 15.5 %copy-start.4 = (bf16[2048,384]{1,0:T(8,128)(2,1)}, bf16[2048,384]{1,0:T(8,128)(2,1)S(1)}, u32[]{:S(2)}) copy-start(bf16[2048,384]{1,0:T(8,128)(2,1)S(1)} %get-tuple-element.403) | copy-start | bytes 4718596
  207.9 160.6 %copy-start.11 = (f32[6,256,64]{1,2,0:T(8,128)}, f32[6,256,64]{1,2,0:T(8,128)S(1)}, u32[]{:S(2)}) copy-start(f32[6,256,64]{1,2,0:T(8,128)S(1)} %get-tuple-element.156) | copy-start | bytes 1179652
  208.0 160.6 %copy-start.18 = (bf16[6,256,64]{1,2,0:T(8,128)(2,1)}, bf16[6,256,64]{1,2,0:T(8,128)(2,1)S(1)}, u32[]{:S(2)}) copy-start(bf16[6,256,64]{1,2,0:T(8,128)(2,1)S(1)} %convert_element_type.180) | copy-start | bytes 589828
  325.5 43.1 %copy-start.42 = (f32[1536]{0:T(1024)S(1)}, f32[1536]{0:T(1024)}, u32[]{:S(2)}) copy-start(f32[1536]{0:T(1024)} %param.30) | copy-start | bytes 18436
  325.5 96.2 %all-reduce.10.cloned.1.call-start = ((), (), s32[]{:S(2)}) async-start(), calls=%async_computation.6 | async-start | bytes 3145728 | tf_op jit(solution)/shard_map/psum | solution.py:277
  366.7 5.4 copy-start.15
  378.7 119.6 %all-gather.11.cloned.1.call-start = ((), (), s32[]{:S(2)}) async-start(), calls=%async_computation.7 | async-start | bytes 1769472 | tf_op jit(solution)/shard_map/all_gather | solution.py:323
  428.6 191.2 %all-reduce.12.cloned.1.call-start = ((), (), s32[]{:S(2)}) async-start(), calls=%async_computation.10 | async-start | bytes 3145728 | tf_op jit(solution)/shard_map/psum | solution.py:269
  447.4 8.3 copy-start.5
  518.2 9.7 %copy-start.6 = (bf16[2048,384]{0,1:T(8,128)(2,1)S(1)}, bf16[2048,384]{0,1:T(8,128)(2,1)}, u32[]{:S(2)}) copy-start(bf16[2048,384]{0,1:T(8,128)(2,1)} %slice.84) | copy-start | bytes 4718596 | tf_op jit(solution)/shard_map/cond
  533.5 38.2 %copy-start.36 = (f32[1536]{0:T(1024)S(1)}, f32[1536]{0:T(1024)}, u32[]{:S(2)}) copy-start(f32[1536]{0:T(1024)} %param.23) | copy-start | bytes 18436
  533.6 38.2 %copy-start.46 = (f32[256]{0:T(256)S(1)}, f32[256]{0:T(256)}, u32[]{:S(2)}) copy-start(f32[256]{0:T(256)} %copy-done.45) | copy-start | bytes 3076
  567.4 6.0 copy-start.7
  567.4 6.0 copy-start.10
  576.5 131.8 %reduce-scatter.7.cloned.1.call-start = ((), (), s32[]{:S(2)}) async-start(), calls=%async_computation.8 | async-start | bytes 4423680
  586.3 305.7 %reduce-scatter.9.cloned.1.call-start = ((), (), s32[]{:S(2)}) async-start(), calls=%async_computation.9 | async-start | bytes 11943936
  610.8 9.0 copy-start.47
  610.8 10.9 %copy-start.51 = (f32[1536]{0:T(1024)S(1)}, f32[1536]{0:T(1024)}, u32[]{:S(2)}) copy-start(f32[1536]{0:T(1024)} %get-tuple-element.379) | copy-start | bytes 18436
  610.8 10.9 %copy-start.61 = (f32[6]{0:T(128)S(1)}, f32[6]{0:T(128)}, u32[]{:S(2)}) copy-start(f32[6]{0:T(128)} %get-tuple-element.414) | copy-start | bytes 76
  619.8 43.7 %copy-start.14 = (bf16[256,1536]{1,0:T(8,128)(2,1)S(1)}, bf16[256,1536]{1,0:T(8,128)(2,1)}, u32[]{:S(2)}) copy-start(bf16[256,1536]{1,0:T(8,128)(2,1)} %get-tuple-element.391) | copy-start | bytes 2359300
  (41 other events, 129.4 us)
Sparse Core Ops, SparseCore 0:
  10.8 72.7 all-gather.4
  90.8 78.6 all-gather.6
  171.7 150.6 all-gather.8
  325.6 41.0 all-reduce.7
  378.8 42.8 all-reduce.9
  428.7 44.8 all-gather.10
  576.6 43.1 all-reduce.11
  623.5 84.8 reduce-scatter.6
  712.4 179.5 reduce-scatter.8

commit v2 on v1

--- a/solution.py
+++ b/solution.py
@@ -1,14 +1,1359 @@
+import functools
+import math
+
 import jax
 import jax.numpy as jnp
 from jax import lax
+from jax.experimental import pallas as pl
+from jax.experimental.pallas import tpu as pltpu
 from jax.sharding import PartitionSpec as P
 
 HEAD_DIM = 64
-
-
 EPSILON = 1e-06
 HIGHEST = lax.Precision.HIGHEST
 MASKED = -1e30
+MESH_ID = pl.DeviceIdType.MESH
+F32 = jnp.float32
+BF16 = jnp.bfloat16
+LANES = 128
+
+
+def dot_nn(left, right):
+    return jnp.dot(left, right, preferred_element_type=F32)
+
+
+def dot_nt(left, right):
+    return lax.dot_general(left, right, (((1,), (1,)), ((), ())), preferred_element_type=F32)
+
+
+class Net:
+    def __init__(self, n_seq, sems):
+        self.n_seq = n_seq
+        self.line = n_seq // 2
+        self.s = lax.axis_index("seq")
+        self.h = lax.axis_index("head")
+        self.z = self.s // 2
+        self.x = self.s % 2
+        self.y = self.h // 2
+        self.c = self.h % 2
+        self.sems = sems
+        self.used = 0
+        self.pending = []
+
+    def alloc(self, count):
+        first = self.used
+        self.used += count
+        return first
+
+    def at_line(self, z):
+        return (z * 2 + self.x, self.h)
+
+    def side(self):
+        return (self.z * 2 + 1 - self.x, self.h)
+
+    def lower(self):
+        return (self.s, self.y * 2 + 1 - self.c)
+
+    def upper(self):
+        return (self.s, (1 - self.y) * 2 + self.c)
+
+    def barrier(self):
+        sem = pltpu.get_barrier_semaphore()
+        for step in range(1, self.n_seq):
+            peer = (self.s + step) % self.n_seq
+            pl.semaphore_signal(sem, 1, device_id=(peer, self.h), device_id_type=MESH_ID)
+        for peer in (self.lower(), self.upper()):
+            pl.semaphore_signal(sem, 1, device_id=peer, device_id_type=MESH_ID)
+        pl.semaphore_wait(sem, self.n_seq + 1)
+
+    def copy(self, src, dst, send, recv, device):
+        return pltpu.make_async_remote_copy(
+            src_ref=src,
+            dst_ref=dst,
+            send_sem=self.sems.at[send],
+            recv_sem=self.sems.at[recv],
+            device_id=device,
+            device_id_type=MESH_ID,
+        )
+
+    def send(self, src, dst, device):
+        first = self.alloc(2)
+        made = self.copy(src, dst, first, first + 1, device)
+        made.start()
+        self.pending.append(made.wait_send)
+        return made
+
+    def drain(self):
+        for wait in self.pending:
+            wait()
+        self.pending = []
+
+
+class Line:
+    def __init__(self, net, slot):
+        self.net = net
+        self.slot = slot
+        self.recv = net.alloc(net.line)
+        self.direct = net.alloc(4)
+        self.passed = net.alloc(net.line)
+        self.deltas = [d for d in (1, -1, 2, -2) if abs(d) < net.line]
+
+    def own(self, index):
+        net = self.net
+        mine = self.slot(net.z)
+        return net.copy(
+            mine,
+            mine,
+            self.direct + index,
+            self.recv + net.z,
+            net.at_line((net.z + self.deltas[index] + net.line) % net.line),
+        )
+
+    def here(self, index):
+        to = self.net.z + self.deltas[index]
+        return (to >= 0) & (to < self.net.line)
+
+    def start(self):
+        for index in range(len(self.deltas)):
+            pl.when(self.here(index))(lambda index=index: self.own(index).start())
+
+    def handed(self, src, sign):
+        net = self.net
+        block = self.slot(src)
+        return net.copy(
+            block,
+            block,
+            self.passed + src,
+            self.recv + src,
+            net.at_line((net.z - sign + net.line) % net.line),
+        )
+
+    def each(self, act):
+        net = self.net
+        for k in range(1, net.line):
+            for sign in (-1, 1):
+                src = net.z + sign * k
+                there = (src >= 0) & (src < net.line)
+                onward = (net.z - sign >= 0) & (net.z - sign < net.line)
+                act(k, sign, (src + net.line) % net.line, there, onward)
+
+    def arrive(self, then=None):
+        def act(k, sign, src, there, onward):
+            @pl.when(there)
+            def _():
+                self.handed(src, sign).wait_recv()
+                if then is not None:
+                    then(src)
+                if k >= 2:
+                    pl.when(onward)(lambda: self.handed(src, sign).start())
+
+        self.each(act)
+
+    def drain(self):
+        for index in range(len(self.deltas)):
+            pl.when(self.here(index))(lambda index=index: self.own(index).wait_send())
+
+        def act(k, sign, src, there, onward):
+            if k >= 2:
+                pl.when(there & onward)(lambda: self.handed(src, sign).wait_send())
+
+        self.each(act)
+
+
+class Spread:
+    def __init__(self, net, slot):
+        self.net = net
+        self.slot = slot
+        self.along = Line(net, lambda z: slot(z * 2 + net.x))
+        self.sent = net.alloc(net.line)
+        self.got = net.alloc(net.line)
+
+    def across(self, z):
+        net = self.net
+        block = self.slot(z * 2 + net.x)
+        return net.copy(block, block, self.sent + z, self.got + z, net.side())
+
+    def start(self):
+        self.along.start()
+        self.across(self.net.z).start()
+
+    def arrive(self):
+        self.along.arrive(lambda z: self.across(z).start())
+
+    def finish(self):
+        net = self.net
+        for z in range(net.line):
+            block = self.slot(z * 2 + 1 - net.x)
+            net.copy(block, block, self.sent + z, self.got + z, net.side()).wait_recv()
+
+    def drain(self):
+        self.along.drain()
+        for z in range(self.net.line):
+            self.across(z).wait_send()
+
+
+def spread_small(net, slot):
+    recv = net.alloc(net.n_seq)
+    sent = net.alloc(net.n_seq)
+
+    def made(step):
+        mine = slot(net.s)
+        return net.copy(
+            mine, mine, sent + step, recv + step, ((net.s + step) % net.n_seq, net.h)
+        )
+
+    for step in range(1, net.n_seq):
+        made(step).start()
+        net.pending.append(made(step).wait_send)
+
+    def wait():
+        for step in range(1, net.n_seq):
+            src = slot((net.s - step + net.n_seq) % net.n_seq)
+            net.copy(src, src, sent + step, recv + step, net.side()).wait_recv()
+
+    return wait
+
+
+def rows_of(first, count):
+    return pl.ds(pl.multiple_of(first, 16), count)
+
+
+def doc_starts(positions, doc_ref, docs):
+    start = jnp.zeros(positions.shape, jnp.int32)
+    end = jnp.int32(0)
+    for k in range(docs - 1):
+        end = end + doc_ref[k]
+        start = jnp.where(positions >= end, end, start)
+    return start
+
+
+def forward_kernel(
+    n_seq,
+    docs,
+    heads,
+    tokens,
+    gain_one,
+    wq,
+    wk,
+    wv,
+    wf,
+    bias,
+    wo_t,
+    gain_two,
+    wg,
+    wu,
+    wd_t,
+    doc_ref,
+    og,
+    queries,
+    keyval,
+    offsets,
+    mass,
+    logit_t,
+    mixed,
+    exact,
+    middle,
+    normed_two,
+    out_grads,
+    w_attn,
+    w_out,
+    w_ffn,
+    h_one,
+    logs,
+    allowed,
+    proj,
+    recv_low,
+    recv_up,
+    half_out,
+    own_off,
+    sems,
+):
+    net = Net(n_seq, sems)
+    rows, width = tokens.shape
+    half = rows // 2
+    quarter = half // 2
+    block = wq.shape[0]
+    hc = wq.shape[1]
+    hidden = wg.shape[1] // 2
+    span = n_seq * half
+    s, z, x, y, c = net.s, net.z, net.x, net.y, net.c
+
+    def seq_rows(ref):
+        return lambda j: ref.at[rows_of(j * block, block), :]
+
+    attn_net = Spread(net, seq_rows(w_attn))
+    out_net = Spread(net, seq_rows(w_out))
+    ffn_net = Line(net, lambda j: w_ffn.at[rows_of(j * 2 * block, 2 * block), :])
+    kv_net = Spread(net, lambda j: keyval.at[:, j])
+
+    mine = rows_of(s * block, block)
+    for index, ref in enumerate((wq, wk, wv)):
+        w_attn[mine, index * hc : (index + 1) * hc] = ref[...]
+    w_attn[mine, 3 * hc :] = wf[...]
+    net.barrier()
+    attn_net.start()
+
+    w_out[mine, :] = wo_t[...]
+    for index, ref in enumerate((wg, wu, wd_t)):
+        cols = slice(index * hidden, (index + 1) * hidden)
+        w_ffn[mine, cols] = ref[:, pl.ds(pl.multiple_of(x * hidden, LANES), hidden)]
+        half_out[:, cols] = ref[:, pl.ds(pl.multiple_of((1 - x) * hidden, LANES), hidden)]
+
+    values_in = tokens[...].astype(F32)
+    inverse = lax.rsqrt(jnp.mean(values_in * values_in, axis=-1, keepdims=True) + EPSILON)
+    h_one[...] = (values_in * inverse * gain_one[...]).astype(BF16)
+    out_grads[rows_of(x * rows, rows), :] = og[...]
+
+    def key_positions(shape, axis):
+        at = lax.broadcasted_iota(jnp.int32, shape, axis)
+        late = at // span
+        owner = (at % span) // half
+        return jnp.where(late == 0, owner, 2 * n_seq - 1 - owner) * half + at % half
+
+    key_pos = key_positions((1, 2 * span), 1)
+    for part in range(2):
+        group = s if part == 0 else 2 * n_seq - 1 - s
+        pos = group * half + lax.broadcasted_iota(jnp.int32, (half, 1), 0)
+        start = doc_starts(pos, doc_ref, docs)
+        seen = (key_pos <= pos) & (key_pos >= start)
+        allowed[part * half : (part + 1) * half, :] = jnp.where(seen, 0.0, MASKED)
+
+    attn_net.arrive()
+    attn_net.finish()
+
+    tile = 256
+    for at in range(w_attn.shape[1] // tile):
+        cols = slice(at * tile, (at + 1) * tile)
+        proj[:, cols] = dot_nn(h_one[...], w_attn[:, cols])
+
+    logit = proj[:, 3 * hc : 3 * hc + LANES] + bias[...]
+    turned = logit.T[:8, :]
+    logit_t[...] = turned
+    logs[s] = jnp.minimum(turned, 0.0) - jnp.log(1.0 + jnp.exp(-jnp.abs(turned)))
+    wait_logs = spread_small(net, lambda j: logs.at[j])
+    for part in range(2):
+        keyval[part, s] = proj[part * half : (part + 1) * half, hc : 3 * hc].astype(BF16)
+    kv_net.start()
+    queries[...] = (proj[:, :hc].astype(BF16).astype(F32) * HEAD_DIM ** (-0.5)).astype(BF16)
+
+    wait_logs()
+    upto = (
+        lax.broadcasted_iota(jnp.int32, (half, half), 0)
+        <= lax.broadcasted_iota(jnp.int32, (half, half), 1)
+    ).astype(F32)
+    before = jnp.zeros((8, 1), F32)
+    for group in range(2 * n_seq):
+        owner = group if group < n_seq else 2 * n_seq - 1 - group
+        late = group // n_seq
+        piece = logs[owner, :, late * half : (late + 1) * half]
+        sums = jnp.dot(piece, upto, precision=HIGHEST, preferred_element_type=F32)
+        at = (late * n_seq + owner) * half
+        offsets[:, at : at + half] = sums + before
+        before = before + jnp.sum(piece, axis=1, keepdims=True)
+
+    kv_net.arrive()
+    half_send = net.send(half_out, w_ffn.at[mine, :], net.side())
+    out_net.start()
+    kv_net.finish()
+
+    lane = lax.broadcasted_iota(jnp.int32, (half, LANES), 1)
+    masses = [jnp.zeros((half, LANES), F32), jnp.zeros((half, LANES), F32)]
+    for pair in range(heads // 2):
+        cols = slice(pair * LANES, (pair + 1) * LANES)
+        vcols = slice(hc + pair * LANES, hc + (pair + 1) * LANES)
+        for part in range(2):
+            mine_rows = slice(part * half, (part + 1) * half)
+            many = span * (part + 1)
+            query_pair = queries[mine_rows, cols]
+            key_pair = keyval[: part + 1, :, :, cols].reshape(many, LANES)
+            value_pair = keyval[: part + 1, :, :, vcols].reshape(many, LANES)
+            low_out, full_out = [], []
+            for side in range(2):
+                head = pair * 2 + side
+                keep = (lane // HEAD_DIM) == side
+                query = jnp.where(keep, query_pair, jnp.zeros_like(query_pair))
+                scores = (
+                    dot_nt(query, key_pair)
+                    - offsets[head : head + 1, :many]
+                    + allowed[mine_rows, :many]
+                )
+                top = jnp.max(scores, axis=1, keepdims=True)
+                probs = jnp.exp(scores - top)
+                total = jnp.sum(probs, axis=1, keepdims=True)
+                high = probs.astype(BF16)
+                rest = (probs - high.astype(F32)).astype(BF16)
+                share = 1.0 / total
+                rounded = dot_nn(high, value_pair)
+                low_out.append(rounded * share)
+                full_out.append((rounded + dot_nn(rest, value_pair)) * share)
+                masses[part] = jnp.where(lane == head, top + jnp.log(total), masses[part])
+            first = (lane // HEAD_DIM) == 0
+            mixed[mine_rows, cols] = jnp.where(first, low_out[0], low_out[1]).astype(BF16)
+            exact[mine_rows, cols] = jnp.where(first, full_out[0], full_out[1])
+        if pair == 0:
+            out_net.arrive()
+            half_send.wait_recv()
+            ffn_net.start()
+            grads_send = net.send(
+                out_grads.at[rows_of(x * rows, rows), :],
+                out_grads.at[rows_of(x * rows, rows), :],
+                net.side(),
+            )
+    for part in range(2):
+        mass[part * half : (part + 1) * half, :] = masses[part]
+    out_net.finish()
+
+    for at in range(width // tile):
+        cols = slice(at * tile, (at + 1) * tile)
+        proj[:, cols] = dot_nt(mixed[...], w_out[cols, :])
+    low_send = net.send(proj.at[rows_of((1 - c) * half, half), :], recv_low, net.lower())
+    low_send.wait_recv()
+    keep_low = rows_of(c * half, half)
+    proj[keep_low, :] = proj[keep_low, :] + recv_low[...]
+    up_send = net.send(
+        proj.at[rows_of(c * half + (1 - y) * quarter, quarter), :], recv_up, net.upper()
+    )
+    up_send.wait_recv()
+    kept = c * half + y * quarter
+    own = rows_of(kept, quarter)
+    total = tokens[own, :].astype(F32) + (proj[own, :] + recv_up[...])
+    middle[...] = total
+    inverse = lax.rsqrt(jnp.mean(total * total, axis=-1, keepdims=True) + EPSILON)
+    here = rows_of(x * rows + kept, quarter)
+    normed_two[here, :] = (total * inverse * gain_two[...]).astype(BF16)
+    gather_rows(net, normed_two, rows)
+
+    ffn_net.arrive()
+    grads_send.wait_recv()
+    for part in (attn_net, out_net, ffn_net, kv_net, net):
+        part.drain()
+
+
+def gather_rows(net, ref, rows):
+    half, quarter = rows // 2, rows // 4
+    base = net.x * rows + net.c * half
+    piece = ref.at[rows_of(base + net.y * quarter, quarter), :]
+    net.send(piece, piece, net.upper()).wait_recv()
+    piece = ref.at[rows_of(base, half), :]
+    across = net.send(piece, piece, net.side())
+    first = net.send(piece, piece, net.lower())
+    across.wait_recv()
+    piece = ref.at[rows_of((1 - net.x) * rows + net.c * half, half), :]
+    second = net.send(piece, piece, net.lower())
+    first.wait_recv()
+    second.wait_recv()
+
+
+def run_forward(
+    n_seq, heads, tokens, attn_gain, wq, wk, wv, wf, bias, wo_t, ffn_gain, wg, wu, wd_t, docs, og
+):
+    rows, width = tokens.shape
+    hc = wq.shape[1]
+    hidden = wg.shape[1] // 2
+    half = rows // 2
+    span = n_seq * half
+    attn_cols = 3 * hc + LANES
+    vmem = pl.BlockSpec(memory_space=pltpu.VMEM)
+    outs = (
+        ((rows, hc), BF16),
+        ((2, n_seq, half, 2 * hc), BF16),
+        ((8, 2 * span), F32),
+        ((rows, LANES), F32),
+        ((8, rows), F32),
+        ((rows, hc), BF16),
+        ((rows, hc), F32),
+        ((rows // 4, width), F32),
+        ((2 * rows, width), BF16),
+        ((2 * rows, width), BF16),
+        ((width, attn_cols), BF16),
+        ((width, hc), BF16),
+        ((width, 3 * hidden), BF16),
+    )
+    return pl.pallas_call(
+        functools.partial(forward_kernel, n_seq, docs.shape[0], heads),
+        out_shape=[jax.ShapeDtypeStruct(*o) for o in outs],
+        in_specs=[vmem] * 12 + [pl.BlockSpec(memory_space=pltpu.SMEM), vmem],
+        out_specs=[vmem] * len(outs),
+        scratch_shapes=[
+            pltpu.VMEM((rows, width), BF16),
+            pltpu.VMEM((n_seq, 8, rows), F32),
+            pltpu.VMEM((rows, 2 * span), F32),
+            pltpu.VMEM((rows, width), F32),
+            pltpu.VMEM((half, width), F32),
+            pltpu.VMEM((half // 2, width), F32),
+            pltpu.VMEM((wq.shape[0], 3 * hidden), BF16),
+            pltpu.VMEM((rows, LANES), F32),
+            pltpu.SemaphoreType.DMA((160,)),
+        ],
+        compiler_params=pltpu.CompilerParams(
+            collective_id=0, has_side_effects=True, vmem_limit_bytes=58 << 20
+        ),
+    )(
+        tokens,
+        attn_gain.reshape(1, width),
+        wq,
+        wk,
+        wv,
+        jnp.pad(wf, ((0, 0), (0, LANES - heads))),
+        jnp.pad(bias, (0, LANES - heads)).reshape(1, LANES),
+        wo_t,
+        ffn_gain.reshape(1, width),
+        wg,
+        wu,
+        wd_t,
+        docs,
+        og,
+    )
+
+
+def dot_tn(left, right):
+    return lax.dot_general(left, right, (((0,), (0,)), ((), ())), preferred_element_type=F32)
+
+
+class LineReduce:
+    def __init__(self, net, block, slots, relay):
+        self.net = net
+        self.block = block
+        self.slots = slots
+        self.relay = relay
+        self.recv = net.alloc(4)
+        self.sent = net.alloc(net.line)
+        self.passing = net.alloc(2 * net.line)
+        counts = {min(z, 2) + min(net.line - 1 - z, 2) for z in range(net.line)}
+        self.counts = sorted(counts)
+        self.count = jnp.minimum(net.z, 2) + jnp.minimum(net.line - 1 - net.z, 2)
+
+    def held(self, sign, k):
+        line = self.net.line
+        if line <= 4:
+            return 0
+        return (0 if sign > 0 else line - 3) + k - 2
+
+    def made(self, sign, k):
+        net = self.net
+        line = net.line
+        to = (net.z + sign * k + 2 * line) % line
+        if k <= 2:
+            low = jnp.minimum(to, 2)
+            place = low - k if sign > 0 else low + k - 1
+            place = (place + 4) % 4
+            last = self.slots.shape[0] - 1
+            dst, recv, hop = self.slots.at[jnp.minimum(place, last)], self.recv + place, to
+        else:
+            index = self.held(sign, k - 1)
+            dst, recv = self.relay.at[index], self.passing + index
+            hop = (net.z + sign + line) % line
+        return net.copy(self.block(to), dst, self.sent + to, recv, net.at_line(hop))
+
+    def cases(self):
+        net = self.net
+        for k in range(net.line - 1, 0, -1):
+            for sign in (1, -1):
+                to = net.z + sign * k
+                back = net.z - sign
+                there = (to >= 0) & (to < net.line)
+                behind = (back >= 0) & (back < net.line)
+                yield sign, k, there, behind
+
+    def start(self):
+        for sign, k, there, behind in self.cases():
+            ready = there if k == 1 else there & jnp.logical_not(behind)
+            pl.when(ready)(lambda sign=sign, k=k: self.made(sign, k).start())
+
+    def hand_on(self):
+        net = self.net
+        for sign, k, there, behind in self.cases():
+            if k == 1:
+                continue
+
+            @pl.when(there & behind)
+            def _(sign=sign, k=k):
+                index = self.held(sign, k)
+                came = self.relay.at[index]
+                net.copy(came, came, self.sent, self.passing + index, net.side()).wait_recv()
+                mine = self.block((net.z + sign * k + 2 * net.line) % net.line)
+                mine[...] = (mine[...].astype(F32) + came[...].astype(F32)).astype(BF16)
+                self.made(sign, k).start()
+
+    def finish(self, use):
+        net = self.net
+        for many in self.counts:
+
+            @pl.when(self.count == many)
+            def _(many=many):
+                for index in range(many):
+                    slot = self.slots.at[index]
+                    net.copy(slot, slot, self.sent, self.recv + index, net.side()).wait_recv()
+                mine = self.block(net.z)
+
+                def total(rows):
+                    out = mine[rows, :].astype(F32)
+                    for index in range(many):
+                        out = out + self.slots[index, rows, :].astype(F32)
+                    return out
+
+                use(total)
+
+    def drain(self):
+        for sign, k, there, behind in self.cases():
+            pl.when(there)(lambda sign=sign, k=k: self.made(sign, k).wait_send())
+
+
+class SeqReduce:
+    def __init__(self, net, grads, across, slots, relay):
+        self.net = net
+        self.grads = grads
+        self.across = across
+        self.block = across.shape[1]
+        self.sent = net.alloc(net.line)
+        self.got = net.alloc(net.line)
+        self.along = LineReduce(net, lambda t: self.rows(t, net.x), slots, relay)
+
+    def rows(self, z, x):
+        return self.grads.at[rows_of((z * 2 + x) * self.block, self.block), :]
+
+    def made(self, z):
+        net = self.net
+        return net.copy(
+            self.rows(z, 1 - net.x), self.across.at[z], self.sent + z, self.got + z, net.side()
+        )
+
+    def start(self):
+        for z in range(self.net.line):
+            self.made(z).start()
+
+    def turn(self):
+        for z in range(self.net.line):
+            self.made(z).wait_recv()
+            mine = self.rows(z, self.net.x)
+            mine[...] = (mine[...].astype(F32) + self.across[z].astype(F32)).astype(BF16)
+        self.along.start()
+
+    def drain(self):
+        for z in range(self.net.line):
+            self.made(z).wait_send()
+        self.along.drain()
+
+
+class RowReduce:
+    def __init__(self, net, parts, recv_low, recv_side, recv_up):
+        self.net = net
+        self.parts = parts
+        self.rows = parts.shape[0] // 2
+        self.recv_low = recv_low
+        self.recv_side = recv_side
+        self.recv_up = recv_up
+
+    def piece(self, x, first, count):
+        return rows_of(x * self.rows + first, count)
+
+    def start(self):
+        net, half = self.net, self.rows // 2
+        self.low = [
+            net.send(
+                self.parts.at[self.piece(x, (1 - net.c) * half, half), :],
+                self.recv_low.at[x],
+                net.lower(),
+            )
+            for x in range(2)
+        ]
+
+    def second(self):
+        net, half = self.net, self.rows // 2
+        for x in range(2):
+            self.low[x].wait_recv()
+            at = self.piece(x, net.c * half, half)
+            self.parts[at, :] = (
+                self.parts[at, :].astype(F32) + self.recv_low[x].astype(F32)
+            ).astype(BF16)
+        self.across = net.send(
+            self.parts.at[self.piece(1 - net.x, net.c * half, half), :], self.recv_side, net.side()
+        )
+
+    def third(self):
+        net, half = self.net, self.rows // 2
+        self.across.wait_recv()
+        at = self.piece(net.x, net.c * half, half)
+        self.parts[at, :] = (
+            self.parts[at, :].astype(F32) + self.recv_side[...].astype(F32)
+        ).astype(BF16)
+        away = net.c * half + (1 - net.y) * (half // 2)
+        self.up = net.send(
+            self.parts.at[self.piece(net.x, away, half // 2), :], self.recv_up, net.upper()
+        )
+
+    def result(self):
+        net, half = self.net, self.rows // 2
+        self.up.wait_recv()
+        at = self.piece(net.x, net.c * half + net.y * (half // 2), half // 2)
+        return self.parts[at, :].astype(F32) + self.recv_up[...].astype(F32)
+
+
+def gather_quarters(net, ref):
+    half = ref.shape[0] // 2
+    base = net.c * half
+    piece = ref.at[rows_of(base + net.y * (half // 2), half // 2), :]
+    up = net.send(piece, piece, net.upper())
+
+    def second():
+        up.wait_recv()
+        whole = ref.at[rows_of(base, half), :]
+        return net.send(whole, whole, net.lower()).wait_recv
+
+    return second
+
+
+def norm_grad(grad_in, values_in, gain):
+    inverse = lax.rsqrt(jnp.mean(values_in * values_in, axis=-1, keepdims=True) + EPSILON)
+    normed = values_in * inverse
+    scaled = grad_in * gain
+    inner = jnp.mean(scaled * normed, axis=-1, keepdims=True)
+    return inverse * (scaled - normed * inner), jnp.sum(grad_in * normed, axis=0, keepdims=True)
+
+
+def to_columns(rows_in):
+    many = rows_in.shape[1]
+    return jnp.concatenate([rows_in, jnp.zeros((LANES - 8, many), F32)], axis=0).T
+
+
+def backward_kernel(
+    n_seq,
+    docs,
+    heads,
+    tokens,
+    gain_one,
+    gain_two,
+    queries,
+    keyval,
+    offsets,
+    mass,
+    logit_t,
+    mixed,
+    exact,
+    middle,
+    normed_two,
+    out_grads,
+    w_attn,
+    w_out,
+    w_ffn_far,
+    doc_ref,
+    layer_out,
+    tokens_grad,
+    gains,
+    bias_grad,
+    g_query,
+    g_key,
+    g_value,
+    g_forget,
+    g_out,
+    g_gate,
+    g_up,
+    g_down,
+    w_ffn,
+    all_query,
+    all_grad,
+    allowed,
+    ffn_grads,
+    part_two,
+    part_out,
+    recv_two_low,
+    recv_two_side,
+    recv_two_up,
+    recv_out_low,
+    recv_out_side,
+    recv_out_up,
+    ffn_slots,
+    ffn_relay,
+    ffn_side,
+    early_grads,
+    early_across,
+    early_slots,
+    early_relay,
+    late_grads,
+    late_across,
+    late_slots,
+    late_relay,
+    last_grads,
+    last_across,
+    last_slots,
+    last_relay,
+    h_one,
+    grad_attn,
+    grad_heads,
+    stats,
+    mass_rows,
+    delta_rows,
+    grad_qkv,
+    grad_offs,
+    one_parts,
+    recv_one_low,
+    recv_one_up,
+    off_all,
+    gain_swap,
+    gain_peer,
+    near_sem,
+    sems,
+):
+    net = Net(n_seq, sems)
+    s, z, x, y, c = net.s, net.z, net.x, net.y, net.c
+    rows, width = tokens.shape
+    half, quarter = rows // 2, rows // 4
+    block = g_query.shape[0]
+    hc = mixed.shape[1]
+    hidden = w_ffn.shape[1] // 3
+    span = n_seq * half
+    tile = 256
+    kept = c * half + y * quarter
+    own = rows_of(kept, quarter)
+    parts = [slice(p * half, (p + 1) * half) for p in range(2)]
+
+    fetch = pltpu.make_async_copy(w_ffn_far, w_ffn, near_sem)
+    fetch.start()
+    query_net = Spread(net, lambda j: all_query.at[:, j])
+    grad_net = Spread(net, lambda j: all_grad.at[:, j])
+    ffn_net = LineReduce(
+        net, lambda t: w_ffn.at[rows_of(t * 2 * block, 2 * block), :], ffn_slots, ffn_relay
+    )
+    early_net = SeqReduce(net, early_grads, early_across, early_slots, early_relay)
+    late_net = SeqReduce(net, late_grads, late_across, late_slots, late_relay)
+    last_net = SeqReduce(net, last_grads, last_across, last_slots, last_relay)
+    for part in range(2):
+        all_query[part, s] = queries[parts[part], :]
+    net.barrier()
+    query_net.start()
+    fetch.wait()
+
+    for at in range(2 * rows // tile):
+        r = slice(at * tile, (at + 1) * tile)
+        for col in range(hidden // tile):
+            cc = [slice(k * hidden + col * tile, k * hidden + (col + 1) * tile) for k in range(3)]
+            gate = dot_nn(normed_two[r, :], w_ffn[:, cc[0]])
+            up = dot_nn(normed_two[r, :], w_ffn[:, cc[1]])
+            grad_act = dot_nn(out_grads[r, :], w_ffn[:, cc[2]])
+            sigmoid = 1.0 / (1.0 + jnp.exp(-gate))
+            silu = gate * sigmoid
+            ffn_grads[r, cc[0]] = (grad_act * up * sigmoid * (1.0 + gate * (1.0 - sigmoid))).astype(
+                BF16
+            )
+            ffn_grads[r, cc[1]] = (grad_act * silu).astype(BF16)
+            ffn_grads[r, cc[2]] = (silu * up).astype(BF16)
+    for at in range(width // tile):
+        cols = slice(at * tile, (at + 1) * tile)
+        part_two[:, cols] = dot_nt(
+            ffn_grads[:, : 2 * hidden], w_ffn[cols, : 2 * hidden]
+        ).astype(BF16)
+    two = RowReduce(net, part_two, recv_two_low, recv_two_side, recv_two_up)
+    two.start()
+    for at in range(width // tile):
+        cols = slice(at * tile, (at + 1) * tile)
+        part_out[:, cols] = dot_nt(ffn_grads[:, 2 * hidden :], w_ffn[cols, 2 * hidden :]).astype(
+            BF16
+        )
+    two.second()
+    out = RowReduce(net, part_out, recv_out_low, recv_out_side, recv_out_up)
+    out.start()
+
+    for at in range(width // tile):
+        cols = slice(at * tile, (at + 1) * tile)
+        w_ffn[cols, : 2 * hidden] = dot_tn(
+            normed_two[:, cols], ffn_grads[:, : 2 * hidden]
+        ).astype(BF16)
+        w_ffn[cols, 2 * hidden :] = dot_tn(out_grads[:, cols], ffn_grads[:, 2 * hidden :]).astype(
+            BF16
+        )
+    two.third()
+    out.second()
+    ffn_net.start()
+
+    values_in = tokens[...].astype(F32)
+    inverse = lax.rsqrt(jnp.mean(values_in * values_in, axis=-1, keepdims=True) + EPSILON)
+    h_one[...] = (values_in * inverse * gain_one[...]).astype(BF16)
+
+    def positions(shape, axis):
+        at = lax.broadcasted_iota(jnp.int32, shape, axis)
+        owner = (at % span) // half
+        group = jnp.where(at // span == 0, owner, 2 * n_seq - 1 - owner)
+        return group * half + at % half
+
+    every_pos = positions((1, 2 * span), 1)
+    own_pos = [
+        (s if part == 0 else 2 * n_seq - 1 - s) * half
+        + lax.broadcasted_iota(jnp.int32, (half, 1), 0)
+        for part in range(2)
+    ]
+    for part in range(2):
+        start = doc_starts(own_pos[part], doc_ref, docs)
+        seen = (every_pos <= own_pos[part]) & (every_pos >= start)
+        allowed[parts[part], :] = jnp.where(seen, 0.0, MASKED)
+
+    grad_two = two.result()
+    back_two, gain_two_part = norm_grad(grad_two, middle[...], gain_two[...])
+    grad_middle = out_grads[rows_of(x * rows + kept, quarter), :].astype(F32) + back_two
+    grad_attn[own, :] = grad_middle.astype(BF16)
+    attn_second = gather_quarters(net, grad_attn)
+    query_net.arrive()
+    attn_second()()
+
+    grad_heads[...] = dot_nn(grad_attn[...], w_out[...]).astype(BF16)
+    for part in range(2):
+        all_grad[part, s] = grad_heads[parts[part], :]
+    grad_net.start()
+    lane = lax.broadcasted_iota(jnp.int32, (rows, LANES), 1)
+    delta = jnp.zeros((rows, LANES), F32)
+    for pair in range(heads // 2):
+        cols = slice(pair * LANES, (pair + 1) * LANES)
+        product = grad_heads[:, cols].astype(F32) * exact[:, cols]
+        for side in range(2):
+            inner = jnp.sum(
+                jnp.where(lane // HEAD_DIM == side, product, 0.0), axis=1, keepdims=True
+            )
+            delta = jnp.where(lane == pair * 2 + side, inner, delta)
+    grad_offs[...] = delta
+    stats[s, :8, :] = mass[...].T[:8, :]
+    stats[s, 8:, :] = delta.T[:8, :]
+    wait_stats = spread_small(net, lambda j: stats.at[j])
+    out.third()
+
+    lane = lax.broadcasted_iota(jnp.int32, (half, LANES), 1)
+    first = (lane // HEAD_DIM) == 0
+    score_sums = [jnp.zeros((half, LANES), F32), jnp.zeros((half, LANES), F32)]
+    for pair in range(heads // 2):
+        cols = slice(pair * LANES, (pair + 1) * LANES)
+        vcols = slice(hc + pair * LANES, hc + (pair + 1) * LANES)
+        for part in range(2):
+            r = parts[part]
+            many = span * (part + 1)
+            key_pair = keyval[: part + 1, :, :, cols].reshape(many, LANES)
+            value_pair = keyval[: part + 1, :, :, vcols].reshape(many, LANES)
+            query_pair, grad_pair = queries[r, cols], grad_heads[r, cols]
+            made = []
+            for side in range(2):
+                head = pair * 2 + side
+                keep = (lane // HEAD_DIM) == side
+                scores = (
+                    dot_nt(jnp.where(keep, query_pair, jnp.zeros_like(query_pair)), key_pair)
+                    - offsets[head : head + 1, :many]
+                    + allowed[r, :many]
+                )
+                probs = jnp.exp(scores - mass[r, head : head + 1])
+                grad_probs = dot_nt(
+                    jnp.where(keep, grad_pair, jnp.zeros_like(grad_pair)), value_pair
+                )
+                grad_scores = (probs * (grad_probs - grad_offs[r, head : head + 1])).astype(BF16)
+                made.append(dot_nn(grad_scores, key_pair))
+                sums = jnp.sum(grad_scores.astype(F32), axis=1, keepdims=True)
+                score_sums[part] = jnp.where(lane == head, sums, score_sums[part])
+            grad_qkv[r, cols] = (jnp.where(first, made[0], made[1]) * HEAD_DIM ** (-0.5)).astype(
+                BF16
+            )
+        if pair == 0:
+            grad_net.arrive()
+            query_net.finish()
+    for part in range(2):
+        grad_offs[parts[part], :] = score_sums[part]
+    ffn_net.hand_on()
+
+    for at in range(width // tile):
+        cols = slice(at * tile, (at + 1) * tile)
+        early_grads[cols, :hc] = dot_tn(h_one[:, cols], grad_qkv[:, :hc]).astype(BF16)
+        early_grads[cols, hc:] = dot_tn(grad_attn[:, cols], mixed[...]).astype(BF16)
+    grad_net.finish()
+    early_net.start()
+    ffn_sum_out = out.result()
+    layer_out[own, :] = (middle[...] + ffn_sum_out).astype(BF16)
+    layer_second = gather_quarters(net, layer_out)
+
+    starts = doc_starts(every_pos, doc_ref, docs)
+    for part in range(2):
+        seen = (own_pos[part] <= every_pos) & (own_pos[part] >= starts)
+        allowed[parts[part], :] = jnp.where(seen, 0.0, MASKED)
+    wait_stats()
+    for j in range(n_seq):
+        for part in range(2):
+            at = (part * n_seq + j) * half
+            mass_rows[:, at : at + half] = stats[j, :8, parts[part]]
+            delta_rows[:, at : at + half] = stats[j, 8:, parts[part]]
+
+    score_sums = [jnp.zeros((half, LANES), F32), jnp.zeros((half, LANES), F32)]
+    own_offs = [
+        to_columns(offsets[:, pl.ds(pl.multiple_of((p * n_seq + s) * half, LANES), half)])
+        for p in range(2)
+    ]
+    for pair in range(heads // 2):
+        cols = slice(pair * LANES, (pair + 1) * LANES)
+        vcols = slice(hc + pair * LANES, hc + (pair + 1) * LANES)
+        for part in range(2):
+            r = parts[part]
+            many = span * (2 - part)
+            lanes = slice(2 * span - many, 2 * span)
+            query_all = all_query[part:, :, :, cols].reshape(many, LANES)
+            grad_all = all_grad[part:, :, :, cols].reshape(many, LANES)
+            key_pair, value_pair = keyval[part, s, :, cols], keyval[part, s, :, vcols]
+            keys_made, values_made = [], []
+            for side in range(2):
+                head = pair * 2 + side
+                keep = (lane // HEAD_DIM) == side
+                scores = (
+                    dot_nt(jnp.where(keep, key_pair, jnp.zeros_like(key_pair)), query_all)
+                    - own_offs[part][:, head : head + 1]
+                    + allowed[r, lanes]
+                )
+                probs = jnp.exp(scores - mass_rows[head : head + 1, lanes])
+                grad_probs = dot_nt(
+                    jnp.where(keep, value_pair, jnp.zeros_like(value_pair)), grad_all
+                )
+                grad_scores = (probs * (grad_probs - delta_rows[head : head + 1, lanes])).astype(
+                    BF16
+                )
+                keys_made.append(dot_nn(grad_scores, query_all))
+                values_made.append(dot_nn(probs.astype(BF16), grad_all))
+                sums = jnp.sum(grad_scores.astype(F32), axis=1, keepdims=True)
+                score_sums[part] = jnp.where(lane == head, sums, score_sums[part])
+            grad_qkv[r, hc + pair * LANES : hc + (pair + 1) * LANES] = jnp.where(
+                first, keys_made[0], keys_made[1]
+            ).astype(BF16)
+            grad_qkv[r, 2 * hc + pair * LANES : 2 * hc + (pair + 1) * LANES] = jnp.where(
+                first, values_made[0], values_made[1]
+            ).astype(BF16)
+        if pair == 0:
+            early_net.turn()
+            layer_wait = layer_second()
+    for part in range(2):
+        grad_offs[parts[part], :] = grad_offs[parts[part], :] - score_sums[part]
+    for at in range(width // tile):
+        cols = slice(at * tile, (at + 1) * tile)
+        late_grads[cols, :] = dot_tn(h_one[:, cols], grad_qkv[:, hc : 3 * hc]).astype(BF16)
+    late_net.start()
+
+    off_all[s] = grad_offs[...].T[:8, :]
+    wait_offs = spread_small(net, lambda j: off_all.at[j])
+    early_net.along.hand_on()
+    wait_offs()
+    after = (
+        lax.broadcasted_iota(jnp.int32, (half, half), 0)
+        >= lax.broadcasted_iota(jnp.int32, (half, half), 1)
+    ).astype(F32)
+    pieces = []
+    for group in range(2 * n_seq):
+        owner = group if group < n_seq else 2 * n_seq - 1 - group
+        pieces.append(off_all[owner, :, parts[group // n_seq]])
+    sums = jnp.dot(
+        jnp.concatenate(pieces, axis=0), after, precision=HIGHEST, preferred_element_type=F32
+    )
+    later = jnp.zeros((8, 1), F32)
+    own_sums = [jnp.zeros((8, half), F32), jnp.zeros((8, half), F32)]
+    for group in range(2 * n_seq - 1, -1, -1):
+        part = group // n_seq
+        wanted = group == (s if part == 0 else 2 * n_seq - 1 - s)
+        here = sums[group * 8 : (group + 1) * 8, :] + later
+        own_sums[part] = jnp.where(wanted, here, own_sums[part])
+        later = later + jnp.sum(pieces[group], axis=1, keepdims=True)
+    grad_logit = jnp.concatenate(own_sums, axis=1) / (1.0 + jnp.exp(logit_t[...]))
+    grad_qkv[:, 3 * hc :] = to_columns(grad_logit).astype(BF16)
+
+    for at in range(width // tile):
+        cols = slice(at * tile, (at + 1) * tile)
+        last_grads[cols, :] = dot_tn(h_one[:, cols], grad_qkv[:, 3 * hc :]).astype(BF16)
+    last_net.start()
+    for at in range(width // tile):
+        cols = slice(at * tile, (at + 1) * tile)
+        for part in range(2):
+            one_parts[part, :, cols] = dot_nt(grad_qkv[parts[part], :], w_attn[cols, :]).astype(
+                BF16
+            )
+    low = net.send(one_parts.at[1 - c], recv_one_low, net.lower())
+    late_net.turn()
+    low.wait_recv()
+    one_parts[c] = (one_parts[c].astype(F32) + recv_one_low[...].astype(F32)).astype(BF16)
+    up = net.send(
+        one_parts.at[c, rows_of((1 - y) * quarter, quarter), :], recv_one_up, net.upper()
+    )
+    last_net.turn()
+    up.wait_recv()
+    grad_one = one_parts[c, rows_of(y * quarter, quarter), :].astype(F32) + recv_one_up[
+        ...
+    ].astype(F32)
+    back_one, gain_one_part = norm_grad(grad_one, tokens[own, :].astype(F32), gain_one[...])
+    tokens_grad[own, :] = (grad_middle + back_one).astype(BF16)
+    grad_second = gather_quarters(net, tokens_grad)
+    line_row = lax.broadcasted_iota(jnp.int32, (8, width), 0)
+    gain_peer[s, :, :width] = jnp.where(
+        line_row == 0, gain_one_part, jnp.where(line_row == 1, gain_two_part, 0.0)
+    )
+    gain_peer[s, :, width:] = jnp.broadcast_to(
+        jnp.sum(grad_logit, axis=1, keepdims=True), (8, LANES)
+    )
+    wait_gains = spread_small(net, lambda j: gain_peer.at[j])
+    late_net.along.hand_on()
+    last_net.along.hand_on()
+    grad_wait = grad_second()
+
+    def write_early(total):
+        got = total(slice(0, block))
+        g_query[...] = got[:, :hc]
+        g_out[...] = got[:, hc:]
+
+    early_net.along.finish(write_early)
+
+    outs = (g_gate, g_up, g_down)
+    side_rows = rows_of((1 - x) * block, block)
+
+    def write_ffn(total):
+        got = total(rows_of(x * block, block))
+        for k, ref in enumerate(outs):
+            ref[:, pl.ds(pl.multiple_of(x * hidden, LANES), hidden)] = got[
+                :, k * hidden : (k + 1) * hidden
+            ]
+        ffn_side[0] = total(side_rows).astype(BF16)
+
+    ffn_net.finish(write_ffn)
+    across = net.send(ffn_side.at[0], ffn_side.at[1], net.side())
+
+    wait_gains()
+    total = gain_peer[0]
+    for j in range(1, n_seq):
+        total = total + gain_peer[j]
+    bias_grad[...] = total[:, width:]
+    for step, peer in enumerate((net.lower(), net.upper())):
+        gain_swap[2 * step] = total[:, :width]
+        swap = net.send(gain_swap.at[2 * step], gain_swap.at[2 * step + 1], peer)
+        swap.wait_recv()
+        total = gain_swap[2 * step] + gain_swap[2 * step + 1]
+    gains[...] = total
+
+    across.wait_recv()
+    for k, ref in enumerate(outs):
+        ref[:, pl.ds(pl.multiple_of((1 - x) * hidden, LANES), hidden)] = ffn_side[
+            1, :, k * hidden : (k + 1) * hidden
+        ].astype(F32)
+
+    def write_late(total):
+        got = total(slice(0, block))
+        g_key[...] = got[:, :hc]
+        g_value[...] = got[:, hc:]
+
+    late_net.along.finish(write_late)
+
+    def write_last(total):
+        g_forget[...] = total(slice(0, block))
+
+    last_net.along.finish(write_last)
+    layer_wait()
+    grad_wait()
+    for part in (query_net, grad_net, ffn_net, early_net, late_net, last_net, net):
+        part.drain()
+
+
+def backward_shapes(n_seq, rows, width, hc, hidden, block):
+    half, quarter = rows // 2, rows // 4
+    line = n_seq // 2
+    places = min(4, line - 1)
+    relays = 1 if line <= 4 else 2 * (line - 3)
+
+    def seq_reduce(columns):
+        return [
+            ((width, columns), BF16),
+            ((line, block, columns), BF16),
+            ((places, block, columns), BF16),
+            ((relays, block, columns), BF16),
+        ]
+
+    ffn = 3 * hidden
+    return [
+        ((width, ffn), BF16),
+        ((2, n_seq, half, hc), BF16),
+        ((2, n_seq, half, hc), BF16),
+        ((rows, 2 * n_seq * half), F32),
+        ((2 * rows, ffn), BF16),
+        ((2 * rows, width), BF16),
+        ((2 * rows, width), BF16),
+        ((2, half, width), BF16),
+        ((half, width), BF16),
+        ((quarter, width), BF16),
+        ((2, half, width), BF16),
+        ((half, width), BF16),
+        ((quarter, width), BF16),
+        ((places, 2 * block, ffn), BF16),
+        ((relays, 2 * block, ffn), BF16),
+        ((2, block, ffn), BF16),
+        *seq_reduce(2 * hc),
+        *seq_reduce(2 * hc),
+        *seq_reduce(LANES),
+        ((rows, width), BF16),
+        ((rows, width), BF16),
+        ((rows, hc), BF16),
+        ((n_seq, 16, rows), F32),
+        ((8, 2 * n_seq * half), F32),
+        ((8, 2 * n_seq * half), F32),
+        ((rows, 3 * hc + LANES), BF16),
+        ((rows, LANES), F32),
+        ((2, half, width), BF16),
+        ((half, width), BF16),
+        ((quarter, width), BF16),
+        ((n_seq, 8, rows), F32),
+        ((4, 8, width), F32),
+        ((n_seq, 8, width + LANES), F32),
+    ]
+
+
+def run_backward(n_seq, heads, hidden, block, tokens, attn_gain, ffn_gain, docs, made):
+    (
+        queries,
+        keyval,
+        offsets,
+        mass,
+        logit_t,
+        mixed,
+        exact,
+        middle,
+        normed_two,
+        out_grads,
+        w_attn,
+        w_out,
+        w_ffn,
+    ) = made
+    rows, width = tokens.shape
+    hc = mixed.shape[1]
+    vmem = pl.BlockSpec(memory_space=pltpu.VMEM)
+    outs = (
+        ((rows, width), BF16),
+        ((rows, width), BF16),
+        ((8, width), F32),
+        ((8, LANES), F32),
+        ((block, hc), F32),
+        ((block, hc), F32),
+        ((block, hc), F32),
+        ((block, LANES), F32),
+        ((block, hc), F32),
+        ((block, 2 * hidden), F32),
+        ((block, 2 * hidden), F32),
+        ((block, 2 * hidden), F32),
+    )
+    scratch = backward_shapes(n_seq, rows, width, hc, hidden, block)
+    return pl.pallas_call(
+        functools.partial(backward_kernel, n_seq, docs.shape[0], heads),
+        out_shape=[jax.ShapeDtypeStruct(*o) for o in outs],
+        in_specs=[vmem] * 15
+        + [
+            pl.BlockSpec(memory_space=pl.ANY),
+            pl.BlockSpec(memory_space=pltpu.SMEM),
+        ],
+        out_specs=[vmem] * len(outs),
+        scratch_shapes=[pltpu.VMEM(*o) for o in scratch]
+        + [pltpu.SemaphoreType.DMA, pltpu.SemaphoreType.DMA((320,))],
+        compiler_params=pltpu.CompilerParams(
+            collective_id=1, has_side_effects=True, vmem_limit_bytes=62 << 20
+        ),
+    )(
+        tokens,
+        attn_gain.reshape(1, width),
+        ffn_gain.reshape(1, width),
+        queries,
+        keyval,
+        offsets,
+        mass,
+        logit_t,
+        mixed,
+        exact,
+        middle,
+        normed_two,
+        out_grads,
+        w_attn,
+        w_out,
+        w_ffn,
+        docs,
+    )
+
+
+def kernel_body(
+    tokens,
+    attn_gain,
+    query_weight,
+    key_weight,
+    value_weight,
+    forget_weight,
+    forget_bias,
+    out_weight,
+    ffn_gain,
+    gate_weight,
+    up_weight,
+    down_weight,
+    doc_lengths,
+    out_grad,
+):
+    n_seq = lax.axis_size("seq")
+    heads = forget_bias.shape[0]
+    block = gate_weight.shape[0]
+    hidden = gate_weight.shape[1] // 2
+    made = run_forward(
+        n_seq,
+        heads,
+        tokens,
+        attn_gain,
+        query_weight,
+        key_weight,
+        value_weight,
+        forget_weight,
+        forget_bias,
+        out_weight.T,
+        ffn_gain,
+        gate_weight,
+        up_weight,
+        down_weight.T,
+        doc_lengths,
+        out_grad,
+    )
+    (
+        layer_out,
+        tokens_grad,
+        gains,
+        bias_grad,
+        g_query,
+        g_key,
+        g_value,
+        g_forget,
+        g_out,
+        g_gate,
+        g_up,
+        g_down,
+    ) = run_backward(
+        n_seq, heads, hidden, block, tokens, attn_gain, ffn_gain, doc_lengths, made
+    )
+    return (
+        layer_out,
+        tokens_grad,
+        gains[0],
+        g_query,
+        g_key,
+        g_value,
+        g_forget[:, :heads],
+        bias_grad[:heads, 0],
+        g_out.T,
+        gains[1],
+        g_gate,
+        g_up,
+        g_down.T,
+    )
+
+
+def kernels_fit(tokens, forget_bias, out_weight, gate_weight):
+    n_seq = lax.axis_size("seq")
+    rows, width = tokens.shape
+    hc = out_weight.shape[0]
+    block, hidden = gate_weight.shape[0], gate_weight.shape[1] // 2
+    shapes = backward_shapes(n_seq, rows, width, hc, hidden, block)
+    size = sum(math.prod(shape) * jnp.dtype(kind).itemsize for shape, kind in shapes)
+    return (
+        size <= (48 << 20)
+        and lax.axis_size("head") == 4
+        and n_seq % 2 == 0
+        and n_seq >= 8
+        and rows == 2 * LANES
+        and width % 256 == 0
+        and hidden % 256 == 0
+        and block % 16 == 0
+        and forget_bias.shape[0] in (2, 4, 6)
+    )
 
 
 def unchanged(carried):
@@ -108,7 +1453,7 @@
     )
 
 
-def body(
+def plain_body(
     tokens,
     attn_gain,
     query_weight,
@@ -419,6 +1764,11 @@
         up_weight_grad,
         down_weight_grad,
     )
+
+
+def body(*args):
+    fits = kernels_fit(args[0], args[6], args[7], args[9])
+    return (kernel_body if fits else plain_body)(*args)
 
 
 def solution(mesh):

time: 918 us -> 488 us (0.53)
  waiting for transfers between devices: 533 us -> 0 us
  Pallas kernels: 0 us -> 464 us
  blocking collectives: 134 us -> 0 us
  matrix products: 108 us -> 0 us
  local copies, waits for them, and re-layouts: 69.3 us -> 19.5 us
  other arithmetic: 43.9 us -> 0 us
  between operations: 20.2 us -> 0.9 us
    pallas_call x0 -> x2, Pallas kernels: none -> 464 us  [the longest x1 246 us: run_backward(): pl.pallas_call(functools.partial(backward_kernel, n_seq, docs.shape[0], h...]
    unnamed x11 -> x0, waiting for transfers between devices: 223 us -> none
    all_gather x4 -> x0, waiting for transfers between devices: 217 us -> none  [the longest x1 114 us: body(): lax.all_gather(jnp.concatenate([out_weight.T, gate_weight, up_weight, dow...]
    dot_general x37 -> x0, matrix products: 108 us -> none  [the longest x2 17.4 us: piece_grads(): jnp.einsum('qhd,khd->hqk', grad_heads, value_heads, preferred_element_typ...]
    all_gather x3 -> x0, blocking collectives: 94.2 us -> none  [the longest x1 32.6 us: body(): lax.all_gather(jnp.concatenate([log_mass.T, row_delta.T], axis=1), 'seq',...]
    psum x3 -> x0, waiting for transfers between devices: 92.7 us -> none  [the longest x1 43 us: body(): grad_two = lax.psum(part_two, 'head')]
    psum x1 -> x0, blocking collectives: 39.4 us -> none  [body(): lax.psum((gain_one, gain_two, jnp.sum(grad_logit, axis=0)), 'seq')]
    unnamed x100 -> x25, local copies, waits for them, and re-layouts: 36.2 us -> 12.2 us
  transfers between devices with their start and end apart: 9 -> 0, of which waited for: 8 -> 0; matrix products, arithmetic and copies ran while one was open for 14% -> 0% of each run, Pallas kernels for 0% -> 0%
where the time goes in v2:
time: 488 us; the launch traced here: 484 us
  Pallas kernels  464 us (95%)
  local copies, waits for them, and re-layouts  19.5 us (4%)
    pallas_call x1, Pallas kernels, run_backward(): pl.pallas_call(functools.partial(backward_kernel, n_seq, docs.shape[0], h...  246 us
    pallas_call x1, Pallas kernels, run_forward(): pl.pallas_call(functools.partial(forward_kernel, n_seq, docs.shape[0], he...  217 us
    unnamed x25, local copies, waits for them, and re-layouts  12.2 us

profile of v2, /device:TPU:0, one launch (start us, length us, event | category | flops | bytes accessed | tf_op | source)
XLA Modules:
  0.0 484.2 jit_solution(6366783655948596824)
XLA Ops:
  0.6 1.2 pad_bitcast_fusion.bias
  1.8 1.3 reshape.37.gain_one
  3.1 1.3 reshape.38.gain_two
  4.4 0.8 copy.29
  5.2 0.6 pad.8.wf
  5.9 217.3 %shard_map.237 = (bf16[256,384]{1,0:T(8,128)(2,1)}, bf16[2,8,128,768]{3,2,1,0:T(8,128)(2,1)}, f32[8,2048]{1,0:T(8,128)}, f32[256,128]{1,0:T(8,128)}, f32[8,256]{...) custom-call(bf16[256,1536]{1,0:T(8,128)(2,1)} %tokens.3, ...), custom_call_target="tpu_custom_call" | custom-call | tf_op jit(solution)/shard_map/pallas_call | solution.py:472
  223.2 246.4 %shard_map.238 = (bf16[256,1536]{1,0:T(8,128)(2,1)}, bf16[256,1536]{1,0:T(8,128)(2,1)}, f32[8,1536]{1,0:T(8,128)}, f32[8,128]{1,0:T(8,128)}, f32[192,384]{1,0:T(...) custom-call(bf16[256,1536]{1,0:T(8,128)(2,1)} %tokens.3, ...), custom_call_target="tpu_custom_call" | custom-call | tf_op jit(solution)/shard_map/pallas_call | solution.py:1233
  469.6 0.0 copy-start.6
  469.6 0.0 copy-start.5
  469.6 0.0 copy-start.4
  469.6 0.0 copy-start.3
  469.7 0.0 copy-start.2
  469.7 1.4 slice_reduce_fusion.2
  471.1 1.6 copy.30
  472.7 1.5 slice_reduce_fusion
  474.2 0.0 copy-start.1
  474.2 2.1 copy.40
  476.3 2.1 copy.41
  478.5 0.0 copy-done.6
  478.5 0.7 copy.42
  479.2 0.0 copy-done.5
  479.2 0.7 copy.43
  479.9 0.0 copy-done.4
  479.9 0.7 copy.44
  480.6 0.0 copy-done.3
  480.6 0.7 copy.45
  481.3 0.0 copy-done.2
  481.3 0.9 copy.46
  482.2 0.0 copy-done.1
  482.2 0.9 copy.47
  483.1 0.0 copy-done
  483.1 0.9 copy.48
  (1 shorter events, 0.0 us)
Async XLA Ops:
  469.6 8.8 %copy-start.6 = (f32[192,384]{1,0:T(8,128)S(1)}, f32[192,384]{1,0:T(8,128)}, u32[]{:S(2)}) copy-start(f32[192,384]{1,0:T(8,128)} %get-tuple-element.107) | copy-start | bytes 884740
  469.6 9.6 %copy-start.5 = (f32[192,384]{1,0:T(8,128)S(1)}, f32[192,384]{1,0:T(8,128)}, u32[]{:S(2)}) copy-start(f32[192,384]{1,0:T(8,128)} %get-tuple-element.108) | copy-start | bytes 884740
  469.6 10.3 %copy-start.4 = (f32[192,384]{1,0:T(8,128)S(1)}, f32[192,384]{1,0:T(8,128)}, u32[]{:S(2)}) copy-start(f32[192,384]{1,0:T(8,128)} %get-tuple-element.109) | copy-start | bytes 884740
  469.6 11.0 %copy-start.3 = (f32[192,384]{1,0:T(8,128)S(1)}, f32[192,384]{1,0:T(8,128)}, u32[]{:S(2)}) copy-start(f32[192,384]{1,0:T(8,128)} %get-tuple-element.59) | copy-start | bytes 884740
  469.7 11.7 %copy-start.2 = (f32[192,1024]{1,0:T(8,128)S(1)}, f32[192,1024]{1,0:T(8,128)}, u32[]{:S(2)}) copy-start(f32[192,1024]{1,0:T(8,128)} %get-tuple-element.114) | copy-start | bytes 2359300
  474.2 8.0 %copy-start.1 = (f32[192,1024]{1,0:T(8,128)S(1)}, f32[192,1024]{1,0:T(8,128)}, u32[]{:S(2)}) copy-start(f32[192,1024]{1,0:T(8,128)} %get-tuple-element.115) | copy-start | bytes 2359300
  476.3 6.8 %copy-start = (f32[192,1024]{1,0:T(8,128)S(1)}, f32[192,1024]{1,0:T(8,128)}, u32[]{:S(2)}) copy-start(f32[192,1024]{1,0:T(8,128)} %get-tuple-element.62) | copy-start | bytes 2359300

commit v3 on v1

--- a/solution.py
+++ b/solution.py
@@ -1,14 +1,1480 @@
 import jax
 import jax.numpy as jnp
 from jax import lax
+from jax.experimental import pallas as pl
+from jax.experimental.pallas import tpu as pltpu
 from jax.sharding import PartitionSpec as P
 
 HEAD_DIM = 64
-
-
 EPSILON = 1e-06
 HIGHEST = lax.Precision.HIGHEST
 MASKED = -1e30
+MESH_ID = pl.DeviceIdType.MESH
+F32 = jnp.float32
+BF16 = jnp.bfloat16
+LANES = 128
+KEY_TILES = ((0, 0), (0, 1), (1, 0))
+VALUE_TILES = ((1, 1), (2, 0), (2, 1))
+OUT_TILES = ((0, 1), (1, 0), (1, 1))
+NEAR_FIRST = (1, 3, 2)
+
+
+def dot_nn(left, right):
+    return jnp.dot(left, right, preferred_element_type=F32)
+
+
+def dot_nt(left, right):
+    return lax.dot_general(left, right, (((1,), (1,)), ((), ())), preferred_element_type=F32)
+
+
+def dot_tn(left, right):
+    return lax.dot_general(left, right, (((0,), (0,)), ((), ())), preferred_element_type=F32)
+
+
+def rows_of(first, count):
+    return pl.ds(pl.multiple_of(first, 16), count)
+
+
+def add_to(ref, other):
+    ref[...] = (ref[...].astype(F32) + other[...].astype(F32)).astype(BF16)
+
+
+class Net:
+    def __init__(self, sems):
+        s = lax.axis_index("seq")
+        h = lax.axis_index("head")
+        self.line = 4
+        self.z, self.x = s // 2, s % 2
+        self.y, self.c = h // 2, h % 2
+        self.sems = sems
+        self.used = 0
+        self.pending = []
+
+    def alloc(self, count):
+        first = self.used
+        self.used += count
+        return first
+
+    def to(self, z=None, x=None, y=None, c=None):
+        z = self.z if z is None else z
+        x = self.x if x is None else x
+        y = self.y if y is None else y
+        c = self.c if c is None else c
+        return (z * 2 + x, y * 2 + c)
+
+    def side(self):
+        return self.to(x=1 - self.x)
+
+    def lower(self):
+        return self.to(c=1 - self.c)
+
+    def upper(self):
+        return self.to(y=1 - self.y)
+
+    def next(self, step):
+        return (self.z + step) % self.line
+
+    def barrier(self):
+        sem = pltpu.get_barrier_semaphore()
+        peers = [self.side(), self.lower(), self.upper(), self.to(x=1 - self.x, c=1 - self.c)]
+        for step in range(1, self.line):
+            peers.append(self.to(z=self.next(step)))
+            peers.append(self.to(z=self.next(step), c=1 - self.c))
+        for peer in peers:
+            pl.semaphore_signal(sem, 1, device_id=peer, device_id_type=MESH_ID)
+        pl.semaphore_wait(sem, len(peers))
+
+    def copy(self, src, dst, send, recv, device):
+        return pltpu.make_async_remote_copy(
+            src_ref=src,
+            dst_ref=dst,
+            send_sem=self.sems.at[send],
+            recv_sem=self.sems.at[recv],
+            device_id=device,
+            device_id_type=MESH_ID,
+        )
+
+    def begin(self, made):
+        made.start()
+        self.pending.append(made.wait_send)
+        return made
+
+    def send(self, src, dst, device):
+        first = self.alloc(2)
+        return self.begin(self.copy(src, dst, first, first + 1, device))
+
+    def got(self, ref, recv):
+        self.copy(ref, ref, recv, recv, self.side()).wait_recv()
+
+    def drain(self):
+        for wait in self.pending:
+            wait()
+        self.pending = []
+
+
+class RowGather:
+    def __init__(self, net, slot, lower=None):
+        self.net = net
+        self.slot = slot
+        self.low = lower
+        self.sent = net.alloc(4)
+        self.came = net.alloc(4)
+        self.up_sent = net.alloc(4)
+        self.up_came = net.alloc(4)
+        self.low_sent = net.alloc(8)
+        self.low_came = net.alloc(8)
+
+    def pass_low(self, y, z):
+        if self.low is not None:
+            net = self.net
+            index = y * 4 + z
+            block = self.slot(y, z)
+            net.begin(
+                net.copy(
+                    block, block, self.low_sent + index, self.low_came + index, net.lower()
+                )
+            )
+
+    def pass_up(self, z):
+        net = self.net
+        block = self.slot(net.y, z)
+        net.begin(net.copy(block, block, self.up_sent + z, self.up_came + z, net.upper()))
+        self.pass_low(net.y, z)
+
+    def start(self):
+        net = self.net
+        mine = self.slot(net.y, net.z)
+        for step in NEAR_FIRST:
+            net.begin(
+                net.copy(
+                    mine, mine, self.sent + step, self.came + net.z, net.to(z=net.next(step))
+                )
+            )
+        self.pass_up(net.z)
+
+    def forward(self):
+        net = self.net
+        for step in NEAR_FIRST:
+            src = net.next(step)
+            net.got(self.slot(net.y, src), self.came + src)
+            self.pass_up(src)
+
+    def finish(self):
+        net = self.net
+        for step in (0,) + NEAR_FIRST:
+            src = net.next(step)
+            net.got(self.slot(1 - net.y, src), self.up_came + src)
+            self.pass_low(1 - net.y, src)
+        if self.low is not None:
+            for y in range(2):
+                for z in range(4):
+                    net.got(self.low(y, z), self.low_came + y * 4 + z)
+
+
+class RowSum:
+    def __init__(self, net, slot, recv_up, recv_line):
+        self.net = net
+        self.slot = slot
+        self.recv_up = recv_up
+        self.recv_line = recv_line
+        self.up_sent = net.alloc(4)
+        self.up_came = net.alloc(4)
+        self.sent = net.alloc(4)
+        self.came = net.alloc(4)
+
+    def start(self):
+        net = self.net
+        for step in (2, 1, 3, 0):
+            z = net.next(step)
+            net.begin(
+                net.copy(
+                    self.slot(1 - net.y, z),
+                    self.recv_up.at[z],
+                    self.up_sent + z,
+                    self.up_came + z,
+                    net.upper(),
+                )
+            )
+
+    def middle(self):
+        net = self.net
+        for step in (2, 1, 3, 0):
+            z = net.next(step)
+            net.got(self.recv_up.at[z], self.up_came + z)
+            mine = self.slot(net.y, z)
+            add_to(mine, self.recv_up.at[z])
+            if step:
+                net.begin(
+                    net.copy(
+                        mine,
+                        self.recv_line.at[net.z],
+                        self.sent + step,
+                        self.came + net.z,
+                        net.to(z=z),
+                    )
+                )
+
+    def result(self):
+        net = self.net
+        total = self.slot(net.y, net.z)[...].astype(F32)
+        for step in NEAR_FIRST:
+            src = net.next(step)
+            net.got(self.recv_line.at[src], self.came + src)
+            total = total + self.recv_line[src].astype(F32)
+        return total
+
+
+class CrossGather:
+    def __init__(self, net, slot):
+        self.net = net
+        self.slot = slot
+
+    def start(self):
+        net = self.net
+        mine = self.slot(net.x, net.c)
+        self.across = net.send(mine, mine, net.side())
+        self.low = net.send(mine, mine, net.lower())
+
+    def forward(self):
+        net = self.net
+        self.across.wait_recv()
+        other = self.slot(1 - net.x, net.c)
+        self.both = net.send(other, other, net.lower())
+
+    def finish(self):
+        self.low.wait_recv()
+        self.both.wait_recv()
+
+
+class WeightSpread:
+    def __init__(self, net, stage, full):
+        self.net = net
+        self.stage = stage
+        self.full = full
+        self.block = stage.shape[1]
+        self.sent = net.alloc(2)
+        self.came = net.alloc(4)
+        self.side_sent = net.alloc(4)
+        self.side_came = net.alloc(4)
+        self.low_sent = net.alloc(8)
+        self.low_came = net.alloc(8)
+        self.first = (net.z // 2) == net.c
+
+    def slot(self, z, x):
+        return self.full.at[rows_of((z * 2 + x) * self.block, self.block), :]
+
+    def away(self, u):
+        net = self.net
+        return net.copy(
+            self.stage.at[u],
+            self.slot(net.z, net.x),
+            self.sent + u,
+            self.came + net.z,
+            net.to(z=2 * net.c + u),
+        )
+
+    def across(self, z):
+        net = self.net
+        block = self.slot(z, net.x)
+        return net.copy(block, block, self.side_sent + z, self.side_came + z, net.side())
+
+    def low(self, z, x):
+        block = self.slot(z, x)
+        index = z * 2 + x
+        return self.net.copy(
+            block, block, self.low_sent + index, self.low_came + index, self.net.lower()
+        )
+
+    def start(self):
+        net = self.net
+        for u in range(2):
+            pl.when(2 * net.c + u != net.z)(lambda u=u: self.away(u).start())
+
+        @pl.when(self.first)
+        def _():
+            self.slot(net.z, net.x)[...] = self.stage[net.z % 2]
+            self.across(net.z).start()
+            self.low(net.z, net.x).start()
+
+    def forward(self):
+        net = self.net
+
+        @pl.when(self.first)
+        def _():
+            for step in NEAR_FIRST:
+                src = net.next(step)
+                net.got(self.slot(src, net.x), self.came + src)
+                self.across(src).start()
+                self.low(src, net.x).start()
+
+    def finish(self):
+        net = self.net
+
+        @pl.when(self.first)
+        def _():
+            for step in (0,) + NEAR_FIRST:
+                src = net.next(step)
+                net.got(self.slot(src, 1 - net.x), self.side_came + src)
+                self.low(src, 1 - net.x).start()
+
+        @pl.when(jnp.logical_not(self.first))
+        def _():
+            for z in range(4):
+                for x in range(2):
+                    net.got(self.slot(z, x), self.low_came + z * 2 + x)
+
+    def drain(self):
+        net = self.net
+        for u in range(2):
+            pl.when(2 * net.c + u != net.z)(lambda u=u: self.away(u).wait_send())
+
+        @pl.when(self.first)
+        def _():
+            for z in range(4):
+                self.across(z).wait_send()
+                for x in range(2):
+                    self.low(z, x).wait_send()
+
+
+class HiddenSpread:
+    def __init__(self, net, stage, full):
+        self.net = net
+        self.stage = stage
+        self.full = full
+        self.block = stage.shape[1]
+        self.sent = net.alloc(4)
+        self.came = net.alloc(4)
+        self.side_sent = net.alloc(4)
+        self.side_came = net.alloc(4)
+
+    def slot(self, z, x):
+        return self.full.at[rows_of((z * 2 + x) * self.block, self.block), :]
+
+    def across(self, z):
+        net = self.net
+        block = self.slot(z, net.x)
+        net.begin(net.copy(block, block, self.side_sent + z, self.side_came + z, net.side()))
+
+    def start(self):
+        net = self.net
+        self.slot(net.z, net.x)[...] = self.stage[net.z]
+        for step in NEAR_FIRST:
+            to = net.next(step)
+            net.begin(
+                net.copy(
+                    self.stage.at[to],
+                    self.slot(net.z, net.x),
+                    self.sent + step,
+                    self.came + net.z,
+                    net.to(z=to),
+                )
+            )
+        self.across(net.z)
+
+    def forward(self):
+        net = self.net
+        for step in NEAR_FIRST:
+            src = net.next(step)
+            net.got(self.slot(src, net.x), self.came + src)
+            self.across(src)
+
+    def finish(self):
+        net = self.net
+        for z in range(4):
+            net.got(self.slot(z, 1 - net.x), self.side_came + z)
+
+
+class WeightSum:
+    def __init__(self, net, grads, recv_low, recv_side, final):
+        self.net = net
+        self.grads = grads
+        self.recv_low = recv_low
+        self.recv_side = recv_side
+        self.final = final
+        self.block = final.shape[1]
+        self.side_sent = net.alloc(2)
+        self.side_came = net.alloc(2)
+        self.sent = net.alloc(2)
+        self.came = net.alloc(2)
+
+    def rows(self, z, x):
+        return self.grads.at[rows_of((z * 2 + x) * self.block, self.block), :]
+
+    def start(self):
+        net = self.net
+        half = 4 * self.block
+        self.low = net.send(
+            self.grads.at[rows_of((1 - net.c) * half, half), :], self.recv_low, net.lower()
+        )
+
+    def second(self):
+        net = self.net
+        self.low.wait_recv()
+        for x in (1 - net.x, net.x):
+            for i in range(2):
+                z = 2 * net.c + i
+                add_to(
+                    self.rows(z, x), self.recv_low.at[rows_of((i * 2 + x) * self.block, self.block)]
+                )
+        for i in range(2):
+            net.begin(
+                net.copy(
+                    self.rows(2 * net.c + i, 1 - net.x),
+                    self.recv_side.at[i],
+                    self.side_sent + i,
+                    self.side_came + i,
+                    net.side(),
+                )
+            )
+
+    def owner(self, i):
+        net = self.net
+        z = 2 * net.c + i
+        made = net.copy(
+            self.rows(z, net.x),
+            self.final.at[net.z % 2],
+            self.sent + i,
+            self.came + net.z % 2,
+            net.to(z=z, c=net.z // 2),
+        )
+        return (z == net.z) & (net.z // 2 == net.c), made
+
+    def third(self):
+        net = self.net
+        for i in range(2):
+            net.got(self.recv_side.at[i], self.side_came + i)
+            mine = self.rows(2 * net.c + i, net.x)
+            add_to(mine, self.recv_side.at[i])
+            local, made = self.owner(i)
+
+            @pl.when(local)
+            def _():
+                self.final[net.z % 2] = mine[...]
+
+            pl.when(jnp.logical_not(local))(made.start)
+
+    def finish(self):
+        net = self.net
+        for u in range(2):
+            pl.when(2 * net.c + u != net.z)(
+                lambda u=u: net.got(self.final.at[u], self.came + u)
+            )
+
+    def drain(self):
+        for i in range(2):
+            local, made = self.owner(i)
+            pl.when(jnp.logical_not(local))(made.wait_send)
+
+
+class HiddenSum:
+    def __init__(self, net, grads, recv_side, final):
+        self.net = net
+        self.grads = grads
+        self.recv_side = recv_side
+        self.final = final
+        self.block = final.shape[1]
+        self.side_sent = net.alloc(4)
+        self.side_came = net.alloc(4)
+        self.sent = net.alloc(4)
+        self.came = net.alloc(4)
+
+    def rows(self, z, x):
+        return self.grads.at[rows_of((z * 2 + x) * self.block, self.block), :]
+
+    def start(self):
+        net = self.net
+        for step in (2, 1, 3, 0):
+            z = net.next(step)
+            net.begin(
+                net.copy(
+                    self.rows(z, 1 - net.x),
+                    self.recv_side.at[z],
+                    self.side_sent + z,
+                    self.side_came + z,
+                    net.side(),
+                )
+            )
+
+    def second(self):
+        net = self.net
+        for step in (2, 1, 3, 0):
+            z = net.next(step)
+            net.got(self.recv_side.at[z], self.side_came + z)
+            mine = self.rows(z, net.x)
+            add_to(mine, self.recv_side.at[z])
+            if step:
+                net.begin(
+                    net.copy(
+                        mine,
+                        self.final.at[net.z],
+                        self.sent + step,
+                        self.came + net.z,
+                        net.to(z=z),
+                    )
+                )
+            else:
+                self.final[net.z] = mine[...]
+
+    def finish(self):
+        net = self.net
+        for step in NEAR_FIRST:
+            src = net.next(step)
+            net.got(self.final.at[src], self.came + src)
+
+
+class Places:
+    def __init__(self, net, chunk):
+        self.net = net
+        self.chunk = chunk
+        self.part = 4 * chunk
+        self.all = 32 * chunk
+
+    def position(self, at):
+        chunk = self.chunk
+        late = at // (16 * chunk)
+        x = (at // (8 * chunk)) % 2
+        c = (at // (4 * chunk)) % 2
+        z = (at // chunk) % 4
+        owner = 2 * z + x
+        group = jnp.where(late == 0, owner, 15 - owner)
+        return group * (2 * chunk) + c * chunk + at % chunk
+
+    def own(self, late):
+        return (late * 4 + self.net.x * 2 + self.net.c) * self.part
+
+    def every(self, shape, axis):
+        return self.position(lax.broadcasted_iota(jnp.int32, shape, axis))
+
+
+def doc_starts(positions, doc_ref):
+    start = jnp.zeros(positions.shape, jnp.int32)
+    end = jnp.int32(0)
+    for k in range(doc_ref.shape[0] - 1):
+        end = end + doc_ref[k]
+        start = jnp.where(positions >= end, end, start)
+    return start
+
+
+def running_sums(places, rows_in, spread, gather, backward):
+    tiles = places.all // LANES
+    chunk = places.chunk
+    row = lax.broadcasted_iota(jnp.int32, (LANES, LANES), 0)
+    col = lax.broadcasted_iota(jnp.int32, (LANES, LANES), 1)
+    reach = row >= col if backward else row <= col
+    within = ((row // chunk == col // chunk) & reach).astype(F32)
+    stacked = jnp.concatenate(
+        [rows_in[:, k * LANES : (k + 1) * LANES] for k in range(tiles)], axis=0
+    )
+    inside = jnp.dot(stacked, within, precision=HIGHEST, preferred_element_type=F32)
+    outside = jnp.dot(rows_in, spread[...], precision=HIGHEST, preferred_element_type=F32)
+    outside = outside[:, : gather.shape[0]]
+    outside = jnp.dot(outside, gather[...], precision=HIGHEST, preferred_element_type=F32)
+    return outside + jnp.concatenate(
+        [inside[k * 8 : (k + 1) * 8, :] for k in range(tiles)], axis=1
+    )
+
+
+def order_tables(places, spread, gather, backward):
+    order = places.every((places.all, LANES), 0) // places.chunk
+    slot = lax.broadcasted_iota(jnp.int32, (places.all, LANES), 1)
+    beyond = order > slot if backward else order < slot
+    spread[...] = beyond.astype(F32)
+    order = places.every(gather.shape, 1) // places.chunk
+    slot = lax.broadcasted_iota(jnp.int32, gather.shape, 0)
+    gather[...] = (order == slot).astype(F32)
+
+
+def tile_of(ref, rows, tile):
+    return ref[rows, tile * LANES : (tile + 1) * LANES]
+
+
+def only(values_in, lane, side):
+    return jnp.where(lane // HEAD_DIM == side, values_in, jnp.zeros_like(values_in))
+
+
+def norm_grad(grad_in, values_in, gain):
+    inverse = lax.rsqrt(jnp.mean(values_in * values_in, axis=-1, keepdims=True) + EPSILON)
+    normed = values_in * inverse
+    scaled = grad_in * gain
+    inner = jnp.mean(scaled * normed, axis=-1, keepdims=True)
+    return inverse * (scaled - normed * inner), jnp.sum(grad_in * normed, axis=0, keepdims=True)
+
+
+def norm(values_in, gain):
+    inverse = lax.rsqrt(jnp.mean(values_in * values_in, axis=-1, keepdims=True) + EPSILON)
+    return (values_in * inverse * gain).astype(BF16)
+
+
+def to_columns(rows_in, first=0):
+    many = rows_in.shape[1]
+    parts = [rows_in, jnp.zeros((LANES - 8 - first, many), F32)]
+    if first:
+        parts = [jnp.zeros((first, many), F32)] + parts
+    return jnp.concatenate(parts, axis=0).T
+
+
+def gather_quarters(net, ref):
+    chunk = ref.shape[0] // 4
+
+    def piece(y):
+        return ref.at[rows_of((2 * y + net.c) * chunk, chunk), :]
+
+    up = net.send(piece(net.y), piece(net.y), net.upper())
+    first = net.send(piece(net.y), piece(net.y), net.lower())
+
+    def second():
+        up.wait_recv()
+        other = net.send(piece(1 - net.y), piece(1 - net.y), net.lower())
+
+        def last():
+            first.wait_recv()
+            other.wait_recv()
+
+        return last
+
+    return second
+
+
+def forward_kernel(
+    tokens,
+    gain_one,
+    gain_two,
+    stage_attn,
+    stage_out,
+    stage_bias,
+    wg,
+    wu,
+    wd_t,
+    doc_ref,
+    og,
+    queries,
+    keyval,
+    offsets,
+    mass,
+    logits,
+    mixed,
+    exact,
+    middle,
+    normed_two,
+    out_grads,
+    w_attn,
+    w_out,
+    w_ffn,
+    h_one,
+    stage_ffn,
+    rows_in,
+    allowed,
+    spread,
+    gather,
+    logit_parts,
+    other_bias,
+    proj,
+    parts,
+    recv_up,
+    recv_line,
+    sems,
+):
+    net = Net(sems)
+    z, x, y, c = net.z, net.x, net.y, net.c
+    width = tokens.shape[1]
+    chunk = tokens.shape[0] // 4
+    part = 4 * chunk
+    places = Places(net, chunk)
+    hidden = wg.shape[1] // 4
+    own = rows_of((2 * y + c) * chunk, chunk)
+    tile = 256
+
+    token_net = RowGather(net, lambda yy, zz: rows_in.at[yy, zz])
+    attn_net = WeightSpread(net, stage_attn, w_attn)
+    out_net = WeightSpread(net, stage_out, w_out)
+    ffn_net = HiddenSpread(net, stage_ffn, w_ffn)
+    kv_net = CrossGather(net, lambda xx, cc: keyval.at[:, xx, cc])
+    logit_net = CrossGather(net, lambda xx, cc: logit_parts.at[xx, cc])
+    two_net = RowGather(
+        net,
+        lambda yy, zz: normed_two.at[c, yy, zz],
+        lambda yy, zz: normed_two.at[1 - c, yy, zz],
+    )
+    grad_net = RowGather(
+        net, lambda yy, zz: out_grads.at[c, yy, zz], lambda yy, zz: out_grads.at[1 - c, yy, zz]
+    )
+    attn_sum = RowSum(
+        net, lambda yy, zz: parts.at[yy, rows_of(zz * chunk, chunk), :], recv_up, recv_line
+    )
+
+    rows_in[y, z] = tokens[own, :]
+    net.barrier()
+    attn_net.start()
+    token_net.start()
+    bias_send = net.send(stage_bias, other_bias, net.lower())
+
+    out_grads[c, y, z] = og[own, :]
+    for index, ref in enumerate((wg, wu, wd_t)):
+        for zz in range(4):
+            stage_ffn[zz, :, index * hidden : (index + 1) * hidden] = ref[
+                :, zz * hidden : (zz + 1) * hidden
+            ]
+    order_tables(places, spread, gather, False)
+    every = places.every((1, places.all), 1)
+    for late in range(2):
+        at = places.own(late) + lax.broadcasted_iota(jnp.int32, (part, 1), 0)
+        pos = places.position(at)
+        start = doc_starts(pos, doc_ref)
+        seen = (every <= pos) & (every >= start)
+        allowed[late * part : (late + 1) * part, :] = jnp.where(seen, 0.0, MASKED)
+
+    token_net.forward()
+    attn_net.forward()
+    grad_net.start()
+    h_one[y] = norm(rows_in[y].reshape(part, width).astype(F32), gain_one[...])
+    token_net.finish()
+    h_one[1 - y] = norm(rows_in[1 - y].reshape(part, width).astype(F32), gain_one[...])
+    attn_net.finish()
+
+    for late in range(2):
+        r = slice(late * part, (late + 1) * part)
+        for at in range(0, w_attn.shape[1], tile):
+            cols = slice(at, min(at + tile, w_attn.shape[1]))
+            proj[r, cols] = dot_nn(h_one[late], w_attn[:, cols])
+        keyval[late, x, c] = proj[r, : 3 * LANES].astype(BF16)
+    kv_net.start()
+    bias_send.wait_recv()
+    bias = jnp.where(attn_net.first, stage_bias[z % 2], other_bias[z % 2])[:, :1]
+    logit_parts[x, c] = proj[:, 4 * LANES :].T[HEAD_DIM : HEAD_DIM + 8, :] + bias
+    logit_net.start()
+    out_net.start()
+    ffn_net.start()
+    queries[...] = (
+        proj[:, 3 * LANES :].astype(BF16).astype(F32) * HEAD_DIM ** (-0.5)
+    ).astype(BF16)
+
+    logit_net.forward()
+    grad_net.forward()
+    logit_net.finish()
+    for late in range(2):
+        for xx in range(2):
+            for cc in range(2):
+                at = (late * 4 + xx * 2 + cc) * part
+                logits[:, at : at + part] = logit_parts[xx, cc, :, late * part : (late + 1) * part]
+    turned = logits[...]
+    logs = jnp.minimum(turned, 0.0) - jnp.log(1.0 + jnp.exp(-jnp.abs(turned)))
+    offsets[...] = running_sums(places, logs, spread, gather, False)
+    kv_net.forward()
+    out_net.forward()
+    kv_net.finish()
+
+    lane = lax.broadcasted_iota(jnp.int32, (LANES, LANES), 1)
+    first = (lane // HEAD_DIM) == 0
+    for block in range(2 * part // LANES):
+        r = slice(block * LANES, (block + 1) * LANES)
+        late = (block * LANES) // part
+        many = places.all // 2 * (late + 1)
+        made, kept = [], []
+        masses = jnp.zeros((LANES, LANES), F32)
+        for head in range(3):
+            tile_k, side_k = KEY_TILES[head]
+            tile_v, side_v = VALUE_TILES[head]
+            keys = keyval[: late + 1, :, :, :, tile_k * LANES : (tile_k + 1) * LANES]
+            values = keyval[: late + 1, :, :, :, tile_v * LANES : (tile_v + 1) * LANES]
+            keys, values = keys.reshape(many, LANES), values.reshape(many, LANES)
+            scores = (
+                dot_nt(only(tile_of(queries, r, tile_k), lane, side_k), keys)
+                - offsets[head : head + 1, :many]
+                + allowed[r, :many]
+            )
+            top = jnp.max(scores, axis=1, keepdims=True)
+            probs = jnp.exp(scores - top)
+            total = jnp.sum(probs, axis=1, keepdims=True)
+            high = probs.astype(BF16)
+            rest = (probs - high.astype(F32)).astype(BF16)
+            share = 1.0 / total
+            rounded = dot_nn(high, values)
+            made.append(rounded * share)
+            kept.append((rounded + dot_nn(rest, values)) * share)
+            masses = jnp.where(lane == head, top + jnp.log(total), masses)
+        mass[r, :] = masses
+        mixed[r, :LANES] = jnp.where(first, 0.0, made[0]).astype(BF16)
+        mixed[r, LANES:] = jnp.where(first, made[1], made[2]).astype(BF16)
+        exact[r, :LANES] = jnp.where(first, 0.0, kept[0])
+        exact[r, LANES:] = jnp.where(first, kept[1], kept[2])
+        if block == 1:
+            out_net.finish()
+            ffn_net.forward()
+
+    def project(late):
+        rows = rows_of(late * part, part)
+        for at in range(0, width, tile):
+            cols = slice(at, at + tile)
+            parts[late, :, cols] = dot_nt(mixed[rows, :], w_out[cols, :]).astype(BF16)
+
+    project(1 - y)
+    attn_sum.start()
+    project(y)
+    attn_sum.middle()
+    total = tokens[own, :].astype(F32) + attn_sum.result()
+    middle[...] = total
+    normed_two[c, y, z] = norm(total, gain_two[...])
+    two_net.start()
+    grad_net.finish()
+    two_net.forward()
+    ffn_net.finish()
+    two_net.finish()
+    attn_net.drain()
+    out_net.drain()
+    net.drain()
+
+
+def backward_kernel(
+    tokens,
+    out_grad,
+    gain_one,
+    gain_two,
+    queries,
+    keyval,
+    offsets,
+    mass,
+    logits,
+    mixed,
+    exact,
+    middle,
+    normed_two,
+    out_grads,
+    w_attn,
+    w_out,
+    w_ffn,
+    h_one,
+    doc_ref,
+    layer_out,
+    tokens_grad,
+    gains,
+    bias_grad,
+    g_query,
+    g_key,
+    g_value,
+    g_forget,
+    g_out,
+    g_gate,
+    g_up,
+    g_down,
+    all_query,
+    all_grad,
+    allowed,
+    spread,
+    gather,
+    ffn_grads,
+    part_two,
+    part_out,
+    two_low,
+    two_up,
+    two_line,
+    out_low,
+    out_up,
+    out_line,
+    ffn_sum,
+    ffn_side,
+    ffn_final,
+    late_sum,
+    late_low,
+    late_side,
+    late_final,
+    last_sum,
+    last_low,
+    last_side,
+    last_final,
+    early_sum,
+    early_low,
+    early_side,
+    early_final,
+    grad_attn,
+    grad_heads,
+    stats,
+    off_parts,
+    every_off,
+    grad_qkv,
+    grad_offs,
+    part_one,
+    one_up,
+    one_line,
+    gain_parts,
+    gain_swap,
+    sems,
+):
+    net = Net(sems)
+    z, x, y, c = net.z, net.x, net.y, net.c
+    width = tokens.shape[1]
+    chunk = tokens.shape[0] // 4
+    part = 4 * chunk
+    places = Places(net, chunk)
+    hidden = w_ffn.shape[1] // 3
+    half_heads = g_query.shape[1] // 2
+    own = rows_of((2 * y + c) * chunk, chunk)
+    tile = 256
+    tiles = [slice(at, at + tile) for at in range(0, width, tile)]
+
+    query_net = CrossGather(net, lambda xx, cc: all_query.at[:, xx, cc])
+    grad_net = CrossGather(net, lambda xx, cc: all_grad.at[:, xx, cc])
+    stat_net = CrossGather(net, lambda xx, cc: stats.at[xx, cc])
+    off_net = CrossGather(net, lambda xx, cc: off_parts.at[xx, cc])
+    attn_net = RowGather(
+        net, lambda yy, zz: grad_attn.at[yy, rows_of(zz * chunk, chunk), :]
+    )
+
+    def chunks_of(ref):
+        return lambda yy, zz: ref.at[c, yy, rows_of(zz * chunk, chunk), :]
+
+    two = RowSum(net, chunks_of(part_two), two_up, two_line)
+    out = RowSum(net, chunks_of(part_out), out_up, out_line)
+    one = RowSum(
+        net, lambda yy, zz: part_one.at[yy, rows_of(zz * chunk, chunk), :], one_up, one_line
+    )
+    ffn_net = HiddenSum(net, ffn_sum, ffn_side, ffn_final)
+    late_net = WeightSum(net, late_sum, late_low, late_side, late_final)
+    last_net = WeightSum(net, last_sum, last_low, last_side, last_final)
+    early_net = WeightSum(net, early_sum, early_low, early_side, early_final)
+
+    for late in range(2):
+        all_query[late, x, c] = queries[late * part : (late + 1) * part, :]
+    net.barrier()
+    query_net.start()
+
+    for at in range(4):
+        cc, late = at // 2, at % 2
+        inputs = normed_two[cc, late].reshape(part, width)
+        gate = dot_nn(inputs, w_ffn[:, :hidden])
+        up = dot_nn(inputs, w_ffn[:, hidden : 2 * hidden])
+        grad_act = dot_nn(out_grads[cc, late].reshape(part, width), w_ffn[:, 2 * hidden :])
+        sigmoid = 1.0 / (1.0 + jnp.exp(-gate))
+        silu = gate * sigmoid
+        ffn_grads[cc, late, :, :hidden] = (
+            grad_act * up * sigmoid * (1.0 + gate * (1.0 - sigmoid))
+        ).astype(BF16)
+        ffn_grads[cc, late, :, hidden : 2 * hidden] = (grad_act * silu).astype(BF16)
+        ffn_grads[cc, late, :, 2 * hidden :] = (silu * up).astype(BF16)
+
+    def project(parts, cc, late, cols):
+        for r in tiles:
+            parts[cc, late, :, r] = dot_nt(ffn_grads[cc, late, :, cols], w_ffn[r, cols]).astype(
+                BF16
+            )
+
+    def lows(parts, recv, cols):
+        project(parts, 1 - c, 1 - y, cols)
+        first = net.send(parts.at[1 - c, 1 - y], recv.at[1 - y], net.lower())
+        project(parts, 1 - c, y, cols)
+        second = net.send(parts.at[1 - c, y], recv.at[y], net.lower())
+        project(parts, c, 1 - y, cols)
+        project(parts, c, y, cols)
+        return first, second
+
+    sends = lows(part_two, two_low, slice(0, 2 * hidden))
+    sends[0].wait_recv()
+    part_two[c, 1 - y] = (part_two[c, 1 - y].astype(F32) + two_low[1 - y].astype(F32)).astype(BF16)
+    two.start()
+    sends[1].wait_recv()
+    part_two[c, y] = (part_two[c, y].astype(F32) + two_low[y].astype(F32)).astype(BF16)
+    two.middle()
+
+    both = 4 * part
+    for cols in tiles:
+        left = normed_two[:, :, :, :, cols].reshape(both, tile)
+        right = ffn_grads[:, :, :, : 2 * hidden].reshape(both, 2 * hidden)
+        ffn_sum[cols, : 2 * hidden] = dot_tn(left, right).astype(BF16)
+        left = out_grads[:, :, :, :, cols].reshape(both, tile)
+        right = ffn_grads[:, :, :, 2 * hidden :].reshape(both, hidden)
+        ffn_sum[cols, 2 * hidden :] = dot_tn(left, right).astype(BF16)
+    ffn_net.start()
+    query_net.forward()
+
+    grad_two = two.result()
+    back_two, gain_two_part = norm_grad(grad_two, middle[...], gain_two[...])
+    grad_middle = out_grad[own, :].astype(F32) + back_two
+    grad_attn[y, rows_of(z * chunk, chunk), :] = grad_middle.astype(BF16)
+    attn_net.start()
+    out_sends = lows(part_out, out_low, slice(2 * hidden, 3 * hidden))
+    every = places.every((1, places.all), 1)
+    own_pos = [
+        places.position(places.own(late) + lax.broadcasted_iota(jnp.int32, (part, 1), 0))
+        for late in range(2)
+    ]
+    for late in range(2):
+        start = doc_starts(own_pos[late], doc_ref)
+        seen = (every <= own_pos[late]) & (every >= start)
+        allowed[late * part : (late + 1) * part, :] = jnp.where(seen, 0.0, MASKED)
+    attn_net.forward()
+    ffn_net.second()
+    query_net.finish()
+    order_tables(places, spread, gather, True)
+    attn_net.finish()
+
+    lane = lax.broadcasted_iota(jnp.int32, (part, LANES), 1)
+    for late in range(2):
+        r = slice(late * part, (late + 1) * part)
+        made = dot_nn(grad_attn[late], w_out[...])
+        grad_heads[r, :] = made.astype(BF16)
+        all_grad[late, x, c] = grad_heads[r, :]
+    grad_net.start()
+    for late in range(2):
+        r = slice(late * part, (late + 1) * part)
+        delta = jnp.zeros((part, LANES), F32)
+        for head, (tile_o, side_o) in enumerate(OUT_TILES):
+            product = tile_of(grad_heads, r, tile_o).astype(F32) * tile_of(exact, r, tile_o)
+            inner = jnp.sum(only(product, lane, side_o), axis=1, keepdims=True)
+            delta = jnp.where(lane == head, inner, delta)
+        grad_offs[r, :] = delta
+    stats[x, c, :8, :] = mass[...].T[:8, :]
+    stats[x, c, 8:, :] = grad_offs[...].T[:8, :]
+    stat_net.start()
+
+    for cols in tiles:
+        left = grad_attn[:, :, cols].reshape(2 * part, tile)
+        early_sum[cols, :] = dot_tn(left, mixed[...]).astype(BF16)
+    early_net.start()
+    out_sends[0].wait_recv()
+    part_out[c, 1 - y] = (part_out[c, 1 - y].astype(F32) + out_low[1 - y].astype(F32)).astype(BF16)
+    out.start()
+    out_sends[1].wait_recv()
+    part_out[c, y] = (part_out[c, y].astype(F32) + out_low[y].astype(F32)).astype(BF16)
+
+    lane = lax.broadcasted_iota(jnp.int32, (LANES, LANES), 1)
+    first = (lane // HEAD_DIM) == 0
+    for block in range(2 * part // LANES):
+        r = slice(block * LANES, (block + 1) * LANES)
+        late = (block * LANES) // part
+        many = places.all // 2 * (late + 1)
+        made = []
+        sums = jnp.zeros((LANES, LANES), F32)
+        for head in range(3):
+            tile_k, side_k = KEY_TILES[head]
+            tile_v, side_v = VALUE_TILES[head]
+            tile_o, side_o = OUT_TILES[head]
+            keys = keyval[: late + 1, :, :, :, tile_k * LANES : (tile_k + 1) * LANES]
+            values = keyval[: late + 1, :, :, :, tile_v * LANES : (tile_v + 1) * LANES]
+            keys, values = keys.reshape(many, LANES), values.reshape(many, LANES)
+            scores = (
+                dot_nt(only(tile_of(queries, r, tile_k), lane, side_k), keys)
+                - offsets[head : head + 1, :many]
+                + allowed[r, :many]
+            )
+            probs = jnp.exp(scores - mass[r, head : head + 1])
+            grad_probs = dot_nt(only(tile_of(grad_heads, r, tile_o), lane, side_o), values)
+            grad_scores = (probs * (grad_probs - grad_offs[r, head : head + 1])).astype(BF16)
+            made.append(dot_nn(grad_scores, keys) * HEAD_DIM ** (-0.5))
+            row_sum = jnp.sum(grad_scores.astype(F32), axis=1, keepdims=True)
+            sums = jnp.where(lane == head, row_sum, sums)
+        grad_qkv[r, 3 * LANES : 4 * LANES] = jnp.where(first, made[0], made[1]).astype(BF16)
+        grad_qkv[r, 4 * LANES :] = jnp.where(first, made[2], 0.0).astype(BF16)
+        grad_offs[r, :] = sums
+        if block == 0:
+            grad_net.forward()
+            stat_net.forward()
+        if block == 1:
+            out.middle()
+            early_net.second()
+
+    starts = doc_starts(every, doc_ref)
+    for late in range(2):
+        seen = (own_pos[late] <= every) & (own_pos[late] >= starts)
+        allowed[late * part : (late + 1) * part, :] = jnp.where(seen, 0.0, MASKED)
+    stat_net.finish()
+    grad_net.finish()
+    for late in range(2):
+        for xx in range(2):
+            for cc in range(2):
+                at = (late * 4 + xx * 2 + cc) * part
+                piece = slice(late * part, (late + 1) * part)
+                every_off[0, :, at : at + part] = stats[xx, cc, :8, piece]
+                every_off[1, :, at : at + part] = stats[xx, cc, 8:, piece]
+
+    own_offs = [
+        to_columns(offsets[:, pl.ds(pl.multiple_of(places.own(late), LANES), part)])
+        for late in range(2)
+    ]
+    for block in range(2 * part // LANES):
+        r = slice(block * LANES, (block + 1) * LANES)
+        late = (block * LANES) // part
+        within = slice(block * LANES - late * part, (block + 1) * LANES - late * part)
+        many = places.all // 2 * (2 - late)
+        lanes = slice(places.all - many, places.all)
+        keys_made, values_made = [], []
+        sums = jnp.zeros((LANES, LANES), F32)
+        for head in range(3):
+            tile_k, side_k = KEY_TILES[head]
+            tile_v, side_v = VALUE_TILES[head]
+            tile_o, side_o = OUT_TILES[head]
+            asked = all_query[late:, :, :, :, tile_k * LANES : (tile_k + 1) * LANES]
+            given = all_grad[late:, :, :, :, tile_o * LANES : (tile_o + 1) * LANES]
+            asked, given = asked.reshape(many, LANES), given.reshape(many, LANES)
+            key = keyval[late, x, c, within, tile_k * LANES : (tile_k + 1) * LANES]
+            value = keyval[late, x, c, within, tile_v * LANES : (tile_v + 1) * LANES]
+            scores = (
+                dot_nt(only(key, lane, side_k), asked)
+                - own_offs[late][within, head : head + 1]
+                + allowed[r, lanes]
+            )
+            probs = jnp.exp(scores - every_off[0, head : head + 1, lanes])
+            grad_probs = dot_nt(only(value, lane, side_v), given)
+            grad_scores = (probs * (grad_probs - every_off[1, head : head + 1, lanes])).astype(
+                BF16
+            )
+            keys_made.append(dot_nn(grad_scores, asked))
+            values_made.append(dot_nn(probs.astype(BF16), given))
+            col_sum = jnp.sum(grad_scores.astype(F32), axis=1, keepdims=True)
+            sums = jnp.where(lane == head, col_sum, sums)
+        for at, (left, right) in enumerate(
+            (
+                (keys_made[0], keys_made[1]),
+                (keys_made[2], values_made[0]),
+                (values_made[1], values_made[2]),
+            )
+        ):
+            grad_qkv[r, at * LANES : (at + 1) * LANES] = jnp.where(first, left, right).astype(BF16)
+        grad_offs[r, :] = grad_offs[r, :] - sums
+        if block == 1:
+            early_net.third()
+    off_parts[x, c] = grad_offs[...].T[:8, :]
+    off_net.start()
+    cut = late_sum.shape[1]
+    for cols in tiles:
+        left = h_one[:, :, cols].reshape(2 * part, tile)
+        late_sum[cols, :] = dot_tn(left, grad_qkv[:, :cut]).astype(BF16)
+    late_net.start()
+    off_net.forward()
+    off_net.finish()
+    for late in range(2):
+        for xx in range(2):
+            for cc in range(2):
+                at = (late * 4 + xx * 2 + cc) * part
+                every_off[0, :, at : at + part] = off_parts[
+                    xx, cc, :, late * part : (late + 1) * part
+                ]
+    late_net.second()
+    grad_logs = running_sums(places, every_off[0], spread, gather, True)
+    grad_logits = grad_logs / (1.0 + jnp.exp(logits[...]))
+    every_off[1] = grad_logits
+    for late in range(2):
+        r = slice(late * part, (late + 1) * part)
+        mine = every_off[1, :, pl.ds(pl.multiple_of(places.own(late), LANES), part)]
+        held = grad_qkv[r, cut:]
+        lane = lax.broadcasted_iota(jnp.int32, (part, LANES), 1)
+        grad_qkv[r, cut:] = jnp.where(
+            lane // HEAD_DIM == 0, held, to_columns(mine, HEAD_DIM).astype(BF16)
+        )
+
+    def back(late):
+        rows = rows_of(late * part, part)
+        for r in tiles:
+            part_one[late, :, r] = dot_nt(grad_qkv[rows, :], w_attn[r, :]).astype(BF16)
+
+    back(1 - y)
+    one.start()
+    back(y)
+    for cols in tiles:
+        left = h_one[:, :, cols].reshape(2 * part, tile)
+        last_sum[cols, :] = dot_tn(left, grad_qkv[:, cut:]).astype(BF16)
+    last_net.start()
+    late_net.third()
+    one.middle()
+    last_net.second()
+    layer_out[own, :] = (middle[...] + out.result()).astype(BF16)
+    layer_second = gather_quarters(net, layer_out)
+    grad_one = one.result()
+    back_one, gain_one_part = norm_grad(grad_one, tokens[own, :].astype(F32), gain_one[...])
+    tokens_grad[own, :] = (grad_middle + back_one).astype(BF16)
+    grad_second = gather_quarters(net, tokens_grad)
+    row = lax.broadcasted_iota(jnp.int32, (8, width), 0)
+    gain_parts[z, :, :width] = jnp.where(
+        row == 0, gain_one_part, jnp.where(row == 1, gain_two_part, 0.0)
+    )
+    gain_parts[z, :, width:] = jnp.broadcast_to(
+        jnp.sum(grad_logits, axis=1, keepdims=True), (8, LANES)
+    )
+    came, sent = net.alloc(4), net.alloc(4)
+    for step in NEAR_FIRST:
+        net.begin(
+            net.copy(
+                gain_parts.at[z], gain_parts.at[z], sent + step, came + z, net.to(z=net.next(step))
+            )
+        )
+    last_net.third()
+    layer_last = layer_second()
+    grad_last = grad_second()
+
+    ffn_net.finish()
+    for zz in range(4):
+        cols = slice(zz * hidden, (zz + 1) * hidden)
+        for index, ref in enumerate((g_gate, g_up, g_down)):
+            ref[:, cols] = ffn_final[zz, :, index * hidden : (index + 1) * hidden].astype(F32)
+    early_net.finish()
+    for u in range(2):
+        cols = slice(u * half_heads, (u + 1) * half_heads)
+        g_out[:, cols] = early_final[u, :, HEAD_DIM:].astype(F32)
+
+    total = jnp.zeros((8, width), F32)
+    for step in (0,) + NEAR_FIRST:
+        src = net.next(step)
+        if step:
+            net.got(gain_parts.at[src], came + src)
+        total = total + gain_parts[src, :, :width]
+    for u in range(2):
+        bias_grad[u] = gain_parts[2 * c + u, :, width:]
+    for step, peer in enumerate((net.lower(), net.upper(), net.side())):
+        gain_swap[2 * step] = total
+        swap = net.send(gain_swap.at[2 * step], gain_swap.at[2 * step + 1], peer)
+        swap.wait_recv()
+        total = total + gain_swap[2 * step + 1]
+    gains[...] = total
+
+    late_net.finish()
+    last_net.finish()
+    for u in range(2):
+        cols = slice(u * half_heads, (u + 1) * half_heads)
+        got = late_final[u].astype(F32)
+        rest = last_final[u].astype(F32)
+        g_key[:, cols] = got[:, :half_heads]
+        g_value[:, cols] = got[:, half_heads : 2 * half_heads]
+        g_query[:, cols] = jnp.concatenate(
+            [got[:, 2 * half_heads :], rest[:, :HEAD_DIM]], axis=1
+        )
+        g_forget[u] = rest
+    layer_last()
+    grad_last()
+    for part_net in (late_net, last_net, early_net, net):
+        part_net.drain()
+
+
+VMEM = pl.BlockSpec(memory_space=pltpu.VMEM)
+
+
+def shapes_of(made):
+    return [jax.ShapeDtypeStruct(*m) for m in made]
+
+
+def forward_shapes(rows, width, heads, hidden):
+    chunk = rows // 4
+    part = 4 * chunk
+    every = 32 * chunk
+    attn = (3 * heads * HEAD_DIM // 2) + HEAD_DIM
+    outs = [
+        ((2 * part, 2 * LANES), BF16),
+        ((2, 2, 2, part, 3 * LANES), BF16),
+        ((8, every), F32),
+        ((2 * part, LANES), F32),
+        ((8, every), F32),
+        ((2 * part, 2 * LANES), BF16),
+        ((2 * part, 2 * LANES), F32),
+        ((chunk, width), F32),
+        ((2, 2, 4, chunk, width), BF16),
+        ((2, 2, 4, chunk, width), BF16),
+        ((width, attn), BF16),
+        ((width, 2 * LANES), BF16),
+        ((width, 3 * hidden), BF16),
+        ((2, part, width), BF16),
+    ]
+    scratch = [
+        ((4, width // 8, 3 * hidden), BF16),
+        ((2, 4, chunk, width), BF16),
+        ((2 * part, every), F32),
+        ((every, LANES), F32),
+        ((every // chunk, every), F32),
+        ((2, 2, 8, 2 * part), F32),
+        ((2, 8, LANES), F32),
+        ((2 * part, attn), F32),
+        ((2, part, width), BF16),
+        ((4, chunk, width), BF16),
+        ((4, chunk, width), BF16),
+    ]
+    return outs, scratch
+
+
+def run_forward(heads, tokens, gain_one, gain_two, stages, ffn, doc_lengths, out_grad):
+    rows, width = tokens.shape
+    outs, scratch = forward_shapes(rows, width, heads, ffn[0].shape[1] // 4)
+    return pl.pallas_call(
+        forward_kernel,
+        out_shape=shapes_of(outs),
+        in_specs=[VMEM] * 9 + [pl.BlockSpec(memory_space=pltpu.SMEM), VMEM],
+        out_specs=[VMEM] * len(outs),
+        scratch_shapes=[pltpu.VMEM(*m) for m in scratch] + [pltpu.SemaphoreType.DMA((256,))],
+        compiler_params=pltpu.CompilerParams(
+            collective_id=0, has_side_effects=True, vmem_limit_bytes=60 << 20
+        ),
+    )(tokens, gain_one, gain_two, *stages, *ffn, doc_lengths, out_grad)
+
+
+def backward_shapes(rows, width, heads, hidden):
+    chunk = rows // 4
+    part = 4 * chunk
+    every = 32 * chunk
+    block = width // 8
+    attn = (3 * heads * HEAD_DIM // 2) + HEAD_DIM
+    head_cols = heads * HEAD_DIM
+    outs = [
+        ((rows, width), BF16),
+        ((rows, width), BF16),
+        ((8, width), F32),
+        ((2, 8, LANES), F32),
+        ((block, head_cols), F32),
+        ((block, head_cols), F32),
+        ((block, head_cols), F32),
+        ((2, block, LANES), F32),
+        ((block, head_cols), F32),
+        ((block, 4 * hidden), F32),
+        ((block, 4 * hidden), F32),
+        ((block, 4 * hidden), F32),
+    ]
+
+    def weight_sum(columns):
+        return [
+            ((width, columns), BF16),
+            ((width // 2, columns), BF16),
+            ((2, block, columns), BF16),
+            ((2, block, columns), BF16),
+        ]
+
+    row_sum = [((2, part, width), BF16), ((4, chunk, width), BF16), ((4, chunk, width), BF16)]
+    scratch = [
+        ((2, 2, 2, part, 2 * LANES), BF16),
+        ((2, 2, 2, part, 2 * LANES), BF16),
+        ((2 * part, every), F32),
+        ((every, LANES), F32),
+        ((every // chunk, every), F32),
+        ((2, 2, part, 3 * hidden), BF16),
+        ((2, 2, part, width), BF16),
+        ((2, 2, part, width), BF16),
+        *row_sum,
+        *row_sum,
+        ((width, 3 * hidden), BF16),
+        ((4, block, 3 * hidden), BF16),
+        ((4, block, 3 * hidden), BF16),
+        *weight_sum(attn - LANES),
+        *weight_sum(LANES),
+        *weight_sum(2 * LANES),
+        ((2, part, width), BF16),
+        ((2 * part, 2 * LANES), BF16),
+        ((2, 2, 16, 2 * part), F32),
+        ((2, 2, 8, 2 * part), F32),
+        ((2, 8, every), F32),
+        ((2 * part, attn), BF16),
+        ((2 * part, LANES), F32),
+        *row_sum,
+        ((4, 8, width + LANES), F32),
+        ((6, 8, width), F32),
+    ]
+    return outs, scratch
+
+
+def run_backward(heads, hidden, tokens, out_grad, gain_one, gain_two, made, doc_lengths):
+    rows, width = tokens.shape
+    outs, scratch = backward_shapes(rows, width, heads, hidden)
+    return pl.pallas_call(
+        backward_kernel,
+        out_shape=shapes_of(outs),
+        in_specs=[VMEM] * 18 + [pl.BlockSpec(memory_space=pltpu.SMEM)],
+        out_specs=[VMEM] * len(outs),
+        scratch_shapes=[pltpu.VMEM(*m) for m in scratch] + [pltpu.SemaphoreType.DMA((320,))],
+        compiler_params=pltpu.CompilerParams(
+            collective_id=1, has_side_effects=True, vmem_limit_bytes=63 << 20
+        ),
+    )(tokens, out_grad, gain_one, gain_two, *made, doc_lengths)
+
+
+def kernel_body(
+    tokens,
+    attn_gain,
+    query_weight,
+    key_weight,
+    value_weight,
+    forget_weight,
+    forget_bias,
+    out_weight,
+    ffn_gain,
+    gate_weight,
+    up_weight,
+    down_weight,
+    doc_lengths,
+    out_grad,
+):
+    heads = forget_bias.shape[0]
+    width = tokens.shape[1]
+    hidden = gate_weight.shape[1] // 4
+    half_heads = heads // 2
+    cols = half_heads * HEAD_DIM
+    block = query_weight.shape[0]
+    out_t = out_weight.T
+
+    def halves(weight):
+        return weight.reshape(block, 2, -1).transpose(1, 0, 2)
+
+    stage_attn = jnp.concatenate(
+        [
+            halves(key_weight),
+            halves(value_weight),
+            halves(query_weight),
+            halves(forget_weight),
+            jnp.zeros((2, block, HEAD_DIM - half_heads), BF16),
+        ],
+        axis=2,
+    )
+    stage_out = jnp.pad(halves(out_t), ((0, 0), (0, 0), (2 * LANES - cols, 0)))
+    stage_bias = jnp.broadcast_to(
+        jnp.pad(forget_bias.reshape(2, half_heads), ((0, 0), (0, 8 - half_heads)))[:, :, None],
+        (2, 8, LANES),
+    )
+    gain_one = attn_gain.reshape(1, width)
+    gain_two = ffn_gain.reshape(1, width)
+    made = run_forward(
+        heads,
+        tokens,
+        gain_one,
+        gain_two,
+        (stage_attn, stage_out, stage_bias),
+        (gate_weight, up_weight, down_weight.T),
+        doc_lengths,
+        out_grad,
+    )
+    (
+        layer_out,
+        tokens_grad,
+        gains,
+        bias_grad,
+        g_query,
+        g_key,
+        g_value,
+        g_forget,
+        g_out,
+        g_gate,
+        g_up,
+        g_down,
+    ) = run_backward(heads, hidden, tokens, out_grad, gain_one, gain_two, made, doc_lengths)
+    return (
+        layer_out,
+        tokens_grad,
+        gains[0],
+        g_query,
+        g_key,
+        g_value,
+        g_forget[:, :, HEAD_DIM : HEAD_DIM + half_heads].transpose(1, 0, 2).reshape(block, heads),
+        bias_grad[:, :half_heads, 0].reshape(heads),
+        g_out.T,
+        gains[1],
+        g_gate,
+        g_up,
+        g_down.T,
+    )
+
+
+def kernels_fit(tokens, forget_bias, gate_weight):
+    rows, width = tokens.shape
+    heads = forget_bias.shape[0]
+    return (
+        lax.axis_size("seq") == 8
+        and lax.axis_size("head") == 4
+        and heads == 6
+        and rows == 2 * LANES
+        and width % 256 == 0
+        and gate_weight.shape[1] % (4 * LANES) == 0
+        and width * gate_weight.shape[1] <= (1536 * 1024)
+    )
 
 
 def unchanged(carried):
@@ -108,7 +1574,7 @@
     )
 
 
-def body(
+def plain_body(
     tokens,
     attn_gain,
     query_weight,
@@ -419,6 +1885,11 @@
         up_weight_grad,
         down_weight_grad,
     )
+
+
+def body(*args):
+    fits = kernels_fit(args[0], args[6], args[9])
+    return (kernel_body if fits else plain_body)(*args)
 
 
 def solution(mesh):

time: 918 us -> 322 us (0.35)
  waiting for transfers between devices: 533 us -> 0 us
  Pallas kernels: 0 us -> 292 us
  blocking collectives: 134 us -> 0 us
  matrix products: 108 us -> 0 us
  local copies, waits for them, and re-layouts: 69.3 us -> 23.5 us
  other arithmetic: 43.9 us -> 0 us
  between operations: 20.2 us -> 0.98 us
    pallas_call x0 -> x2, Pallas kernels: none -> 292 us  [the longest x1 154 us: run_backward(): pl.pallas_call(backward_kernel, out_shape=shapes_of(outs), in_specs=[VMEM...]
    unnamed x11 -> x0, waiting for transfers between devices: 223 us -> none
    all_gather x4 -> x0, waiting for transfers between devices: 217 us -> none  [the longest x1 114 us: body(): lax.all_gather(jnp.concatenate([out_weight.T, gate_weight, up_weight, dow...]
    dot_general x37 -> x0, matrix products: 108 us -> none  [the longest x2 17.4 us: piece_grads(): jnp.einsum('qhd,khd->hqk', grad_heads, value_heads, preferred_element_typ...]
    all_gather x3 -> x0, blocking collectives: 94.2 us -> none  [the longest x1 32.6 us: body(): lax.all_gather(jnp.concatenate([log_mass.T, row_delta.T], axis=1), 'seq',...]
    psum x3 -> x0, waiting for transfers between devices: 92.7 us -> none  [the longest x1 43 us: body(): grad_two = lax.psum(part_two, 'head')]
    psum x1 -> x0, blocking collectives: 39.4 us -> none  [body(): lax.psum((gain_one, gain_two, jnp.sum(grad_logit, axis=0)), 'seq')]
    unnamed x100 -> x27, local copies, waits for them, and re-layouts: 36.2 us -> 8.52 us
  transfers between devices with their start and end apart: 9 -> 0, of which waited for: 8 -> 0; matrix products, arithmetic and copies ran while one was open for 14% -> 0% of each run, Pallas kernels for 0% -> 0%
where the time goes in v3:
time: 322 us; the launch traced here: 317 us
  Pallas kernels  292 us (91%)
  local copies, waits for them, and re-layouts  23.5 us (7%)
    pallas_call x1, Pallas kernels, run_backward(): pl.pallas_call(backward_kernel, out_shape=shapes_of(outs), in_specs=[VMEM...  154 us
    pallas_call x1, Pallas kernels, run_forward(): pl.pallas_call(forward_kernel, out_shape=shapes_of(outs), in_specs=[VMEM]...  139 us
    unnamed x27, local copies, waits for them, and re-layouts  8.52 us

profile of v3, /device:TPU:0, one launch (start us, length us, event | category | flops | bytes accessed | tf_op | source)
XLA Modules:
  0.0 316.7 jit_solution(14189495334407359888)
XLA Ops:
  0.6 0.0 copy-start.8
  0.7 0.8 reshape.61
  1.4 0.7 reshape.59
  2.1 1.3 reshape.54.gain_one
  3.4 1.3 reshape.55.gain_two
  4.7 0.7 broadcast_in_dim.10.stage_bias
  5.4 0.2 copy.30
  5.6 1.1 reshape.58
  6.6 1.1 reshape.56
  7.7 1.1 reshape.57
  8.9 1.1 concatenate.3.stage_attn
  10.0 0.1 reshape.60
  10.2 0.8 pad.8.stage_out
  11.0 138.7 %shard_map.237 = (bf16[512,256]{1,0:T(8,128)(2,1)}, bf16[2,2,2,256,384]{4,3,2,1,0:T(8,128)(2,1)}, f32[8,2048]{1,0:T(8,128)}, f32[512,128]{1,0:T(8,128)}, f32[8,2...) custom-call(bf16[256,1536]{1,0:T(8,128)(2,1)} %tokens.3, ...), custom_call_target="tpu_custom_call" | custom-call | tf_op jit(solution)/shard_map/pallas_call | solution.py:1292
  149.7 153.5 %shard_map.238 = (bf16[256,1536]{1,0:T(8,128)(2,1)}, bf16[256,1536]{1,0:T(8,128)(2,1)}, f32[8,1536]{1,0:T(8,128)}, f32[2,8,128]{2,1,0:T(8,128)}, f32[192,384]{1,...) custom-call(bf16[256,1536]{1,0:T(8,128)(2,1)} %tokens.3, ...), custom_call_target="tpu_custom_call" | custom-call | tf_op jit(solution)/shard_map/pallas_call | solution.py:1369
  303.3 0.9 slice_reduce_fusion.2
  304.1 0.6 reshape_squeeze.3
  304.7 1.5 slice_reduce_fusion
  306.2 1.0 slice_bitcast_fusion
  307.3 0.1 copy.32
  307.4 0.6 reshape.62
  308.0 2.1 copy.48
  310.1 0.9 copy.49
  311.0 0.7 copy.50
  311.7 0.0 copy-done.6
  311.7 0.7 copy.51
  312.5 0.7 copy.52
  313.2 0.7 copy.53
  313.9 0.9 copy.54
  314.8 0.0 copy-done.1
  314.8 0.9 copy.55
  315.7 0.9 copy.56
  (20 shorter events, 0.1 us)
Async XLA Ops:
  0.6 9.3 %copy-start.8 = (bf16[384,192]{0,1:T(8,128)(2,1)S(1)}, bf16[384,192]{0,1:T(8,128)(2,1)}, u32[]{:S(2)}) copy-start(bf16[384,192]{0,1:T(8,128)(2,1)} %param.21) | copy-start | bytes 442372
  303.2 6.9 %copy-start.3 = (bf16[256,1536]{1,0:T(8,128)(2,1)S(1)}, bf16[256,1536]{1,0:T(8,128)(2,1)}, u32[]{:S(2)}) copy-start(bf16[256,1536]{1,0:T(8,128)(2,1)} %get-tuple-element.83) | copy-start | bytes 2359300
  303.2 7.8 %copy-start.7 = (f32[192,384]{1,0:T(8,128)S(1)}, f32[192,384]{1,0:T(8,128)}, u32[]{:S(2)}) copy-start(f32[192,384]{1,0:T(8,128)} %get-tuple-element.85) | copy-start | bytes 884740
  303.2 8.5 %copy-start.6 = (f32[192,384]{1,0:T(8,128)S(1)}, f32[192,384]{1,0:T(8,128)}, u32[]{:S(2)}) copy-start(f32[192,384]{1,0:T(8,128)} %get-tuple-element.86) | copy-start | bytes 884740
  307.3 5.2 %copy-start.5 = (f32[192,384]{1,0:T(8,128)S(1)}, f32[192,384]{1,0:T(8,128)}, u32[]{:S(2)}) copy-start(f32[192,384]{1,0:T(8,128)} %get-tuple-element.87) | copy-start | bytes 884740
  308.0 5.2 %copy-start.4 = (f32[192,384]{1,0:T(8,128)S(1)}, f32[192,384]{1,0:T(8,128)}, u32[]{:S(2)}) copy-start(f32[192,384]{1,0:T(8,128)} %get-tuple-element.61) | copy-start | bytes 884740
  310.1 3.8 %copy-start.2 = (f32[192,1024]{1,0:T(8,128)S(1)}, f32[192,1024]{1,0:T(8,128)}, u32[]{:S(2)}) copy-start(f32[192,1024]{1,0:T(8,128)} %get-tuple-element.92) | copy-start | bytes 2359300
  311.0 3.8 %copy-start.1 = (f32[192,1024]{1,0:T(8,128)S(1)}, f32[192,1024]{1,0:T(8,128)}, u32[]{:S(2)}) copy-start(f32[192,1024]{1,0:T(8,128)} %get-tuple-element.93) | copy-start | bytes 2359300
  311.7 3.9 %copy-start = (f32[192,1024]{1,0:T(8,128)S(1)}, f32[192,1024]{1,0:T(8,128)}, u32[]{:S(2)}) copy-start(f32[192,1024]{1,0:T(8,128)} %get-tuple-element.64) | copy-start | bytes 2359300

commit v4 on v3

--- a/solution.py
+++ b/solution.py
@@ -635,18 +635,38 @@
     return second
 
 
-def forward_kernel(
+def layer_kernel(
     tokens,
+    out_grad,
     gain_one,
     gain_two,
-    stage_attn,
-    stage_out,
-    stage_bias,
+    wq,
+    wk,
+    wv,
+    forget_t,
+    bias_in,
+    wo_t,
     wg,
     wu,
     wd_t,
     doc_ref,
-    og,
+    layer_out,
+    tokens_grad,
+    gains,
+    bias_grad,
+    late_final,
+    last_final,
+    early_final,
+    ffn_final,
+    stage_attn,
+    stage_out,
+    stage_bias,
+    other_bias,
+    h_one,
+    allowed,
+    spread,
+    gather,
+    logit_parts,
     queries,
     keyval,
     offsets,
@@ -660,18 +680,42 @@
     w_attn,
     w_out,
     w_ffn,
-    h_one,
-    stage_ffn,
-    rows_in,
-    allowed,
-    spread,
-    gather,
-    logit_parts,
-    other_bias,
-    proj,
-    parts,
-    recv_up,
-    recv_line,
+    all_query,
+    all_grad,
+    ffn_grads,
+    part_two,
+    part_out,
+    two_low,
+    two_up,
+    two_line,
+    out_low,
+    out_up,
+    out_line,
+    ffn_sum,
+    ffn_side,
+    late_sum,
+    late_low,
+    late_side,
+    last_sum,
+    last_low,
+    last_side,
+    early_sum,
+    early_low,
+    early_side,
+    grad_attn,
+    grad_heads,
+    stats,
+    off_parts,
+    every_off,
+    grad_qkv,
+    grad_offs,
+    part_one,
+    one_up,
+    one_line,
+    gain_parts,
+    gain_swap,
+    own_tokens,
+    near_sems,
     sems,
 ):
     net = Net(sems)
@@ -683,11 +727,13 @@
     hidden = wg.shape[1] // 4
     own = rows_of((2 * y + c) * chunk, chunk)
     tile = 256
-
-    token_net = RowGather(net, lambda yy, zz: rows_in.at[yy, zz])
-    attn_net = WeightSpread(net, stage_attn, w_attn)
+    scale_one = gain_one[...].reshape(1, width)
+    scale_two = gain_two[...].reshape(1, width)
+
+    token_net = RowGather(net, lambda yy, zz: grad_attn.at[yy, rows_of(zz * chunk, chunk), :])
+    weight_net = WeightSpread(net, stage_attn, w_attn)
     out_net = WeightSpread(net, stage_out, w_out)
-    ffn_net = HiddenSpread(net, stage_ffn, w_ffn)
+    units_net = HiddenSpread(net, ffn_side, w_ffn)
     kv_net = CrossGather(net, lambda xx, cc: keyval.at[:, xx, cc])
     logit_net = CrossGather(net, lambda xx, cc: logit_parts.at[xx, cc])
     two_net = RowGather(
@@ -695,25 +741,64 @@
         lambda yy, zz: normed_two.at[c, yy, zz],
         lambda yy, zz: normed_two.at[1 - c, yy, zz],
     )
-    grad_net = RowGather(
+    given_net = RowGather(
         net, lambda yy, zz: out_grads.at[c, yy, zz], lambda yy, zz: out_grads.at[1 - c, yy, zz]
     )
     attn_sum = RowSum(
-        net, lambda yy, zz: parts.at[yy, rows_of(zz * chunk, chunk), :], recv_up, recv_line
-    )
-
-    rows_in[y, z] = tokens[own, :]
+        net, lambda yy, zz: part_one.at[yy, rows_of(zz * chunk, chunk), :], one_up, one_line
+    )
+
+    near = [
+        (tokens.at[own, :], own_tokens),
+        (tokens.at[own, :], grad_attn.at[y, rows_of(z * chunk, chunk), :]),
+        (out_grad.at[own, :], out_grads.at[c, y, z]),
+    ]
+    for index, ref in enumerate((wg, wu, wd_t)):
+        for zz in range(4):
+            near.append(
+                (
+                    ref.at[:, zz * hidden : (zz + 1) * hidden],
+                    ffn_side.at[zz, :, index * hidden : (index + 1) * hidden],
+                )
+            )
+    fetched = [
+        pltpu.make_async_copy(src, dst, near_sems.at[at]) for at, (src, dst) in enumerate(near)
+    ]
+    for copy in fetched:
+        copy.start()
+    half_cols = wq.shape[1] // 2
+    half_heads = half_cols // HEAD_DIM
+    block = wq.shape[0]
+    forget = forget_t[...].astype(F32)
+    row8 = lax.broadcasted_iota(jnp.int32, (8, LANES), 0)
+    for u in range(2):
+        cols = slice(u * half_cols, (u + 1) * half_cols)
+        for index, ref in enumerate((wk, wv)):
+            stage_attn[u, :, index * half_cols : (index + 1) * half_cols] = ref[:, cols]
+        rows8 = jnp.concatenate(
+            [
+                forget[u * half_heads : (u + 1) * half_heads, :],
+                jnp.zeros((8 - half_heads, block), F32),
+            ],
+            axis=0,
+        )
+        rows8 = jnp.concatenate([rows8, jnp.zeros((8, 2 * LANES - block), F32)], axis=1)
+        stage_attn[u, :, 4 * LANES :] = to_columns(rows8, HEAD_DIM)[:block].astype(BF16)
+        stage_attn[u, :, 2 * half_cols : 3 * half_cols] = wq[:, cols]
+        biases = jnp.zeros((8, LANES), F32)
+        for head in range(half_heads):
+            biases = jnp.where(row8 == head, bias_in[u * half_heads + head], biases)
+        stage_bias[u] = biases
     net.barrier()
-    attn_net.start()
+    for copy in fetched[:3]:
+        copy.wait()
+    weight_net.start()
     token_net.start()
     bias_send = net.send(stage_bias, other_bias, net.lower())
-
-    out_grads[c, y, z] = og[own, :]
-    for index, ref in enumerate((wg, wu, wd_t)):
-        for zz in range(4):
-            stage_ffn[zz, :, index * hidden : (index + 1) * hidden] = ref[
-                :, zz * hidden : (zz + 1) * hidden
-            ]
+    for u in range(2):
+        stage_out[u, :, :HEAD_DIM] = jnp.zeros((block, HEAD_DIM), BF16)
+        stage_out[u, :, HEAD_DIM:] = wo_t[:, u * half_cols : (u + 1) * half_cols]
+
     order_tables(places, spread, gather, False)
     every = places.every((1, places.all), 1)
     for late in range(2):
@@ -721,35 +806,34 @@
         pos = places.position(at)
         start = doc_starts(pos, doc_ref)
         seen = (every <= pos) & (every >= start)
-        allowed[late * part : (late + 1) * part, :] = jnp.where(seen, 0.0, MASKED)
+        allowed[late * part : (late + 1) * part, :] = jnp.where(seen, 0.0, MASKED).astype(BF16)
 
     token_net.forward()
-    attn_net.forward()
-    grad_net.start()
-    h_one[y] = norm(rows_in[y].reshape(part, width).astype(F32), gain_one[...])
+    weight_net.forward()
+    given_net.start()
+    h_one[y] = norm(grad_attn[y].astype(F32), scale_one)
     token_net.finish()
-    h_one[1 - y] = norm(rows_in[1 - y].reshape(part, width).astype(F32), gain_one[...])
-    attn_net.finish()
-
+    h_one[1 - y] = norm(grad_attn[1 - y].astype(F32), scale_one)
+    weight_net.finish()
+
+    for late in range(2):
+        keyval[late, x, c] = dot_nn(h_one[late], w_attn[:, : 3 * LANES]).astype(BF16)
+    kv_net.start()
+    bias_send.wait_recv()
+    bias = jnp.where(weight_net.first, stage_bias[z % 2], other_bias[z % 2])[:, :1]
     for late in range(2):
         r = slice(late * part, (late + 1) * part)
-        for at in range(0, w_attn.shape[1], tile):
-            cols = slice(at, min(at + tile, w_attn.shape[1]))
-            proj[r, cols] = dot_nn(h_one[late], w_attn[:, cols])
-        keyval[late, x, c] = proj[r, : 3 * LANES].astype(BF16)
-    kv_net.start()
-    bias_send.wait_recv()
-    bias = jnp.where(attn_net.first, stage_bias[z % 2], other_bias[z % 2])[:, :1]
-    logit_parts[x, c] = proj[:, 4 * LANES :].T[HEAD_DIM : HEAD_DIM + 8, :] + bias
+        made = dot_nn(h_one[late], w_attn[:, 3 * LANES :])
+        logit_parts[x, c, :, r] = made[:, LANES:].T[HEAD_DIM : HEAD_DIM + 8, :] + bias
+        queries[r, :] = (made.astype(BF16).astype(F32) * HEAD_DIM ** (-0.5)).astype(BF16)
     logit_net.start()
     out_net.start()
-    ffn_net.start()
-    queries[...] = (
-        proj[:, 3 * LANES :].astype(BF16).astype(F32) * HEAD_DIM ** (-0.5)
-    ).astype(BF16)
+    for copy in fetched[3:]:
+        copy.wait()
+    units_net.start()
 
     logit_net.forward()
-    grad_net.forward()
+    given_net.forward()
     logit_net.finish()
     for late in range(2):
         for xx in range(2):
@@ -780,7 +864,7 @@
             scores = (
                 dot_nt(only(tile_of(queries, r, tile_k), lane, side_k), keys)
                 - offsets[head : head + 1, :many]
-                + allowed[r, :many]
+                + allowed[r, :many].astype(F32)
             )
             top = jnp.max(scores, axis=1, keepdims=True)
             probs = jnp.exp(scores - top)
@@ -799,116 +883,29 @@
         exact[r, LANES:] = jnp.where(first, kept[1], kept[2])
         if block == 1:
             out_net.finish()
-            ffn_net.forward()
+            units_net.forward()
 
     def project(late):
         rows = rows_of(late * part, part)
         for at in range(0, width, tile):
             cols = slice(at, at + tile)
-            parts[late, :, cols] = dot_nt(mixed[rows, :], w_out[cols, :]).astype(BF16)
+            part_one[late, :, cols] = dot_nt(mixed[rows, :], w_out[cols, :]).astype(BF16)
 
     project(1 - y)
     attn_sum.start()
     project(y)
     attn_sum.middle()
-    total = tokens[own, :].astype(F32) + attn_sum.result()
+    total = own_tokens[...].astype(F32) + attn_sum.result()
     middle[...] = total
-    normed_two[c, y, z] = norm(total, gain_two[...])
+    normed_two[c, y, z] = norm(total, scale_two)
+    net.drain()
     two_net.start()
-    grad_net.finish()
+    given_net.finish()
     two_net.forward()
-    ffn_net.finish()
+    units_net.finish()
     two_net.finish()
-    attn_net.drain()
-    out_net.drain()
-    net.drain()
-
-
-def backward_kernel(
-    tokens,
-    out_grad,
-    gain_one,
-    gain_two,
-    queries,
-    keyval,
-    offsets,
-    mass,
-    logits,
-    mixed,
-    exact,
-    middle,
-    normed_two,
-    out_grads,
-    w_attn,
-    w_out,
-    w_ffn,
-    h_one,
-    doc_ref,
-    layer_out,
-    tokens_grad,
-    gains,
-    bias_grad,
-    g_query,
-    g_key,
-    g_value,
-    g_forget,
-    g_out,
-    g_gate,
-    g_up,
-    g_down,
-    all_query,
-    all_grad,
-    allowed,
-    spread,
-    gather,
-    ffn_grads,
-    part_two,
-    part_out,
-    two_low,
-    two_up,
-    two_line,
-    out_low,
-    out_up,
-    out_line,
-    ffn_sum,
-    ffn_side,
-    ffn_final,
-    late_sum,
-    late_low,
-    late_side,
-    late_final,
-    last_sum,
-    last_low,
-    last_side,
-    last_final,
-    early_sum,
-    early_low,
-    early_side,
-    early_final,
-    grad_attn,
-    grad_heads,
-    stats,
-    off_parts,
-    every_off,
-    grad_qkv,
-    grad_offs,
-    part_one,
-    one_up,
-    one_line,
-    gain_parts,
-    gain_swap,
-    sems,
-):
-    net = Net(sems)
-    z, x, y, c = net.z, net.x, net.y, net.c
-    width = tokens.shape[1]
-    chunk = tokens.shape[0] // 4
-    part = 4 * chunk
-    places = Places(net, chunk)
-    hidden = w_ffn.shape[1] // 3
-    half_heads = g_query.shape[1] // 2
-    own = rows_of((2 * y + c) * chunk, chunk)
-    tile = 256
+
+    half_heads = half_cols
     tiles = [slice(at, at + tile) for at in range(0, width, tile)]
 
     query_net = CrossGather(net, lambda xx, cc: all_query.at[:, xx, cc])
@@ -934,7 +931,6 @@
 
     for late in range(2):
         all_query[late, x, c] = queries[late * part : (late + 1) * part, :]
-    net.barrier()
     query_net.start()
 
     for at in range(4):
@@ -982,12 +978,12 @@
         left = out_grads[:, :, :, :, cols].reshape(both, tile)
         right = ffn_grads[:, :, :, 2 * hidden :].reshape(both, hidden)
         ffn_sum[cols, 2 * hidden :] = dot_tn(left, right).astype(BF16)
+    query_net.forward()
     ffn_net.start()
-    query_net.forward()
 
     grad_two = two.result()
-    back_two, gain_two_part = norm_grad(grad_two, middle[...], gain_two[...])
-    grad_middle = out_grad[own, :].astype(F32) + back_two
+    back_two, gain_two_part = norm_grad(grad_two, middle[...], scale_two)
+    grad_middle = out_grads[c, y, z].astype(F32) + back_two
     grad_attn[y, rows_of(z * chunk, chunk), :] = grad_middle.astype(BF16)
     attn_net.start()
     out_sends = lows(part_out, out_low, slice(2 * hidden, 3 * hidden))
@@ -999,7 +995,7 @@
     for late in range(2):
         start = doc_starts(own_pos[late], doc_ref)
         seen = (every <= own_pos[late]) & (every >= start)
-        allowed[late * part : (late + 1) * part, :] = jnp.where(seen, 0.0, MASKED)
+        allowed[late * part : (late + 1) * part, :] = jnp.where(seen, 0.0, MASKED).astype(BF16)
     attn_net.forward()
     ffn_net.second()
     query_net.finish()
@@ -1053,7 +1049,7 @@
             scores = (
                 dot_nt(only(tile_of(queries, r, tile_k), lane, side_k), keys)
                 - offsets[head : head + 1, :many]
-                + allowed[r, :many]
+                + allowed[r, :many].astype(F32)
             )
             probs = jnp.exp(scores - mass[r, head : head + 1])
             grad_probs = dot_nt(only(tile_of(grad_heads, r, tile_o), lane, side_o), values)
@@ -1074,7 +1070,7 @@
     starts = doc_starts(every, doc_ref)
     for late in range(2):
         seen = (own_pos[late] <= every) & (own_pos[late] >= starts)
-        allowed[late * part : (late + 1) * part, :] = jnp.where(seen, 0.0, MASKED)
+        allowed[late * part : (late + 1) * part, :] = jnp.where(seen, 0.0, MASKED).astype(BF16)
     stat_net.finish()
     grad_net.finish()
     for late in range(2):
@@ -1109,7 +1105,7 @@
             scores = (
                 dot_nt(only(key, lane, side_k), asked)
                 - own_offs[late][within, head : head + 1]
-                + allowed[r, lanes]
+                + allowed[r, lanes].astype(F32)
             )
             probs = jnp.exp(scores - every_off[0, head : head + 1, lanes])
             grad_probs = dot_nt(only(value, lane, side_v), given)
@@ -1178,7 +1174,7 @@
     layer_out[own, :] = (middle[...] + out.result()).astype(BF16)
     layer_second = gather_quarters(net, layer_out)
     grad_one = one.result()
-    back_one, gain_one_part = norm_grad(grad_one, tokens[own, :].astype(F32), gain_one[...])
+    back_one, gain_one_part = norm_grad(grad_one, own_tokens[...].astype(F32), scale_one)
     tokens_grad[own, :] = (grad_middle + back_one).astype(BF16)
     grad_second = gather_quarters(net, tokens_grad)
     row = lax.broadcasted_iota(jnp.int32, (8, width), 0)
@@ -1200,14 +1196,7 @@
     grad_last = grad_second()
 
     ffn_net.finish()
-    for zz in range(4):
-        cols = slice(zz * hidden, (zz + 1) * hidden)
-        for index, ref in enumerate((g_gate, g_up, g_down)):
-            ref[:, cols] = ffn_final[zz, :, index * hidden : (index + 1) * hidden].astype(F32)
     early_net.finish()
-    for u in range(2):
-        cols = slice(u * half_heads, (u + 1) * half_heads)
-        g_out[:, cols] = early_final[u, :, HEAD_DIM:].astype(F32)
 
     total = jnp.zeros((8, width), F32)
     for step in (0,) + NEAR_FIRST:
@@ -1226,35 +1215,105 @@
 
     late_net.finish()
     last_net.finish()
-    for u in range(2):
-        cols = slice(u * half_heads, (u + 1) * half_heads)
-        got = late_final[u].astype(F32)
-        rest = last_final[u].astype(F32)
-        g_key[:, cols] = got[:, :half_heads]
-        g_value[:, cols] = got[:, half_heads : 2 * half_heads]
-        g_query[:, cols] = jnp.concatenate(
-            [got[:, 2 * half_heads :], rest[:, :HEAD_DIM]], axis=1
-        )
-        g_forget[u] = rest
     layer_last()
     grad_last()
-    for part_net in (late_net, last_net, early_net, net):
+    for part_net in (weight_net, out_net, late_net, last_net, early_net, net):
         part_net.drain()
 
 
+def narrow_kernel(
+    layer,
+    tokens,
+    gains,
+    biases,
+    late,
+    last,
+    early,
+    units,
+    layer_out,
+    tokens_grad,
+    gain_one,
+    g_query,
+    g_key,
+    g_value,
+    g_forget,
+    g_bias,
+    g_out,
+    gain_two,
+    g_gate,
+    g_up,
+    g_down,
+):
+    layer_out[...] = layer[...]
+    tokens_grad[...] = tokens[...]
+    gain_one[...] = gains[0]
+    gain_two[...] = gains[1]
+    half = g_query.shape[1] // 2
+    heads = half // HEAD_DIM
+    hidden = units.shape[2] // 3
+    block = g_query.shape[0]
+    for u in range(2):
+        cols = slice(u * half, (u + 1) * half)
+        got = late[u].astype(F32)
+        rest = last[u].astype(F32)
+        g_key[:, cols] = got[:, :half]
+        g_value[:, cols] = got[:, half : 2 * half]
+        g_query[:, cols] = jnp.concatenate([got[:, 2 * half :], rest[:, :HEAD_DIM]], axis=1)
+        g_out[:, cols] = early[u, :, HEAD_DIM:].astype(F32)
+        padded = jnp.concatenate([rest, jnp.zeros((2 * LANES - block, LANES), F32)], axis=0)
+        g_forget[u * heads : (u + 1) * heads, :] = padded.T[HEAD_DIM : HEAD_DIM + heads, :block]
+        g_bias[u * heads : (u + 1) * heads, :] = biases[u, :heads, :]
+    for zz in range(4):
+        cols = slice(zz * hidden, (zz + 1) * hidden)
+        for index, ref in enumerate((g_gate, g_up, g_down)):
+            ref[:, cols] = units[zz, :, index * hidden : (index + 1) * hidden].astype(F32)
+
+
 VMEM = pl.BlockSpec(memory_space=pltpu.VMEM)
+SMEM = pl.BlockSpec(memory_space=pltpu.SMEM)
+HBM = pl.BlockSpec(memory_space=pl.ANY)
 
 
 def shapes_of(made):
     return [jax.ShapeDtypeStruct(*m) for m in made]
 
 
-def forward_shapes(rows, width, heads, hidden):
+def layer_shapes(rows, width, heads, hidden):
     chunk = rows // 4
     part = 4 * chunk
     every = 32 * chunk
+    block = width // 8
     attn = (3 * heads * HEAD_DIM // 2) + HEAD_DIM
+    cut = attn - LANES
     outs = [
+        ((rows, width), BF16),
+        ((rows, width), BF16),
+        ((8, width), F32),
+        ((2, 8, LANES), F32),
+        ((2, block, cut), BF16),
+        ((2, block, LANES), BF16),
+        ((2, block, 2 * LANES), BF16),
+        ((4, block, 3 * hidden), BF16),
+    ]
+
+    def weight_sum(columns):
+        return [
+            ((width, columns), BF16),
+            ((width // 2, columns), BF16),
+            ((2, block, columns), BF16),
+        ]
+
+    row_sum = [((2, part, width), BF16), ((4, chunk, width), BF16), ((4, chunk, width), BF16)]
+    scratch = [
+        ((2, block, attn), BF16),
+        ((2, block, 2 * LANES), BF16),
+        ((2, 8, LANES), F32),
+        ((2, 8, LANES), F32),
+        ((2, part, width), BF16),
+        ((2 * part, every), BF16),
+        ((every, LANES), F32),
+        ((every // chunk, every), F32),
+        ((2, 2, 8, 2 * part), F32),
         ((2 * part, 2 * LANES), BF16),
         ((2, 2, 2, part, 3 * LANES), BF16),
         ((8, every), F32),
@@ -1268,76 +1327,8 @@
         ((width, attn), BF16),
         ((width, 2 * LANES), BF16),
         ((width, 3 * hidden), BF16),
-        ((2, part, width), BF16),
-    ]
-    scratch = [
-        ((4, width // 8, 3 * hidden), BF16),
-        ((2, 4, chunk, width), BF16),
-        ((2 * part, every), F32),
-        ((every, LANES), F32),
-        ((every // chunk, every), F32),
-        ((2, 2, 8, 2 * part), F32),
-        ((2, 8, LANES), F32),
-        ((2 * part, attn), F32),
-        ((2, part, width), BF16),
-        ((4, chunk, width), BF16),
-        ((4, chunk, width), BF16),
-    ]
-    return outs, scratch
-
-
-def run_forward(heads, tokens, gain_one, gain_two, stages, ffn, doc_lengths, out_grad):
-    rows, width = tokens.shape
-    outs, scratch = forward_shapes(rows, width, heads, ffn[0].shape[1] // 4)
-    return pl.pallas_call(
-        forward_kernel,
-        out_shape=shapes_of(outs),
-        in_specs=[VMEM] * 9 + [pl.BlockSpec(memory_space=pltpu.SMEM), VMEM],
-        out_specs=[VMEM] * len(outs),
-        scratch_shapes=[pltpu.VMEM(*m) for m in scratch] + [pltpu.SemaphoreType.DMA((256,))],
-        compiler_params=pltpu.CompilerParams(
-            collective_id=0, has_side_effects=True, vmem_limit_bytes=60 << 20
-        ),
-    )(tokens, gain_one, gain_two, *stages, *ffn, doc_lengths, out_grad)
-
-
-def backward_shapes(rows, width, heads, hidden):
-    chunk = rows // 4
-    part = 4 * chunk
-    every = 32 * chunk
-    block = width // 8
-    attn = (3 * heads * HEAD_DIM // 2) + HEAD_DIM
-    head_cols = heads * HEAD_DIM
-    outs = [
-        ((rows, width), BF16),
-        ((rows, width), BF16),
-        ((8, width), F32),
-        ((2, 8, LANES), F32),
-        ((block, head_cols), F32),
-        ((block, head_cols), F32),
-        ((block, head_cols), F32),
-        ((2, block, LANES), F32),
-        ((block, head_cols), F32),
-        ((block, 4 * hidden), F32),
-        ((block, 4 * hidden), F32),
-        ((block, 4 * hidden), F32),
-    ]
-
-    def weight_sum(columns):
-        return [
-            ((width, columns), BF16),
-            ((width // 2, columns), BF16),
-            ((2, block, columns), BF16),
-            ((2, block, columns), BF16),
-        ]
-
-    row_sum = [((2, part, width), BF16), ((4, chunk, width), BF16), ((4, chunk, width), BF16)]
-    scratch = [
         ((2, 2, 2, part, 2 * LANES), BF16),
         ((2, 2, 2, part, 2 * LANES), BF16),
-        ((2 * part, every), F32),
-        ((every, LANES), F32),
-        ((every // chunk, every), F32),
         ((2, 2, part, 3 * hidden), BF16),
         ((2, 2, part, width), BF16),
         ((2, 2, part, width), BF16),
@@ -1345,8 +1336,7 @@
         *row_sum,
         ((width, 3 * hidden), BF16),
         ((4, block, 3 * hidden), BF16),
-        ((4, block, 3 * hidden), BF16),
-        *weight_sum(attn - LANES),
+        *weight_sum(cut),
         *weight_sum(LANES),
         *weight_sum(2 * LANES),
         ((2, part, width), BF16),
@@ -1359,23 +1349,9 @@
         *row_sum,
         ((4, 8, width + LANES), F32),
         ((6, 8, width), F32),
+        ((chunk, width), BF16),
     ]
     return outs, scratch
-
-
-def run_backward(heads, hidden, tokens, out_grad, gain_one, gain_two, made, doc_lengths):
-    rows, width = tokens.shape
-    outs, scratch = backward_shapes(rows, width, heads, hidden)
-    return pl.pallas_call(
-        backward_kernel,
-        out_shape=shapes_of(outs),
-        in_specs=[VMEM] * 18 + [pl.BlockSpec(memory_space=pltpu.SMEM)],
-        out_specs=[VMEM] * len(outs),
-        scratch_shapes=[pltpu.VMEM(*m) for m in scratch] + [pltpu.SemaphoreType.DMA((320,))],
-        compiler_params=pltpu.CompilerParams(
-            collective_id=1, has_side_effects=True, vmem_limit_bytes=63 << 20
-        ),
-    )(tokens, out_grad, gain_one, gain_two, *made, doc_lengths)
 
 
 def kernel_body(
@@ -1395,71 +1371,64 @@
     out_grad,
 ):
     heads = forget_bias.shape[0]
-    width = tokens.shape[1]
-    hidden = gate_weight.shape[1] // 4
-    half_heads = heads // 2
-    cols = half_heads * HEAD_DIM
-    block = query_weight.shape[0]
-    out_t = out_weight.T
-
-    def halves(weight):
-        return weight.reshape(block, 2, -1).transpose(1, 0, 2)
-
-    stage_attn = jnp.concatenate(
-        [
-            halves(key_weight),
-            halves(value_weight),
-            halves(query_weight),
-            halves(forget_weight),
-            jnp.zeros((2, block, HEAD_DIM - half_heads), BF16),
-        ],
-        axis=2,
-    )
-    stage_out = jnp.pad(halves(out_t), ((0, 0), (0, 0), (2 * LANES - cols, 0)))
-    stage_bias = jnp.broadcast_to(
-        jnp.pad(forget_bias.reshape(2, half_heads), ((0, 0), (0, 8 - half_heads)))[:, :, None],
-        (2, 8, LANES),
-    )
-    gain_one = attn_gain.reshape(1, width)
-    gain_two = ffn_gain.reshape(1, width)
-    made = run_forward(
-        heads,
+    rows, width = tokens.shape
+    block, units = gate_weight.shape
+    cols = query_weight.shape[1]
+    outs, scratch = layer_shapes(rows, width, heads, units // 4)
+    made = pl.pallas_call(
+        layer_kernel,
+        out_shape=shapes_of(outs),
+        in_specs=[HBM] * 2 + [VMEM] * 6 + [SMEM] + [VMEM] + [HBM] * 3 + [SMEM],
+        out_specs=[VMEM] * len(outs),
+        scratch_shapes=[pltpu.VMEM(*m) for m in scratch] + [pltpu.SemaphoreType.DMA((15,)), pltpu.SemaphoreType.DMA((512,))],
+        compiler_params=pltpu.CompilerParams(
+            collective_id=0, has_side_effects=True, vmem_limit_bytes=63 << 20
+        ),
+    )(
         tokens,
-        gain_one,
-        gain_two,
-        (stage_attn, stage_out, stage_bias),
-        (gate_weight, up_weight, down_weight.T),
+        out_grad,
+        attn_gain,
+        ffn_gain,
+        query_weight,
+        key_weight,
+        value_weight,
+        forget_weight.T,
+        forget_bias,
+        out_weight.T,
+        gate_weight,
+        up_weight,
+        down_weight.T,
         doc_lengths,
-        out_grad,
-    )
-    (
-        layer_out,
-        tokens_grad,
-        gains,
-        bias_grad,
-        g_query,
-        g_key,
-        g_value,
-        g_forget,
-        g_out,
-        g_gate,
-        g_up,
-        g_down,
-    ) = run_backward(heads, hidden, tokens, out_grad, gain_one, gain_two, made, doc_lengths)
+    )
+    finals = [
+        ((rows, width), BF16),
+        ((rows, width), BF16),
+        ((width,), F32),
+        ((block, cols), F32),
+        ((block, cols), F32),
+        ((block, cols), F32),
+        ((heads, block), F32),
+        ((heads, LANES), F32),
+        ((block, cols), F32),
+        ((width,), F32),
+        ((block, units), F32),
+        ((block, units), F32),
+        ((block, units), F32),
+    ]
+    final = pl.pallas_call(
+        narrow_kernel,
+        out_shape=shapes_of(finals),
+        in_specs=[VMEM] * len(outs),
+        out_specs=[VMEM] * len(finals),
+        compiler_params=pltpu.CompilerParams(vmem_limit_bytes=63 << 20),
+    )(*made)
     return (
-        layer_out,
-        tokens_grad,
-        gains[0],
-        g_query,
-        g_key,
-        g_value,
-        g_forget[:, :, HEAD_DIM : HEAD_DIM + half_heads].transpose(1, 0, 2).reshape(block, heads),
-        bias_grad[:, :half_heads, 0].reshape(heads),
-        g_out.T,
-        gains[1],
-        g_gate,
-        g_up,
-        g_down.T,
+        *final[:6],
+        final[6].T,
+        final[7][:, 0],
+        final[8].T,
+        *final[9:12],
+        final[12].T,
     )
 
 

time: 322 us -> 287 us (0.89)
  local copies, waits for them, and re-layouts: 23.5 us -> 1.31 us
  Pallas kernels: 292 us -> 281 us
    pallas_call x2, Pallas kernels: 292 us -> 281 us  [the longest x1 276 us: kernel_body(): pl.pallas_call(layer_kernel, out_shape=shapes_of(outs), in_specs=[HBM] *...]
    unnamed x27 -> x0, local copies, waits for them, and re-layouts: 8.52 us -> none
    reshape x12 -> x0, local copies, waits for them, and re-layouts: 8.24 us -> none  [the longest x8 4.26 us: halves(): return weight.reshape(block, 2, -1).transpose(1, 0, 2)]
where the time goes in v4:
time: 287 us; the launch traced here: 283 us
  Pallas kernels  281 us (98%)
    pallas_call x1, Pallas kernels, kernel_body(): pl.pallas_call(layer_kernel, out_shape=shapes_of(outs), in_specs=[HBM] *...  276 us

profile of v4, /device:TPU:0, one launch (start us, length us, event | category | flops | bytes accessed | tf_op | source)
XLA Modules:
  0.0 282.8 jit_solution(14597506150027494587)
XLA Ops:
  0.7 276.2 %shard_map.237 = (bf16[256,1536]{1,0:T(8,128)(2,1)}, bf16[256,1536]{1,0:T(8,128)(2,1)}, f32[8,1536]{1,0:T(8,128)}, f32[2,8,128]{2,1,0:T(8,128)}, bf16[2,192,512]...) custom-call(bf16[256,1536]{1,0:T(8,128)(2,1)} %tokens.1, ...), custom_call_target="tpu_custom_call" | custom-call | tf_op jit(solution)/shard_map/pallas_call | solution.py:1378
  276.8 4.5 %shard_map.238 = (bf16[256,1536]{1,0:T(8,128)(2,1)}, bf16[256,1536]{1,0:T(8,128)(2,1)}, f32[1536]{0:T(1024)}, f32[192,384]{1,0:T(8,128)}, f32[192,384]{1,0:T(8,1...) custom-call(bf16[256,1536]{1,0:T(8,128)(2,1)} %get-tuple-element.34., ...), custom_call_target="tpu_custom_call" | custom-call | tf_op jit(solution)/shard_map/pallas_call | solution.py:1418
  281.3 1.3 slice_reduce_fusion
